TPU v7x, 32 devices: a whole 2x2x4 slice. The times are simulated.
32 devices in a mesh: dp: 8 (over z, core), expert: 4 (over y, x).
Axes of the slice: x: 2, y: 2, z: 4, core: 2. Of those that a mesh axis runs over, the one named last changes fastest.
Arguments:
- tokens: bfloat16 [4096, 2048], P(('dp', 'expert')), may hold values from -6 to 6
- queries: bfloat16 [4096, 128], P(('dp', 'expert')), may hold values from -4.5 to 4.5
- key_vectors: bfloat16 [4096, 128], P(('dp', 'expert')), may hold values from -4.5 to 4.5
- gate_logits: float32 [4096, 8], P(('dp', 'expert')), may hold values from -6 to 6
- value_routes: int32 [4096, 2], P(('dp', 'expert')), may hold values from 0 to 3, all different within a row; in each aligned block of 128 rows (0 to 127, 128 to 255, ...) at most 80 rows name the same one
- output_routes: int32 [4096, 2], P(('dp', 'expert')), may hold values from 0 to 3, all different within a row; in each aligned block of 128 rows (0 to 127, 128 to 255, ...) at most 80 rows name the same one
- value_weight: bfloat16 [4, 2048, 128], P('expert', 'dp'), may hold values from -0.125 to 0.125
- output_weight: bfloat16 [4, 2048, 128], P('expert', 'dp'), may hold values from -0.5 to 0.5
- cotangent: bfloat16 [4096, 2048], P(('dp', 'expert')), may hold values from -6 to 6
Outputs:
- token_grad: bfloat16 [4096, 2048], P(('dp', 'expert'))
- query_grad: bfloat16 [4096, 128], P(('dp', 'expert'))
- key_grad: bfloat16 [4096, 128], P(('dp', 'expert'))
- logit_grad: float32 [4096, 8], P(('dp', 'expert'))
- value_weight_grad: float32 [4, 2048, 128], P('expert', 'dp')
- output_weight_grad: float32 [4, 2048, 128], P('expert', 'dp')
Inputs may be any that keep to these rules, and one draw needn't show every extreme that they name: `value_routes`: among one device's 128 tokens no value expert is named more than 80 times, a bound that some block reaches. `output_routes`: among one device's 128 tokens no output expert is named more than 80 times, a bound that some block reaches.
All inputs are finite; a program needn't handle non-finite values.
Results may differ from a plain program's by a relative error of at most 0.025.
Values may be sent and summed in bfloat16 or wider, within the bound.
No kernel may reach another device: no remote copies, remote signals or barrier semaphores. Data moves between devices by JAX's collectives and lax.ppermute only.
A program may use at most 64 MiB of HBM per device.

v0:
```python
import math

import jax
import jax.numpy as jnp
from jax import lax
from jax.sharding import PartitionSpec as P


def slot_index(routes, experts, capacity):
    flattened = routes.reshape(-1)
    onehot = (flattened[:, None] == jnp.arange(experts, dtype=jnp.int32)[None, :]).astype(jnp.int32)
    before = jnp.cumsum(onehot, axis=0) - onehot
    return flattened * capacity + jnp.sum(before * onehot, axis=1)


def owner_rows(slots, experts, capacity):
    row_count = slots.shape[0]
    owner_table = jnp.full((experts * capacity,), row_count, jnp.int32)
    return owner_table.at[slots].set(jnp.arange(row_count, dtype=jnp.int32))


def causal_probs(queries, key_vectors):
    length_rows = queries.shape[0]
    scores = jnp.dot(queries, key_vectors.T, preferred_element_type=jnp.float32) / math.sqrt(
        queries.shape[1]
    )
    row_ids = lax.broadcasted_iota(jnp.int32, (length_rows, length_rows), 0)
    col_ids = lax.broadcasted_iota(jnp.int32, (length_rows, length_rows), 1)
    scores = jnp.where(row_ids >= col_ids, scores, -1e30)
    row_max = jnp.max(scores, axis=1, keepdims=True)
    exponent = jnp.exp(scores - row_max)
    return exponent / jnp.sum(exponent, axis=1, keepdims=True)


def to_owners(buffer):
    return lax.all_to_all(buffer, "expert", split_axis=0, concat_axis=0, tiled=True)


def from_owners(buffer):
    return lax.all_to_all(buffer, "expert", split_axis=0, concat_axis=0, tiled=True)


def transpose_product(left, right):
    return lax.dot_general(
        left, right, (((0,), (0,)), ((), ())), preferred_element_type=jnp.float32
    )


def on_device(
    tokens,
    queries,
    key_vectors,
    gate_logits,
    value_routes,
    output_routes,
    value_weight,
    output_weight,
    cotangent,
):
    tok_rows = tokens.shape[0]
    features = tokens.shape[1]
    head_size = queries.shape[1]
    experts = gate_logits.shape[1] // 2
    capacity = 5 * tok_rows // (2 * experts)
    groups = lax.axis_size("dp")
    gate_values = jax.nn.sigmoid(gate_logits)
    value_gate = jnp.take_along_axis(gate_values[:, :experts], value_routes, axis=1)
    output_gate = jnp.take_along_axis(gate_values[:, experts:], output_routes, axis=1)
    slot_value = slot_index(value_routes, experts, capacity)
    slot_output = slot_index(output_routes, experts, capacity)
    owner_value = owner_rows(slot_value, experts, capacity)
    owner_output = owner_rows(slot_output, experts, capacity)
    full_value, full_output = (
        lax.all_gather(value_weight, "dp", axis=1, tiled=True),
        lax.all_gather(output_weight, "dp", axis=1, tiled=True),
    )
    matrix_value = full_value[0]
    sent_tokens = jnp.take(tokens, owner_value // 2, axis=0, mode="fill", fill_value=0).reshape(
        experts, capacity, features
    )
    sent_grads = jnp.take(cotangent, owner_output // 2, axis=0, mode="fill", fill_value=0)
    held_tokens = to_owners(sent_tokens).reshape(experts * capacity, features)
    expert_out = jnp.dot(held_tokens, matrix_value, preferred_element_type=jnp.float32).astype(
        jnp.bfloat16
    )
    returned_value = from_owners(expert_out.reshape(experts, capacity, head_size)).reshape(
        experts * capacity, head_size
    )
    expert_value = returned_value[slot_value].reshape(tok_rows, 2, head_size).astype(jnp.float32)
    mixed_value = jnp.sum(value_gate[:, :, None] * expert_value, axis=1).astype(jnp.bfloat16)
    probs = causal_probs(queries, key_vectors)
    weights = probs.astype(jnp.bfloat16)
    hidden = jnp.dot(weights, mixed_value, preferred_element_type=jnp.float32).astype(jnp.bfloat16)
    gated_hidden = (
        (output_gate[:, :, None] * hidden[:, None, :].astype(jnp.float32))
        .astype(jnp.bfloat16)
        .reshape(2 * tok_rows, head_size)
    )
    sent_hidden = jnp.take(gated_hidden, owner_output, axis=0, mode="fill", fill_value=0)
    packed = jnp.concatenate([sent_grads, sent_hidden], axis=1).reshape(
        experts, capacity, features + head_size
    )
    held_output = to_owners(packed).reshape(experts * capacity, features + head_size)
    held_grads = held_output[:, :features]
    held_hidden = held_output[:, features:]
    matrix_output = full_output[0]
    head_rows = jnp.dot(held_grads, matrix_output, preferred_element_type=jnp.float32).astype(
        jnp.bfloat16
    )
    grad_output = transpose_product(held_grads, held_hidden)
    returned_output = from_owners(head_rows.reshape(experts, capacity, head_size)).reshape(
        experts * capacity, head_size
    )
    head_back = returned_output[slot_output].reshape(tok_rows, 2, head_size).astype(jnp.float32)
    output_gate_grad = jnp.sum(hidden[:, None, :].astype(jnp.float32) * head_back, axis=2)
    hidden_grad = jnp.sum(output_gate[:, :, None] * head_back, axis=1).astype(jnp.bfloat16)
    prob_grad = jnp.dot(hidden_grad, mixed_value.T, preferred_element_type=jnp.float32)
    score_grad = probs * (prob_grad - jnp.sum(prob_grad * probs, axis=1, keepdims=True))
    scaled_grad = (score_grad / math.sqrt(head_size)).astype(jnp.bfloat16)
    query_grad = jnp.dot(scaled_grad, key_vectors, preferred_element_type=jnp.float32).astype(
        jnp.bfloat16
    )
    key_grad = jnp.dot(scaled_grad.T, queries, preferred_element_type=jnp.float32).astype(
        jnp.bfloat16
    )
    value_grad = jnp.dot(weights.T, hidden_grad, preferred_element_type=jnp.float32).astype(
        jnp.bfloat16
    )
    gated_value = (
        (value_gate[:, :, None] * value_grad[:, None, :].astype(jnp.float32))
        .astype(jnp.bfloat16)
        .reshape(2 * tok_rows, head_size)
    )
    value_gate_grad = jnp.sum(value_grad[:, None, :].astype(jnp.float32) * expert_value, axis=2)
    sent_value = jnp.take(gated_value, owner_value, axis=0, mode="fill", fill_value=0).reshape(
        experts, capacity, head_size
    )
    held_value = to_owners(sent_value).reshape(experts * capacity, head_size)
    grad_value = transpose_product(held_tokens, held_value)
    token_rows_back = lax.dot_general(
        held_value, matrix_value, (((1,), (1,)), ((), ())), preferred_element_type=jnp.float32
    ).astype(jnp.bfloat16)
    returned_tokens = from_owners(token_rows_back.reshape(experts, capacity, features)).reshape(
        experts * capacity, features
    )
    token_grad = jnp.sum(
        returned_tokens[slot_value].reshape(tok_rows, 2, features).astype(jnp.float32), axis=1
    ).astype(jnp.bfloat16)
    summed_value, summed_output = (
        lax.psum_scatter(
            grad_value[None].astype(jnp.bfloat16), "dp", scatter_dimension=1, tiled=True
        ).astype(jnp.float32),
        lax.psum_scatter(
            grad_output[None].astype(jnp.bfloat16), "dp", scatter_dimension=1, tiled=True
        ).astype(jnp.float32),
    )
    value_weight_grad = summed_value / groups
    output_weight_grad = summed_output / groups
    expert_ids = jnp.arange(experts, dtype=jnp.int32)[None, None, :]
    hot_value = (value_routes[:, :, None] == expert_ids).astype(jnp.float32)
    hot_output = (output_routes[:, :, None] == expert_ids).astype(jnp.float32)
    logit_value = jnp.sum(
        hot_value * (value_gate_grad * value_gate * (1.0 - value_gate))[:, :, None], axis=1
    )
    logit_output = jnp.sum(
        hot_output * (output_gate_grad * output_gate * (1.0 - output_gate))[:, :, None], axis=1
    )
    logit_grad = jnp.concatenate([logit_value, logit_output], axis=1)
    return (token_grad, query_grad, key_grad, logit_grad, value_weight_grad, output_weight_grad)


def solution(mesh):
    in_specs = (
        P(("dp", "expert"), None),
        P(("dp", "expert"), None),
        P(("dp", "expert"), None),
        P(("dp", "expert"), None),
        P(("dp", "expert"), None),
        P(("dp", "expert"), None),
        P("expert", "dp", None),
        P("expert", "dp", None),
        P(("dp", "expert"), None),
    )
    out_specs = (
        P(("dp", "expert"), None),
        P(("dp", "expert"), None),
        P(("dp", "expert"), None),
        P(("dp", "expert"), None),
        P("expert", "dp", None),
        P("expert", "dp", None),
    )
    return jax.shard_map(
        on_device, mesh=mesh, in_specs=in_specs, out_specs=out_specs, check_vma=False
    )
```

profile of v0, /device:TPU:0, one launch (start us, length us, event | category | flops | bytes accessed | tf_op | source)
XLA Modules:
  0.0 174.3 jit_solution(8050320770959163487)
XLA Ops:
  12.9 2.4 %gather_fusion.6 = bf16[320,2048]{1,0:T(8,128)(2,1)S(1)} fusion(bf16[128,2048]{1,0:T(8,128)(2,1)S(1)} %copy-done, s32[1024]{0:T(1024)S(1)} %pad_clamp_fusion.4), kind=kCustom, calls=%fused_computation.4.clone | custom fusion | bytes 2622720 | tf_op jit(solution)/shard_map/jit(_take)/gather | solution.py:78
  16.6 5.3 %all-to-all-start = ((bf16[4,80,2048]{2,1,0:T(8,128)(2,1)}), bf16[4,80,2048]{2,1,0:T(8,128)(2,1)S(1)}, u32[]{:S(2)}, u32[]{:S(2)}) async-start(bf16[4,80,2048]{2,1,0:T(8,128)(2,1)} %bitcast.10), calls=%async_computation | async-start | bytes 2621440 | tf_op jit(solution)/shard_map/all_to_all | solution.py:36
  22.6 2.4 %gather_fusion.4 = f32[256]{0:T(256)S(1)} fusion(f32[128,4]{0,1:T(4,128)S(1)} %get-tuple-element.15, s32[256]{0:T(256)S(1)} %reshape.331), kind=kCustom, calls=%fused_computation.3.clone | custom fusion | bytes 4096 | tf_op jit(solution)/shard_map/jit(take_along_axis)/gather | solution.py:68
  25.8 2.4 %gather_fusion.3 = f32[256]{0:T(256)S(1)} fusion(f32[128,4]{0,1:T(4,128)S(1)} %get-tuple-element.16, s32[256]{0:T(256)S(1)} %reshape.326), kind=kCustom, calls=%fused_computation.clone | custom fusion | bytes 4096 | tf_op jit(solution)/shard_map/jit(take_along_axis)/gather | solution.py:67
  33.2 3.0 %gather_fusion.5 = bf16[320,2048]{1,0:T(8,128)(2,1)} fusion(bf16[128,2048]{1,0:T(8,128)(2,1)S(1)} %copy-done.1, s32[1024]{0:T(1024)S(1)} %pad_clamp_fusion.5), kind=kCustom, calls=%fused_computation.1.clone | custom fusion | bytes 2622720 | tf_op jit(solution)/shard_map/jit(_take)/gather | solution.py:81
  36.2 16.1 %all_gather.6 = bf16[1,2048,128]{2,1,0:T(8,128)(2,1)} all-gather(bf16[1,256,128]{2,1,0:T(8,128)(2,1)S(1)} %copy-done.9), channel_id=1, replica_groups=mesh['dp'=8,'expert'=4] {'dp'}, dimensions={1}, use_global_device_ids=true | all-gather | bytes 589824 | tf_op jit(solution)/shard_map/all_gather | solution.py:74
  53.9 2.2 %convolution_convert_fusion.2 = bf16[320,128]{1,0:T(8,128)(2,1)} fusion(bf16[320,2048]{1,0:T(8,128)(2,1)S(1)} %bitcast.103, bf16[1,2048,128]{2,1,0:T(8,128)(2,1)} %all_gather.6), kind=kOutput, calls=%fused_computation.24 | convolution fusion | flops 167813120 | bytes 1916928 | tf_op jit(solution)/shard_map/dot_general | solution.py:83
  56.0 4.3 %all-to-all-start.1 = ((bf16[4,80,128]{2,1,0:T(8,128)(2,1)}), bf16[4,80,128]{2,1,0:T(8,128)(2,1)S(1)}, u32[]{:S(2)}, u32[]{:S(2)}) async-start(bf16[4,80,128]{2,1,0:T(8,128)(2,1)} %bitcast.13), calls=%async_computation.1 | async-start | bytes 163840 | tf_op jit(solution)/shard_map/all_to_all | solution.py:40
  60.3 4.9 %all-to-all-done.1 = bf16[4,80,128]{2,1,0:T(8,128)(2,1)S(1)} async-done(((bf16[4,80,128]{2,1,0:T(8,128)(2,1)}), bf16[4,80,128]{2,1,0:T(8,128)(2,1)S(1)}, u32[]{:S(2)}, u32[]{:S(2)}) %all-to-all-start.1) | async-done | bytes 81952 | tf_op jit(solution)/shard_map/all_to_all | solution.py:40
  70.7 3.7 %all-to-all-start.2 = ((bf16[4,80,2176]{2,1,0:T(8,128)(2,1)}), bf16[4,80,2176]{2,1,0:T(8,128)(2,1)S(1)}, u32[]{:S(2)}, u32[]{:S(2)}) async-start(bf16[4,80,2176]{2,1,0:T(8,128)(2,1)} %bitcast.17), calls=%async_computation.2 | async-start | bytes 2785280 | tf_op jit(solution)/shard_map/all_to_all | solution.py:36
  76.3 15.9 %all_gather.7 = bf16[1,2048,128]{2,1,0:T(8,128)(2,1)} all-gather(bf16[1,256,128]{2,1,0:T(8,128)(2,1)S(1)} %copy-done.10), channel_id=1, replica_groups=mesh['dp'=8,'expert'=4] {'dp'}, dimensions={1}, use_global_device_ids=true | all-gather | bytes 589824 | tf_op jit(solution)/shard_map/all_gather | solution.py:75
  92.1 2.2 %fusion.6 = bf16[320,128]{1,0:T(8,128)(2,1)} fusion(bf16[320,2176]{1,0:T(8,128)(2,1)S(1)} %bitcast.106, bf16[1,2048,128]{2,1,0:T(8,128)(2,1)} %all_gather.7), kind=kOutput, calls=%fused_computation.23 | convolution fusion | flops 167813120 | bytes 1916928 | tf_op jit(solution)/shard_map/dot_general | solution.py:107
  94.3 4.1 %all-to-all-start.3 = ((bf16[4,80,128]{2,1,0:T(8,128)(2,1)}), bf16[4,80,128]{2,1,0:T(8,128)(2,1)S(1)}, u32[]{:S(2)}, u32[]{:S(2)}) async-start(bf16[4,80,128]{2,1,0:T(8,128)(2,1)} %bitcast.114), calls=%async_computation.3 | async-start | bytes 163840 | tf_op jit(solution)/shard_map/all_to_all | solution.py:40
  99.9 3.4 %all-to-all-done.3 = bf16[4,80,128]{2,1,0:T(8,128)(2,1)S(1)} async-done(((bf16[4,80,128]{2,1,0:T(8,128)(2,1)}), bf16[4,80,128]{2,1,0:T(8,128)(2,1)S(1)}, u32[]{:S(2)}, u32[]{:S(2)}) %all-to-all-start.3) | async-done | bytes 81952 | tf_op jit(solution)/shard_map/all_to_all | solution.py:40
  109.2 3.3 %all-to-all-start.4 = ((bf16[4,80,128]{2,1,0:T(8,128)(2,1)}), bf16[4,80,128]{2,1,0:T(8,128)(2,1)S(1)}, u32[]{:S(2)}, u32[]{:S(2)}) async-start(bf16[4,80,128]{2,1,0:T(8,128)(2,1)} %bitcast.24), calls=%async_computation.4 | async-start | bytes 163840 | tf_op jit(solution)/shard_map/all_to_all | solution.py:36
  112.8 4.5 %all-to-all-done.4 = bf16[4,80,128]{2,1,0:T(8,128)(2,1)S(1)} async-done(((bf16[4,80,128]{2,1,0:T(8,128)(2,1)}), bf16[4,80,128]{2,1,0:T(8,128)(2,1)S(1)}, u32[]{:S(2)}, u32[]{:S(2)}) %all-to-all-start.4) | async-done | bytes 81952 | tf_op jit(solution)/shard_map/all_to_all | solution.py:36
  118.8 1.6 convolution_convert_fusion
  120.4 3.7 %all-to-all-start.5 = ((bf16[4,80,2048]{2,1,0:T(8,128)(2,1)}), bf16[4,80,2048]{2,1,0:T(8,128)(2,1)S(1)}, u32[]{:S(2)}, u32[]{:S(2)}) async-start(bf16[4,80,2048]{2,1,0:T(8,128)(2,1)} %bitcast.26), calls=%async_computation.5 | async-start | bytes 2621440 | tf_op jit(solution)/shard_map/all_to_all | solution.py:40
  126.3 8.2 %reduce-scatter.5.cloned.1.call-done = bf16[1,256,128]{2,1,0:T(8,128)(2,1)} async-done(((bf16[1,2048,128]{2,1,0:T(8,128)(2,1)}), bf16[1,256,128]{2,1,0:T(8,128)(2,1)}) %reduce-scatter.5.cloned.1.call-update) | async-done | bytes 65552 | tf_op jit(solution)/shard_map/reduce_scatter | solution.py:153
  134.5 1.5 convert_multiply_fusion.4
  136.0 3.1 %all-to-all-done.5 = bf16[4,80,2048]{2,1,0:T(8,128)(2,1)S(1)} async-done(((bf16[4,80,2048]{2,1,0:T(8,128)(2,1)}), bf16[4,80,2048]{2,1,0:T(8,128)(2,1)S(1)}, u32[]{:S(2)}, u32[]{:S(2)}) %all-to-all-start.5) | async-done | bytes 1310752 | tf_op jit(solution)/shard_map/all_to_all | solution.py:40
  141.4 3.6 %reduce_sum.113 = bf16[128,2048]{1,0:T(8,128)(2,1)} reduce(bf16[128,2,2048]{2,1,0:T(2,128)(2,1)S(1)} %reshape.223, bf16[]{:T(256)} %constant.84.clone.1), dimensions={1}, to_apply=%region_12.16 | reduce | flops 262144 | bytes 1572866 | tf_op jit(solution)/shard_map/reduce_sum | solution.py:146
  145.0 21.0 %reduce-scatter.3.cloned.1.call-done = bf16[1,256,128]{2,1,0:T(8,128)(2,1)} async-done(((bf16[1,2048,128]{2,1,0:T(8,128)(2,1)}), bf16[1,256,128]{2,1,0:T(8,128)(2,1)}) %reduce-scatter.3.cloned.1.call-update) | async-done | bytes 65552 | tf_op jit(solution)/shard_map/reduce_scatter | solution.py:150
  165.9 1.5 convert_multiply_fusion.5
  (156 shorter events, 35.4 us)
Async XLA Ops:
  7.2 5.7 %copy-start = (bf16[128,2048]{1,0:T(8,128)(2,1)S(1)}, bf16[128,2048]{1,0:T(8,128)(2,1)}, u32[]{:S(2)}) copy-start(bf16[128,2048]{1,0:T(8,128)(2,1)} %param.15) | copy-start | bytes 1572868
  16.6 5.8 %copy-start.22 = (f32[128,8]{0,1:T(8,128)S(1)}, f32[128,8]{0,1:T(8,128)}, u32[]{:S(2)}) copy-start(f32[128,8]{0,1:T(8,128)} %param.18) | copy-start | bytes 12292
  16.6 37.3 %all-to-all-start = ((bf16[4,80,2048]{2,1,0:T(8,128)(2,1)}), bf16[4,80,2048]{2,1,0:T(8,128)(2,1)S(1)}, u32[]{:S(2)}, u32[]{:S(2)}) async-start(bf16[4,80,2048]{2,1,0:T(8,128)(2,1)} %bitcast.10), calls=%async_computation | async-start | bytes 2621440 | tf_op jit(solution)/shard_map/all_to_all | solution.py:36
  21.9 43.2 %copy-start.15 = (s32[1024]{0:T(1024)}, s32[1024]{0:T(1024)S(1)}, u32[]{:S(2)}) copy-start(s32[1024]{0:T(1024)S(1)} %pad_clamp_fusion.3) | copy-start | bytes 12292
  25.8 6.8 %copy-start.6 = (bf16[128,128]{1,0:T(8,128)(2,1)S(1)}, bf16[128,128]{1,0:T(8,128)(2,1)}, u32[]{:S(2)}) copy-start(bf16[128,128]{1,0:T(8,128)(2,1)} %param.16) | copy-start | bytes 98308
  25.8 6.8 %copy-start.7 = (bf16[128,128]{1,0:T(8,128)(2,1)S(1)}, bf16[128,128]{1,0:T(8,128)(2,1)}, u32[]{:S(2)}) copy-start(bf16[128,128]{1,0:T(8,128)(2,1)} %param.17) | copy-start | bytes 98308
  32.7 33.6 %copy-start.17 = (f32[128]{0:T(128)}, f32[128]{0:T(128)S(1)}, u32[]{:S(2)}) copy-start(f32[128]{0:T(128)S(1)} %get-tuple-element.19) | copy-start | bytes 1540
  32.8 33.5 %copy-start.23 = (f32[128]{0:T(128)}, f32[128]{0:T(128)S(1)}, u32[]{:S(2)}) copy-start(f32[128]{0:T(128)S(1)} %fusion.21) | copy-start | bytes 1540
  56.0 9.1 %all-to-all-start.1 = ((bf16[4,80,128]{2,1,0:T(8,128)(2,1)}), bf16[4,80,128]{2,1,0:T(8,128)(2,1)S(1)}, u32[]{:S(2)}, u32[]{:S(2)}) async-start(bf16[4,80,128]{2,1,0:T(8,128)(2,1)} %bitcast.13), calls=%async_computation.1 | async-start | bytes 163840 | tf_op jit(solution)/shard_map/all_to_all | solution.py:40
  70.7 5.6 %copy-start.10 = (bf16[1,256,128]{2,1,0:T(8,128)(2,1)S(1)}, bf16[1,256,128]{2,1,0:T(8,128)(2,1)}, u32[]{:S(2)}) copy-start(bf16[1,256,128]{2,1,0:T(8,128)(2,1)} %param.22) | copy-start | bytes 196612
  70.7 21.5 %all-to-all-start.2 = ((bf16[4,80,2176]{2,1,0:T(8,128)(2,1)}), bf16[4,80,2176]{2,1,0:T(8,128)(2,1)S(1)}, u32[]{:S(2)}, u32[]{:S(2)}) async-start(bf16[4,80,2176]{2,1,0:T(8,128)(2,1)} %bitcast.17), calls=%async_computation.2 | async-start | bytes 2785280 | tf_op jit(solution)/shard_map/all_to_all | solution.py:36
  94.3 9.0 %all-to-all-start.3 = ((bf16[4,80,128]{2,1,0:T(8,128)(2,1)}), bf16[4,80,128]{2,1,0:T(8,128)(2,1)S(1)}, u32[]{:S(2)}, u32[]{:S(2)}) async-start(bf16[4,80,128]{2,1,0:T(8,128)(2,1)} %bitcast.114), calls=%async_computation.3 | async-start | bytes 163840 | tf_op jit(solution)/shard_map/all_to_all | solution.py:40
  98.4 5.9 %copy-start.4 = (f32[128,2]{1,0:T(8,128)S(1)}, f32[128,2]{1,0:T(8,128)}, u32[]{:S(2)}) copy-start(f32[128,2]{1,0:T(8,128)} %copy-done.3) | copy-start | bytes 3076
  98.4 36.0 %reduce-scatter.5.cloned.1.call-start = ((), (), s32[]{:S(2)}) async-start(), calls=%async_computation.9 | async-start | bytes 589824 | tf_op jit(solution)/shard_map/reduce_scatter | solution.py:153
  99.9 6.7 %copy-start.19 = (f32[256]{0:T(256)S(1)}, f32[256]{0:T(256)}, u32[]{:S(2)}) copy-start(f32[256]{0:T(256)} %mul.138) | copy-start | bytes 3076
  99.9 6.8 %copy-start.16 = (s32[1024]{0:T(1024)S(1)}, s32[1024]{0:T(1024)}, u32[]{:S(2)}) copy-start(s32[1024]{0:T(1024)} %pad_clamp_fusion) | copy-start | bytes 12292
  99.9 8.2 %copy-start.25 = (pred[320]{0:T(512)(128)(4,1)S(1)}, pred[320]{0:T(512)(128)(4,1)}, u32[]{:S(2)}) copy-start(pred[320]{0:T(512)(128)(4,1)} %get-tuple-element.17) | copy-start | bytes 964
  104.3 8.2 %copy-start.12 = (bf16[128,128]{1,0:T(8,128)(2,1)S(1)}, bf16[128,128]{1,0:T(8,128)(2,1)}, u32[]{:S(2)}) copy-start(bf16[128,128]{1,0:T(8,128)(2,1)} %copy-done.11) | copy-start | bytes 98308
  104.3 8.2 %copy-start.18 = (f32[128]{0:T(128)S(1)}, f32[128]{0:T(128)}, u32[]{:S(2)}) copy-start(f32[128]{0:T(128)} %copy-done.17) | copy-start | bytes 1540
  104.3 8.2 %copy-start.24 = (f32[128]{0:T(128)S(1)}, f32[128]{0:T(128)}, u32[]{:S(2)}) copy-start(f32[128]{0:T(128)} %copy-done.23) | copy-start | bytes 1540
  109.2 8.2 %all-to-all-start.4 = ((bf16[4,80,128]{2,1,0:T(8,128)(2,1)}), bf16[4,80,128]{2,1,0:T(8,128)(2,1)S(1)}, u32[]{:S(2)}, u32[]{:S(2)}) async-start(bf16[4,80,128]{2,1,0:T(8,128)(2,1)} %bitcast.24), calls=%async_computation.4 | async-start | bytes 163840 | tf_op jit(solution)/shard_map/all_to_all | solution.py:36
  112.5 53.5 %reduce-scatter.3.cloned.1.call-start = ((), (), s32[]{:S(2)}) async-start(), calls=%async_computation.8 | async-start | bytes 589824 | tf_op jit(solution)/shard_map/reduce_scatter | solution.py:150
  112.6 6.2 %copy-start.2 = (bf16[1,2048,128]{2,1,0:T(8,128)(2,1)S(1)}, bf16[1,2048,128]{2,1,0:T(8,128)(2,1)}, u32[]{:S(2)}) copy-start(bf16[1,2048,128]{2,1,0:T(8,128)(2,1)} %all_gather.6) | copy-start | bytes 1572868
  120.4 18.7 %all-to-all-start.5 = ((bf16[4,80,2048]{2,1,0:T(8,128)(2,1)}), bf16[4,80,2048]{2,1,0:T(8,128)(2,1)S(1)}, u32[]{:S(2)}, u32[]{:S(2)}) async-start(bf16[4,80,2048]{2,1,0:T(8,128)(2,1)} %bitcast.26), calls=%async_computation.5 | async-start | bytes 2621440 | tf_op jit(solution)/shard_map/all_to_all | solution.py:40
  (10 other events, 33.1 us)
Sparse Core Ops, SparseCore 0:
  102.1 32.3 reduce-scatter.4
  136.8 29.0 reduce-scatter.2
where the time goes:
time: 175 us; the launch traced here: 174 us
  waiting for transfers between devices  45.2 us (26%)
  blocking collectives  32 us (18%)
  local copies, waits for them, and re-layouts  25.8 us (15%)
  starting transfers between devices  24.4 us (14%)
  other arithmetic  20.5 us (12%)
  between operations  14.6 us (8%)
  matrix products  11.8 us (7%)
    reduce_scatter x1, waiting for transfers between devices, on_device(): lax.psum_scatter(grad_value[None].astype(jnp.bfloat16), 'dp', scatter_dim...  21 us
    all_gather x1, blocking collectives, on_device(): lax.all_gather(value_weight, 'dp', axis=1, tiled=True)  16.1 us
    all_gather x1, blocking collectives, on_device(): lax.all_gather(output_weight, 'dp', axis=1, tiled=True)  15.9 us
    all_to_all x3, starting transfers between devices, to_owners(): lax.all_to_all(buffer, 'expert', split_axis=0, concat_axis=0, tiled=True)  12.3 us
    all_to_all x3, starting transfers between devices, from_owners(): lax.all_to_all(buffer, 'expert', split_axis=0, concat_axis=0, tiled=True)  12.1 us
    all_to_all x3, waiting for transfers between devices, from_owners(): lax.all_to_all(buffer, 'expert', split_axis=0, concat_axis=0, tiled=True)  11.4 us
    reduce_scatter x1, waiting for transfers between devices, on_device(): lax.psum_scatter(grad_output[None].astype(jnp.bfloat16), 'dp', scatter_di...  8.21 us
    all_to_all x3, waiting for transfers between devices, to_owners(): lax.all_to_all(buffer, 'expert', split_axis=0, concat_axis=0, tiled=True)  4.56 us
  transfers between devices with their start and end apart: 8, of which 6 were waited for; matrix products, arithmetic and copies ran while one was open for 21% of the time, Pallas kernels for 0%

commit v1 on v0

v1 whole, which is shorter than its diff:
```python
import math

import jax
import jax.numpy as jnp
from jax import lax
from jax.experimental import pallas as pl
from jax.experimental.pallas import tpu as pltpu
from jax.sharding import PartitionSpec as P

F32, BF16 = jnp.float32, jnp.bfloat16
VALUE_GATE, OUTPUT_GATE, VALUE_ROUTE, OUTPUT_ROUTE, LOW_PART = 0, 2, 4, 6, 8


def kernel_call(body, outs, *args, scalars=0, flops=0):
    moved = sum(x.size * x.dtype.itemsize for x in args) + sum(
        math.prod(s) * jnp.dtype(t).itemsize for s, t in outs
    )
    return pl.pallas_call(
        body,
        out_shape=[jax.ShapeDtypeStruct(s, t) for s, t in outs],
        in_specs=[pl.BlockSpec(memory_space=pltpu.SMEM)] * scalars
        + [pl.BlockSpec(memory_space=pltpu.VMEM)] * (len(args) - scalars),
        out_specs=[pl.BlockSpec(memory_space=pltpu.VMEM)] * len(outs),
        cost_estimate=pl.CostEstimate(flops=flops, bytes_accessed=moved, transcendentals=0),
        compiler_params=pltpu.CompilerParams(vmem_limit_bytes=24 * 2**20),
    )(*args)


def dot(left, right):
    return jnp.dot(left, right, preferred_element_type=F32)


def dot_nt(left, right):
    return lax.dot_general(left, right, (((1,), (1,)), ((), ())), preferred_element_type=F32)


def table_body(me_ref, logits_ref, vr_ref, or_ref, q_ref, k_ref, table_ref, sent_ref, probs_ref, weights_ref, back_ref):
    rows, both = logits_ref.shape
    experts = both // 2
    gates = jax.nn.sigmoid(logits_ref[...])
    ids = lax.broadcasted_iota(jnp.int32, (rows, both), 1)
    lane = lax.broadcasted_iota(jnp.int32, table_ref.shape, 1)
    table = jnp.zeros(table_ref.shape, F32)
    for j in range(2):
        route_v, route_o = vr_ref[:, j : j + 1], or_ref[:, j : j + 1]
        gate_v = jnp.sum(jnp.where(ids == route_v, gates, 0.0), axis=1, keepdims=True)
        gate_o = jnp.sum(jnp.where(ids == route_o + experts, gates, 0.0), axis=1, keepdims=True)
        table = jnp.where(lane == VALUE_GATE + j, gate_v, table)
        table = jnp.where(lane == OUTPUT_GATE + j, gate_o, table)
        table = jnp.where(lane == VALUE_ROUTE + j, (route_v ^ me_ref[0]).astype(F32), table)
        table = jnp.where(lane == OUTPUT_ROUTE + j, (route_o ^ me_ref[0]).astype(F32), table)
    table_ref[...] = table
    high = table.astype(BF16).astype(F32)
    low = table - high
    for j in range(4):
        high = jnp.where(lane == LOW_PART + j, low[:, j : j + 1], high)
    sent_ref[...] = high.astype(BF16)
    length = q_ref.shape[0]
    scores = dot_nt(q_ref[...], k_ref[...]) / math.sqrt(q_ref.shape[1])
    row_ids = lax.broadcasted_iota(jnp.int32, (length, length), 0)
    col_ids = lax.broadcasted_iota(jnp.int32, (length, length), 1)
    scores = jnp.where(row_ids >= col_ids, scores, -1e30)
    exponent = jnp.exp(scores - jnp.max(scores, axis=1, keepdims=True))
    probs = exponent / jnp.sum(exponent, axis=1, keepdims=True)
    probs_ref[...] = probs
    weights_ref[...] = probs.astype(BF16)
    back_ref[...] = probs.T.astype(BF16)


def transpose_body(own_ref, got_ref, out_ref):
    rows, width = own_ref.shape
    out_ref[:, :rows] = own_ref[...].T
    out_ref[:, rows:] = got_ref[:, :width].T


def gate_columns(own_table, got_table, gate, route):
    columns = []
    for j in range(2):
        far_gate = got_table[:, gate + j : gate + j + 1].astype(F32) + got_table[
            :, LOW_PART + gate + j : LOW_PART + gate + j + 1
        ].astype(F32)
        columns.append(
            (
                jnp.concatenate([own_table[:, gate + j : gate + j + 1], far_gate], axis=0),
                jnp.concatenate(
                    [
                        own_table[:, route + j : route + j + 1],
                        got_table[:, route + j : route + j + 1].astype(F32),
                    ],
                    axis=0,
                ),
            )
        )
    return columns


def pair_up(refs):
    return [
        jnp.concatenate([r[...] for r in refs[i : i + 2]], axis=1) for i in range(0, len(refs), 2)
    ]


def partial_body(experts, gate, route, own_ref, got_ref, table_ref, got_table_ref, *refs):
    near, far, keep_ref, send_ref = refs[:experts], refs[experts : 2 * experts], refs[-2], refs[-1]
    rows, width = own_ref.shape
    half = width // 2
    left = jnp.concatenate([own_ref[...], got_ref[:, :width]], axis=0)
    columns = gate_columns(table_ref[...], got_table_ref[...], gate, route)
    slots = [jnp.zeros((2 * rows, near[0].shape[1]), F32) for _ in range(2)]
    size = near[0].shape[1]
    for i, (w_near, w_far) in enumerate(zip(pair_up(near), pair_up(far))):
        product = dot(left[:, :half], w_near) + dot(left[:, half:], w_far)
        for p in range(product.shape[1] // size):
            piece = product[:, p * size : (p + 1) * size]
            for j in range(2):
                slots[j] = jnp.where(columns[j][1] == float(2 * i + p), piece, slots[j])
    for j in range(2):
        keep_ref[:, j * size : (j + 1) * size] = slots[j][:rows]
        send_ref[:, j * size : (j + 1) * size] = slots[j][rows:].astype(BF16)


def hidden_body(keep_ref, got_ref, table_ref, weights_ref, value_ref, mixed_ref, hidden_ref):
    size = mixed_ref.shape[1]
    value = (keep_ref[...] + got_ref[...].astype(F32)).astype(BF16)
    value_ref[...] = value
    mixed = jnp.zeros(mixed_ref.shape, F32)
    for j in range(2):
        gate = table_ref[:, VALUE_GATE + j : VALUE_GATE + j + 1]
        mixed += gate * value[:, j * size : (j + 1) * size].astype(F32)
    mixed_ref[...] = mixed.astype(BF16)
    hidden_ref[...] = dot(weights_ref[...], mixed.astype(BF16)).astype(BF16)


def head_body(keep_ref, got_ref, table_ref, back_ref, head_ref, grad_ref, value_grad_ref):
    size = grad_ref.shape[1]
    head = (keep_ref[...] + got_ref[...].astype(F32)).astype(BF16)
    head_ref[...] = head
    grad = jnp.zeros(grad_ref.shape, F32)
    for j in range(2):
        gate = table_ref[:, OUTPUT_GATE + j : OUTPUT_GATE + j + 1]
        grad += gate * head[:, j * size : (j + 1) * size].astype(F32)
    grad_ref[...] = grad.astype(BF16)
    value_grad_ref[...] = dot(back_ref[...], grad.astype(BF16)).astype(BF16)


def gated_rows(experts, columns, rows):
    gated = []
    for k in range(experts):
        gate = sum(jnp.where(route == float(k), g, 0.0) for g, route in columns)
        gated.append((gate * rows).astype(BF16))
    return gated


def weight_grad_body(experts, gate, route, turned_ref, own_ref, got_ref, table_ref, got_table_ref, keep_ref, send_ref):
    rows = jnp.concatenate([own_ref[...], got_ref[...]], axis=0).astype(F32)
    columns = gate_columns(table_ref[...], got_table_ref[...], gate, route)
    gated = gated_rows(experts, columns, rows)
    half, size = turned_ref.shape[0] // 2, own_ref.shape[1]
    for i in range(0, experts, 2):
        right = jnp.concatenate(gated[i : i + 2], axis=1)
        product = dot(turned_ref[...], right)
        for p in range(right.shape[1] // size):
            piece = product[:, p * size : (p + 1) * size]
            keep_ref[i + p] = piece[:half]
            send_ref[i + p] = piece[half:].astype(BF16)


def core_sum_body(keep_ref, got_ref, own_ref, *send_refs):
    own_ref[...] = keep_ref[0] + got_ref[0].astype(F32)
    for k, send_ref in enumerate(send_refs):
        send_ref[...] = (keep_ref[k + 1] + got_ref[k + 1].astype(F32)).astype(BF16)


def token_back_body(experts, own_ref, got_ref, table_ref, got_table_ref, *refs):
    near, far, keep_ref, send_ref = refs[:experts], refs[experts : 2 * experts], refs[-2], refs[-1]
    rows = jnp.concatenate([own_ref[...], got_ref[...]], axis=0).astype(F32)
    columns = gate_columns(table_ref[...], got_table_ref[...], VALUE_GATE, VALUE_ROUTE)
    gated = gated_rows(experts, columns, rows)
    count, half = own_ref.shape[0], near[0].shape[0]
    for side, weights in enumerate((near, far)):
        total = None
        for i, right in enumerate(pair_up(weights)):
            left = jnp.concatenate(gated[2 * i : 2 * i + 2], axis=1)
            product = dot_nt(left, right)
            total = product if total is None else total + product
        keep_ref[:, side * half : (side + 1) * half] = total[:count]
        send_ref[:, side * half : (side + 1) * half] = total[count:].astype(BF16)


def attention_back_body(vr_ref, or_ref, table_ref, probs_ref, q_ref, k_ref, mixed_ref, hidden_ref, value_ref, head_ref, grad_ref, value_grad_ref, query_grad_ref, key_grad_ref, logit_ref):
    size = q_ref.shape[1]
    experts = logit_ref.shape[1] // 2
    probs = probs_ref[...]
    prob_grad = dot_nt(grad_ref[...], mixed_ref[...])
    score_grad = probs * (prob_grad - jnp.sum(prob_grad * probs, axis=1, keepdims=True))
    scaled = score_grad / math.sqrt(size)
    query_grad_ref[...] = dot(scaled.astype(BF16), k_ref[...]).astype(BF16)
    key_grad_ref[...] = dot(scaled.T.astype(BF16), q_ref[...]).astype(BF16)
    ids = lax.broadcasted_iota(jnp.int32, logit_ref.shape, 1)
    logit = jnp.zeros(logit_ref.shape, F32)
    hidden, value_grad = hidden_ref[...].astype(F32), value_grad_ref[...].astype(F32)
    for j in range(2):
        for gate_at, route, left, right, base in (
            (VALUE_GATE, vr_ref, value_grad, value_ref, 0),
            (OUTPUT_GATE, or_ref, hidden, head_ref, experts),
        ):
            gate = table_ref[:, gate_at + j : gate_at + j + 1]
            gate_grad = jnp.sum(
                left * right[:, j * size : (j + 1) * size].astype(F32), axis=1, keepdims=True
            )
            logit = jnp.where(
                ids == route[:, j : j + 1] + base, gate_grad * gate * (1.0 - gate), logit
            )
    logit_ref[...] = logit


def on_device(
    tokens,
    queries,
    key_vectors,
    gate_logits,
    value_routes,
    output_routes,
    value_weight,
    output_weight,
    cotangent,
):
    rows, features = tokens.shape
    size = queries.shape[1]
    experts = gate_logits.shape[1] // 2
    block = value_weight.shape[1]
    groups = lax.axis_size("dp")
    quads = groups // 4
    half = quads * block
    width = 2 * half
    at = lax.axis_index("dp")
    me = lax.axis_index("expert")

    def over_dp(x, flip):
        return lax.ppermute(x, "dp", [(i, i ^ flip) for i in range(groups)])

    def over_experts(x, flip):
        return lax.ppermute(x, "expert", [(i, i ^ flip) for i in range(experts)])

    def gather_weight(weight):
        own = weight[0]
        own = jnp.concatenate([own] + [over_dp(own, 4 * k) for k in range(1, quads)], axis=0)
        near = [own] + [over_experts(own, k) for k in range(1, experts)]
        return near, [over_dp(w, 1) for w in near]

    def feature_blocks(x, other):
        parts = []
        for core in range(2):
            for k in range(quads):
                start = (at ^ (4 * k + 2 * other + core)) * block
                parts.append(lax.dynamic_slice(x, (0, start), (rows, block)))
        return parts

    near_value, far_value = gather_weight(value_weight)
    near_output, far_output = gather_weight(output_weight)

    table, sent_table, probs, weights, weights_back = kernel_call(
        table_body,
        [((rows, 128), F32), ((rows, 128), BF16), ((rows, rows), F32), ((rows, rows), BF16), ((rows, rows), BF16)],
        me[None],
        gate_logits,
        value_routes,
        output_routes,
        queries,
        key_vectors,
        scalars=1,
    )
    got_table = over_dp(sent_table, 2)
    own_tokens = jnp.concatenate(feature_blocks(tokens, 0), axis=1)
    got_tokens = over_dp(jnp.concatenate(feature_blocks(tokens, 1), axis=1), 2)
    own_cotangent = jnp.concatenate(feature_blocks(cotangent, 0), axis=1)
    got_cotangent = over_dp(jnp.concatenate(feature_blocks(cotangent, 1), axis=1), 2)
    (turned_tokens,) = kernel_call(transpose_body, [((width, 2 * rows), BF16)], own_tokens, got_tokens)
    (turned_cotangent,) = kernel_call(
        transpose_body, [((width, 2 * rows), BF16)], own_cotangent, got_cotangent
    )

    product_flops = 2 * 2 * rows * width * experts * size

    def partial_products(own, got, near, far, gate, route):
        def body(*refs):
            partial_body(experts, gate, route, *refs)

        keep, send = kernel_call(
            body,
            [((rows, 2 * size), F32), ((rows, 2 * size), BF16)],
            own,
            got,
            table,
            got_table,
            *near,
            *far,
            flops=product_flops,
        )
        return keep, over_dp(send, 2)

    def weight_grad(turned, own, gate, route):
        got = over_dp(own, 2)

        def body(*refs):
            weight_grad_body(experts, gate, route, *refs)

        keep, send = kernel_call(
            body,
            [((experts, half, size), F32), ((experts, half, size), BF16)],
            turned,
            own,
            got,
            table,
            got_table,
            flops=product_flops,
        )
        sums = kernel_call(
            core_sum_body,
            [((half, size), F32)] + [((half, size), BF16)] * (experts - 1),
            keep,
            over_dp(send, 1),
        )
        total = sums[0]
        for k in range(1, experts):
            total = total + over_experts(sums[k], k).astype(F32)
        result = total[:block]
        for k in range(1, quads):
            sent = total[k * block : (k + 1) * block].astype(BF16)
            result = result + over_dp(sent, 4 * k).astype(F32)
        return (result / groups)[None], got

    value_parts = partial_products(own_tokens, got_tokens, near_value, far_value, VALUE_GATE, VALUE_ROUTE)
    expert_value, mixed_value, hidden = kernel_call(
        hidden_body,
        [((rows, 2 * size), BF16), ((rows, size), BF16), ((rows, size), BF16)],
        *value_parts,
        table,
        weights,
    )
    output_weight_grad, _ = weight_grad(turned_cotangent, hidden, OUTPUT_GATE, OUTPUT_ROUTE)

    head_parts = partial_products(
        own_cotangent, got_cotangent, near_output, far_output, OUTPUT_GATE, OUTPUT_ROUTE
    )
    head_back, hidden_grad, value_grad = kernel_call(
        head_body,
        [((rows, 2 * size), BF16), ((rows, size), BF16), ((rows, size), BF16)],
        *head_parts,
        table,
        weights_back,
    )
    value_weight_grad, got_value_grad = weight_grad(
        turned_tokens, value_grad, VALUE_GATE, VALUE_ROUTE
    )

    def back_body(*refs):
        token_back_body(experts, *refs)

    kept_back, sent_back = kernel_call(
        back_body,
        [((rows, width), F32), ((rows, width), BF16)],
        value_grad,
        got_value_grad,
        table,
        got_table,
        *near_value,
        *far_value,
        flops=product_flops,
    )
    parts = jnp.concatenate([kept_back.astype(BF16), over_dp(sent_back, 2)], axis=1)
    pieces = []
    for b in range(groups):
        flip = at ^ b
        place = ((flip >> 1) & 1) * 2 * quads + (flip & 1) * quads + (flip >> 2)
        pieces.append(lax.dynamic_slice(parts, (0, place * block), (rows, block)))
    token_grad = jnp.concatenate(pieces, axis=1)

    query_grad, key_grad, logit_grad = kernel_call(
        attention_back_body,
        [((rows, size), BF16), ((rows, size), BF16), ((rows, 2 * experts), F32)],
        value_routes,
        output_routes,
        table,
        probs,
        queries,
        key_vectors,
        mixed_value,
        hidden,
        expert_value,
        head_back,
        hidden_grad,
        value_grad,
    )
    return (token_grad, query_grad, key_grad, logit_grad, value_weight_grad, output_weight_grad)


def solution(mesh):
    rows, banks = P(("dp", "expert"), None), P("expert", "dp", None)
    return jax.shard_map(
        on_device,
        mesh=mesh,
        in_specs=(rows,) * 6 + (banks, banks, rows),
        out_specs=(rows,) * 4 + (banks, banks),
        check_vma=False,
    )
```

time: 175 us -> 81.8 us (0.47)
  blocking collectives: 32 us -> 0 us
  local copies, waits for them, and re-layouts: 25.8 us -> 5.53 us
  waiting for transfers between devices: 45.2 us -> 28.2 us
  other arithmetic: 20.5 us -> 5.27 us
  between operations: 14.6 us -> 0.97 us
  matrix products: 11.8 us -> 0 us
  starting transfers between devices: 24.4 us -> 33.9 us
  Pallas kernels: 0 us -> 7.27 us
    ppermute x0 -> x34, starting transfers between devices: none -> 33.9 us  [the longest x22 18.9 us: over_dp(): return lax.ppermute(x, 'dp', [(i, i ^ flip) for i in range(groups)])]
    all_gather x2 -> x0, blocking collectives: 32 us -> none  [the longest x1 16.1 us: on_device(): lax.all_gather(value_weight, 'dp', axis=1, tiled=True)]
    reduce_scatter x2 -> x0, waiting for transfers between devices: 29.2 us -> none  [the longest x1 21 us: on_device(): lax.psum_scatter(grad_value[None].astype(jnp.bfloat16), 'dp', scatter_dim...]
    ppermute x0 -> x34, waiting for transfers between devices: none -> 28.2 us  [the longest x22 17.1 us: over_dp(): return lax.ppermute(x, 'dp', [(i, i ^ flip) for i in range(groups)])]
    all_to_all x6 -> x0, starting transfers between devices: 24.3 us -> none  [the longest x3 12.3 us: to_owners(): lax.all_to_all(buffer, 'expert', split_axis=0, concat_axis=0, tiled=True)]
    gather x17 -> x0, local copies, waits for them, and re-layouts: 17.2 us -> none  [the longest x1 3.02 us: on_device(): jnp.take(cotangent, owner_output // 2, axis=0, mode='fill', fill_value=0)]
    all_to_all x6 -> x0, waiting for transfers between devices: 16 us -> none  [the longest x3 11.4 us: from_owners(): lax.all_to_all(buffer, 'expert', split_axis=0, concat_axis=0, tiled=True)]
    dot_general x11 -> x0, matrix products: 11.8 us -> none  [the longest x2 2.89 us: transpose_product(): lax.dot_general(left, right, (((0,), (0,)), ((), ())), preferred_element_...]
  transfers between devices with their start and end apart: 8 -> 34, of which waited for: 6 -> 12; matrix products, arithmetic and copies ran while one was open for 21% -> 9% of each run, Pallas kernels for 0% -> 9%
where the time goes in v1:
time: 81.8 us; the launch traced here: 81.2 us
  starting transfers between devices  33.9 us (41%)
  waiting for transfers between devices  28.2 us (34%)
  Pallas kernels  7.27 us (9%)
  local copies, waits for them, and re-layouts  5.53 us (7%)
  other arithmetic  5.27 us (6%)
  between operations  0.97 us (1%)
    ppermute x22, starting transfers between devices, over_dp(): return lax.ppermute(x, 'dp', [(i, i ^ flip) for i in range(groups)])  18.9 us
    ppermute x22, waiting for transfers between devices, over_dp(): return lax.ppermute(x, 'dp', [(i, i ^ flip) for i in range(groups)])  17.1 us
    ppermute x12, starting transfers between devices, over_experts(): return lax.ppermute(x, 'expert', [(i, i ^ flip) for i in range(experts)])  15 us
    ppermute x12, waiting for transfers between devices, over_experts(): return lax.ppermute(x, 'expert', [(i, i ^ flip) for i in range(experts)])  11.1 us
    pallas_call x13, Pallas kernels, kernel_call(): pl.pallas_call(body, out_shape=[jax.ShapeDtypeStruct(s, t) for s, t in ou...  7.27 us
    unnamed x20, local copies, waits for them, and re-layouts  4.16 us
    unnamed x7, other arithmetic  2.81 us
  transfers between devices with their start and end apart: 34, of which 12 were waited for; matrix products, arithmetic and copies ran while one was open for 9% of the time, Pallas kernels for 9%

profile of v1, /device:TPU:0, one launch (start us, length us, event | category | flops | bytes accessed | tf_op | source)
XLA Modules:
  0.0 81.2 jit_solution(10891128625915968134)
XLA Ops:
  0.6 4.1 %collective-permute-start.12 = (bf16[256,128]{1,0:T(8,128)(2,1)}, bf16[256,128]{1,0:T(8,128)(2,1)S(1)}, u32[]{:S(2)}, u32[]{:S(2)}) collective-permute-start(bf16[256,128]{1,0:T(8,128)(2,1)} %bitcast.9), channel_id=1, source_target_pairs={{0,16},{4,20},{8,24},{12,28},{16,0},{20,4},{24,8},{28,12},{1,17},{... | collective-permute-start | bytes 196616 | tf_op jit(solution)/shard_map/ppermute | solution.py:240
  8.7 1.9 %collective-permute-start.1 = (bf16[128,128]{1,0:T(8,128)(2,1)S(1)}, bf16[128,128]{1,0:T(8,128)(2,1)S(1)}, u32[]{:S(2)}, u32[]{:S(2)}) collective-permute-start(bf16[128,128]{1,0:T(8,128)(2,1)S(1)} %get-tuple-element.39), channel_id=1, source_target_pairs={{0,8},{4,12},{8,0},{12,4},{16,24},{20,28},{24,16},{28,20},{1,9},{5... | collective-permute-start | bytes 98312 | tf_op jit(solution)/shard_map/ppermute | solution.py:240
  10.6 1.3 %constant_dynamic-slice_fusion.3 = (bf16[128,256]{1,0:T(8,128)(2,1)S(1)}, bf16[128,256]{1,0:T(8,128)(2,1)S(1)}, bf16[128,256]{1,0:T(8,128)(2,1)S(1)}, bf16[128,2...) fusion(bf16[128,2048]{1,0:T(8,128)(2,1)} %param.9, ...), kind=kLoop, calls=%fused_computation.51 | loop fusion | bytes 2097184 | tf_op jit(solution)/shard_map/dynamic_slice | solution.py:256
  12.0 2.5 %collective-permute-start.5 = (bf16[512,128]{1,0:T(8,128)(2,1)S(1)}, bf16[512,128]{1,0:T(8,128)(2,1)S(1)}, u32[]{:S(2)}, u32[]{:S(2)}) collective-permute-start(bf16[512,128]{1,0:T(8,128)(2,1)S(1)} %pad_maximum_fusion.4.refs_4_), channel_id=1, source_target_pairs={{0,3},{1,2},{2,1},{3,0},{4,7},{5,6},{6,5},{7,4},{8,11},{9,10},{10,... | collective-permute-start | bytes 393224 | tf_op jit(solution)/shard_map/ppermute | solution.py:243
  16.0 2.7 %collective-permute-start.15 = (bf16[512,128]{1,0:T(8,128)(2,1)S(1)}, bf16[512,128]{1,0:T(8,128)(2,1)S(1)}, u32[]{:S(2)}, u32[]{:S(2)}) collective-permute-start(bf16[512,128]{1,0:T(8,128)(2,1)S(1)} %pad_maximum_fusion.5.refs_4_), channel_id=1, source_target_pairs={{0,3},{1,2},{2,1},{3,0},{4,7},{5,6},{6,5},{7,4},{8,11},{9,10},{10,... | collective-permute-start | bytes 393224 | tf_op jit(solution)/shard_map/ppermute | solution.py:243
  18.9 1.9 %collective-permute-start.14 = (bf16[512,128]{1,0:T(8,128)(2,1)S(1)}, bf16[512,128]{1,0:T(8,128)(2,1)S(1)}, u32[]{:S(2)}, u32[]{:S(2)}) collective-permute-start(bf16[512,128]{1,0:T(8,128)(2,1)S(1)} %pad_maximum_fusion.5.refs_4_), channel_id=1, source_target_pairs={{0,2},{1,3},{2,0},{3,1},{4,6},{5,7},{6,4},{7,5},{8,10},{9,11},{10,... | collective-permute-start | bytes 393224 | tf_op jit(solution)/shard_map/ppermute | solution.py:243
  20.8 3.7 %collective-permute-done.4.refs_6_ = bf16[512,128]{1,0:T(8,128)(2,1)S(1)} collective-permute-done((bf16[512,128]{1,0:T(8,128)(2,1)S(1)}, bf16[512,128]{1,0:T(8,128)(2,1)S(1)}, u32[]{:S(2)}, u32[]{:S(2)}) %collective-permute-start.4) | collective-permute-done | bytes 131104 | tf_op jit(solution)/shard_map/ppermute | solution.py:243
  25.1 2.2 %collective-permute-done.14.refs_6_ = bf16[512,128]{1,0:T(8,128)(2,1)S(1)} collective-permute-done((bf16[512,128]{1,0:T(8,128)(2,1)S(1)}, bf16[512,128]{1,0:T(8,128)(2,1)S(1)}, u32[]{:S(2)}, u32[]{:S(2)}) %collective-permute-start.14) | collective-permute-done | bytes 131104 | tf_op jit(solution)/shard_map/ppermute | solution.py:243
  27.3 2.2 %collective-permute-done.13.refs_5_ = bf16[512,128]{1,0:T(8,128)(2,1)S(1)} collective-permute-done((bf16[512,128]{1,0:T(8,128)(2,1)S(1)}, bf16[512,128]{1,0:T(8,128)(2,1)S(1)}, u32[]{:S(2)}, u32[]{:S(2)}) %collective-permute-start.13) | collective-permute-done | bytes 131104 | tf_op jit(solution)/shard_map/ppermute | solution.py:243
  31.1 4.2 %collective-permute-done.10.got_ref = bf16[128,256]{1,0:T(8,128)(2,1)S(1)} collective-permute-done((bf16[128,256]{1,0:T(8,128)(2,1)S(1)}, bf16[128,256]{1,0:T(8,128)(2,1)S(1)}, u32[]{:S(2)}, u32[]{:S(2)}) %collective-permute-start.10) | collective-permute-done | bytes 65568 | tf_op jit(solution)/shard_map/ppermute | solution.py:240
  35.7 2.0 %collective-permute-start.11 = (bf16[128,128]{1,0:T(8,128)(2,1)S(1)}, bf16[128,128]{1,0:T(8,128)(2,1)S(1)}, u32[]{:S(2)}, u32[]{:S(2)}) collective-permute-start(bf16[128,128]{1,0:T(8,128)(2,1)S(1)} %get-tuple-element.43.refs_0_.value_grad_ref.refs_1_), channel_id=1, source_target_pairs={{0,8},{4,12},{8,0},{12,4},{16,24},{20,28},{24,16},{28,20},{1,9},{5... | collective-permute-start | bytes 98312 | tf_op jit(solution)/shard_map/ppermute | solution.py:240
  37.7 5.5 %collective-permute-done.11.refs_1_.refs_2_ = bf16[128,128]{1,0:T(8,128)(2,1)S(1)} collective-permute-done((bf16[128,128]{1,0:T(8,128)(2,1)S(1)}, bf16[128,128]{1,0:T(8,128)(2,1)S(1)}, u32[]{:S(2)}, u32[]{:S(2)}) %collective-permute-start.11) | collective-permute-done | bytes 32800 | tf_op jit(solution)/shard_map/ppermute | solution.py:240
  45.2 1.4 %collective-permute-start.22 = (bf16[128,256]{1,0:T(8,128)(2,1)S(1)}, bf16[128,256]{1,0:T(8,128)(2,1)S(1)}, u32[]{:S(2)}, u32[]{:S(2)}) collective-permute-start(bf16[128,256]{1,0:T(8,128)(2,1)S(1)} %get-tuple-element.48), channel_id=1, source_target_pairs={{0,8},{4,12},{8,0},{12,4},{16,24},{20,28},{24,16},{28,20},{1,9},{5... | collective-permute-start | bytes 196616 | tf_op jit(solution)/shard_map/ppermute | solution.py:240
  46.6 5.0 %collective-permute-done.22.got_ref = bf16[128,256]{1,0:T(8,128)(2,1)S(1)} collective-permute-done((bf16[128,256]{1,0:T(8,128)(2,1)S(1)}, bf16[128,256]{1,0:T(8,128)(2,1)S(1)}, u32[]{:S(2)}, u32[]{:S(2)}) %collective-permute-start.22) | collective-permute-done | bytes 65568 | tf_op jit(solution)/shard_map/ppermute | solution.py:240
  51.9 1.4 %collective-permute-start.28 = (bf16[128,128]{1,0:T(8,128)(2,1)S(1)}, bf16[128,128]{1,0:T(8,128)(2,1)}, u32[]{:S(2)}, u32[]{:S(2)}) collective-permute-start(bf16[128,128]{1,0:T(8,128)(2,1)S(1)} %get-tuple-element.51.hidden_ref.refs_1_), channel_id=1, source_target_pairs={{0,8},{4,12},{8,0},{12,4},{16,24},{20,28},{24,16},{28,20},{1,9},{5... | collective-permute-start | bytes 98312 | tf_op jit(solution)/shard_map/ppermute | solution.py:240
  55.9 1.6 %shard_map.147 = (f32[4,512,128]{2,1,0:T(8,128)S(1)}, bf16[4,512,128]{2,1,0:T(8,128)(2,1)S(1)}) custom-call(bf16[1024,256]{1,0:T(8,128)(2,1)S(1)} %shard_map.146.refs_0_, bf16[128,128]{1,0:T(8,128)(2,1)S(1)} %get-tuple-element.51.hidden_ref.refs_1_, bf16[128,128]{1,0:T(8,128)(2,1)} %collective-permute-done.28.refs_2_, ...), custom_call_target="tpu_custom_call" | custom-call | flops 268435456 | bytes 2260992 | tf_op jit(solution)/shard_map/pallas_call | solution.py:18
  61.2 1.7 %collective-permute-start.31 = (bf16[512,128]{1,0:T(8,128)(2,1)S(1)}, bf16[512,128]{1,0:T(8,128)(2,1)S(1)}, u32[]{:S(2)}, u32[]{:S(2)}) collective-permute-start(bf16[512,128]{1,0:T(8,128)(2,1)S(1)} %get-tuple-element.68), channel_id=1, source_target_pairs={{0,2},{1,3},{2,0},{3,1},{4,6},{5,7},{6,4},{7,5},{8,10},{9,11},{10,... | collective-permute-start | bytes 393224 | tf_op jit(solution)/shard_map/ppermute | solution.py:243
  62.9 1.8 %collective-permute-start.32 = (bf16[512,128]{1,0:T(8,128)(2,1)S(1)}, bf16[512,128]{1,0:T(8,128)(2,1)S(1)}, u32[]{:S(2)}, u32[]{:S(2)}) collective-permute-start(bf16[512,128]{1,0:T(8,128)(2,1)S(1)} %get-tuple-element.69), channel_id=1, source_target_pairs={{0,3},{1,2},{2,1},{3,0},{4,7},{5,6},{6,5},{7,4},{8,11},{9,10},{10,... | collective-permute-start | bytes 393224 | tf_op jit(solution)/shard_map/ppermute | solution.py:243
  67.3 1.7 %collective-permute-start.25 = (bf16[512,128]{1,0:T(8,128)(2,1)S(1)}, bf16[512,128]{1,0:T(8,128)(2,1)S(1)}, u32[]{:S(2)}, u32[]{:S(2)}) collective-permute-start(bf16[512,128]{1,0:T(8,128)(2,1)S(1)} %get-tuple-element.62), channel_id=1, source_target_pairs={{0,2},{1,3},{2,0},{3,1},{4,6},{5,7},{6,4},{7,5},{8,10},{9,11},{10,... | collective-permute-start | bytes 393224 | tf_op jit(solution)/shard_map/ppermute | solution.py:243
  68.9 1.8 %collective-permute-start.26 = (bf16[512,128]{1,0:T(8,128)(2,1)S(1)}, bf16[512,128]{1,0:T(8,128)(2,1)S(1)}, u32[]{:S(2)}, u32[]{:S(2)}) collective-permute-start(bf16[512,128]{1,0:T(8,128)(2,1)S(1)} %get-tuple-element.63), channel_id=1, source_target_pairs={{0,3},{1,2},{2,1},{3,0},{4,7},{5,6},{6,5},{7,4},{8,11},{9,10},{10,... | collective-permute-start | bytes 393224 | tf_op jit(solution)/shard_map/ppermute | solution.py:243
  70.8 1.7 %collective-permute-start.33 = (bf16[256,128]{1,0:T(8,128)(2,1)S(1)}, bf16[256,128]{1,0:T(8,128)(2,1)S(1)}, u32[]{:S(2)}, u32[]{:S(2)}) collective-permute-start(bf16[256,128]{1,0:T(8,128)(2,1)S(1)} %slice.34), channel_id=1, source_target_pairs={{0,16},{4,20},{8,24},{12,28},{16,0},{20,4},{24,8},{28,12},{1,17},{... | collective-permute-start | bytes 196616 | tf_op jit(solution)/shard_map/ppermute | solution.py:240
  73.7 1.5 %collective-permute-done.26 = bf16[512,128]{1,0:T(8,128)(2,1)S(1)} collective-permute-done((bf16[512,128]{1,0:T(8,128)(2,1)S(1)}, bf16[512,128]{1,0:T(8,128)(2,1)S(1)}, u32[]{:S(2)}, u32[]{:S(2)}) %collective-permute-start.26) | collective-permute-done | bytes 131104 | tf_op jit(solution)/shard_map/ppermute | solution.py:243
  75.3 2.7 %collective-permute-start.27 = (bf16[256,128]{1,0:T(8,128)(2,1)S(1)}, bf16[256,128]{1,0:T(8,128)(2,1)S(1)}, u32[]{:S(2)}, u32[]{:S(2)}) collective-permute-start(bf16[256,128]{1,0:T(8,128)(2,1)S(1)} %slice.35), channel_id=1, source_target_pairs={{0,16},{4,20},{8,24},{12,28},{16,0},{20,4},{24,8},{28,12},{1,17},{... | collective-permute-start | bytes 196616 | tf_op jit(solution)/shard_map/ppermute | solution.py:240
  78.7 1.8 %collective-permute-done.27 = bf16[256,128]{1,0:T(8,128)(2,1)S(1)} collective-permute-done((bf16[256,128]{1,0:T(8,128)(2,1)S(1)}, bf16[256,128]{1,0:T(8,128)(2,1)S(1)}, u32[]{:S(2)}, u32[]{:S(2)}) %collective-permute-start.27) | collective-permute-done | bytes 65568 | tf_op jit(solution)/shard_map/ppermute | solution.py:240
  (99 shorter events, 22.0 us)
Async XLA Ops:
  0.6 14.5 %collective-permute-start.12 = (bf16[256,128]{1,0:T(8,128)(2,1)}, bf16[256,128]{1,0:T(8,128)(2,1)S(1)}, u32[]{:S(2)}, u32[]{:S(2)}) collective-permute-start(bf16[256,128]{1,0:T(8,128)(2,1)} %bitcast.9), channel_id=1, source_target_pairs={{0,16},{4,20},{8,24},{12,28},{16,0},{20,4},{24,8},{28,12},{1,17},{... | collective-permute-start | bytes 196616 | tf_op jit(solution)/shard_map/ppermute | solution.py:240
  4.7 7.2 %collective-permute-start.2 = (bf16[256,128]{1,0:T(8,128)(2,1)}, bf16[256,128]{1,0:T(8,128)(2,1)S(1)}, u32[]{:S(2)}, u32[]{:S(2)}) collective-permute-start(bf16[256,128]{1,0:T(8,128)(2,1)} %bitcast.7), channel_id=1, source_target_pairs={{0,16},{4,20},{8,24},{12,28},{16,0},{20,4},{24,8},{28,12},{1,17},{... | collective-permute-start | bytes 196616 | tf_op jit(solution)/shard_map/ppermute | solution.py:240
  8.7 7.0 %collective-permute-start.1 = (bf16[128,128]{1,0:T(8,128)(2,1)S(1)}, bf16[128,128]{1,0:T(8,128)(2,1)S(1)}, u32[]{:S(2)}, u32[]{:S(2)}) collective-permute-start(bf16[128,128]{1,0:T(8,128)(2,1)S(1)} %get-tuple-element.39), channel_id=1, source_target_pairs={{0,8},{4,12},{8,0},{12,4},{16,24},{20,28},{24,16},{28,20},{1,9},{5... | collective-permute-start | bytes 98312 | tf_op jit(solution)/shard_map/ppermute | solution.py:240
  12.0 6.9 %collective-permute-start.5 = (bf16[512,128]{1,0:T(8,128)(2,1)S(1)}, bf16[512,128]{1,0:T(8,128)(2,1)S(1)}, u32[]{:S(2)}, u32[]{:S(2)}) collective-permute-start(bf16[512,128]{1,0:T(8,128)(2,1)S(1)} %pad_maximum_fusion.4.refs_4_), channel_id=1, source_target_pairs={{0,3},{1,2},{2,1},{3,0},{4,7},{5,6},{6,5},{7,4},{8,11},{9,10},{10,... | collective-permute-start | bytes 393224 | tf_op jit(solution)/shard_map/ppermute | solution.py:243
  14.6 15.0 %collective-permute-start = (bf16[128,1024]{1,0:T(8,128)(2,1)S(1)}, bf16[128,1024]{1,0:T(8,128)(2,1)S(1)}, u32[]{:S(2)}, u32[]{:S(2)}) collective-permute-start(bf16[128,1024]{1,0:T(8,128)(2,1)S(1)} %pad_maximum_fusion.1), channel_id=1, source_target_pairs={{0,8},{4,12},{8,0},{12,4},{16,24},{20,28},{24,16},{28,20},{1,9},{5... | collective-permute-start | bytes 786440 | tf_op jit(solution)/shard_map/ppermute | solution.py:240
  15.1 9.5 %collective-permute-start.4 = (bf16[512,128]{1,0:T(8,128)(2,1)S(1)}, bf16[512,128]{1,0:T(8,128)(2,1)S(1)}, u32[]{:S(2)}, u32[]{:S(2)}) collective-permute-start(bf16[512,128]{1,0:T(8,128)(2,1)S(1)} %pad_maximum_fusion.4.refs_4_), channel_id=1, source_target_pairs={{0,2},{1,3},{2,0},{3,1},{4,6},{5,7},{6,4},{7,5},{8,10},{9,11},{10,... | collective-permute-start | bytes 393224 | tf_op jit(solution)/shard_map/ppermute | solution.py:243
  15.6 8.9 %collective-permute-start.3 = (bf16[512,128]{1,0:T(8,128)(2,1)S(1)}, bf16[512,128]{1,0:T(8,128)(2,1)S(1)}, u32[]{:S(2)}, u32[]{:S(2)}) collective-permute-start(bf16[512,128]{1,0:T(8,128)(2,1)S(1)} %pad_maximum_fusion.4.refs_4_), channel_id=1, source_target_pairs={{0,1},{1,0},{2,3},{3,2},{4,5},{5,4},{6,7},{7,6},{8,9},{9,8},{10,11... | collective-permute-start | bytes 393224 | tf_op jit(solution)/shard_map/ppermute | solution.py:243
  16.0 8.6 %collective-permute-start.15 = (bf16[512,128]{1,0:T(8,128)(2,1)S(1)}, bf16[512,128]{1,0:T(8,128)(2,1)S(1)}, u32[]{:S(2)}, u32[]{:S(2)}) collective-permute-start(bf16[512,128]{1,0:T(8,128)(2,1)S(1)} %pad_maximum_fusion.5.refs_4_), channel_id=1, source_target_pairs={{0,3},{1,2},{2,1},{3,0},{4,7},{5,6},{6,5},{7,4},{8,11},{9,10},{10,... | collective-permute-start | bytes 393224 | tf_op jit(solution)/shard_map/ppermute | solution.py:243
  18.9 8.3 %collective-permute-start.14 = (bf16[512,128]{1,0:T(8,128)(2,1)S(1)}, bf16[512,128]{1,0:T(8,128)(2,1)S(1)}, u32[]{:S(2)}, u32[]{:S(2)}) collective-permute-start(bf16[512,128]{1,0:T(8,128)(2,1)S(1)} %pad_maximum_fusion.5.refs_4_), channel_id=1, source_target_pairs={{0,2},{1,3},{2,0},{3,1},{4,6},{5,7},{6,4},{7,5},{8,10},{9,11},{10,... | collective-permute-start | bytes 393224 | tf_op jit(solution)/shard_map/ppermute | solution.py:243
  29.5 8.2 %collective-permute-start.19 = (bf16[512,128]{1,0:T(8,128)(2,1)S(1)}, bf16[512,128]{1,0:T(8,128)(2,1)S(1)}, u32[]{:S(2)}, u32[]{:S(2)}) collective-permute-start(bf16[512,128]{1,0:T(8,128)(2,1)S(1)} %collective-permute-done.15.refs_7_), channel_id=1, source_target_pairs={{0,4},{4,0},{8,12},{12,8},{16,20},{20,16},{24,28},{28,24},{1,5},{5... | collective-permute-start | bytes 393224 | tf_op jit(solution)/shard_map/ppermute | solution.py:240
  30.0 7.6 %collective-permute-start.18 = (bf16[512,128]{1,0:T(8,128)(2,1)S(1)}, bf16[512,128]{1,0:T(8,128)(2,1)S(1)}, u32[]{:S(2)}, u32[]{:S(2)}) collective-permute-start(bf16[512,128]{1,0:T(8,128)(2,1)S(1)} %collective-permute-done.14.refs_6_), channel_id=1, source_target_pairs={{0,4},{4,0},{8,12},{12,8},{16,20},{20,16},{24,28},{28,24},{1,5},{5... | collective-permute-start | bytes 393224 | tf_op jit(solution)/shard_map/ppermute | solution.py:240
  30.1 7.6 %collective-permute-start.17 = (bf16[512,128]{1,0:T(8,128)(2,1)S(1)}, bf16[512,128]{1,0:T(8,128)(2,1)S(1)}, u32[]{:S(2)}, u32[]{:S(2)}) collective-permute-start(bf16[512,128]{1,0:T(8,128)(2,1)S(1)} %collective-permute-done.13.refs_5_), channel_id=1, source_target_pairs={{0,4},{4,0},{8,12},{12,8},{16,20},{20,16},{24,28},{28,24},{1,5},{5... | collective-permute-start | bytes 393224 | tf_op jit(solution)/shard_map/ppermute | solution.py:240
  35.3 9.4 %collective-permute-start.21 = (bf16[128,1024]{1,0:T(8,128)(2,1)S(1)}, bf16[128,1024]{1,0:T(8,128)(2,1)S(1)}, u32[]{:S(2)}, u32[]{:S(2)}) collective-permute-start(bf16[128,1024]{1,0:T(8,128)(2,1)S(1)} %pad_maximum_fusion.3), channel_id=1, source_target_pairs={{0,8},{4,12},{8,0},{12,4},{16,24},{20,28},{24,16},{28,20},{1,9},{5... | collective-permute-start | bytes 786440 | tf_op jit(solution)/shard_map/ppermute | solution.py:240
  35.7 7.5 %collective-permute-start.11 = (bf16[128,128]{1,0:T(8,128)(2,1)S(1)}, bf16[128,128]{1,0:T(8,128)(2,1)S(1)}, u32[]{:S(2)}, u32[]{:S(2)}) collective-permute-start(bf16[128,128]{1,0:T(8,128)(2,1)S(1)} %get-tuple-element.43.refs_0_.value_grad_ref.refs_1_), channel_id=1, source_target_pairs={{0,8},{4,12},{8,0},{12,4},{16,24},{20,28},{24,16},{28,20},{1,9},{5... | collective-permute-start | bytes 98312 | tf_op jit(solution)/shard_map/ppermute | solution.py:240
  43.9 15.0 %collective-permute-start.20 = (bf16[128,1024]{1,0:T(8,128)(2,1)S(1)}, bf16[128,1024]{1,0:T(8,128)(2,1)}, u32[]{:S(2)}, u32[]{:S(2)}) collective-permute-start(bf16[128,1024]{1,0:T(8,128)(2,1)S(1)} %get-tuple-element.45), channel_id=1, source_target_pairs={{0,8},{4,12},{8,0},{12,4},{16,24},{20,28},{24,16},{28,20},{1,9},{5... | collective-permute-start | bytes 786440 | tf_op jit(solution)/shard_map/ppermute | solution.py:240
  45.2 6.4 %collective-permute-start.22 = (bf16[128,256]{1,0:T(8,128)(2,1)S(1)}, bf16[128,256]{1,0:T(8,128)(2,1)S(1)}, u32[]{:S(2)}, u32[]{:S(2)}) collective-permute-start(bf16[128,256]{1,0:T(8,128)(2,1)S(1)} %get-tuple-element.48), channel_id=1, source_target_pairs={{0,8},{4,12},{8,0},{12,4},{16,24},{20,28},{24,16},{28,20},{1,9},{5... | collective-permute-start | bytes 196616 | tf_op jit(solution)/shard_map/ppermute | solution.py:240
  58.4 8.0 %collective-permute-start.23 = (bf16[4,512,128]{2,1,0:T(8,128)(2,1)S(1)}, bf16[4,512,128]{2,1,0:T(8,128)(2,1)S(1)}, u32[]{:S(2)}, u32[]{:S(2)}) collective-permute-start(bf16[4,512,128]{2,1,0:T(8,128)(2,1)S(1)} %get-tuple-element.59), channel_id=1, source_target_pairs={{0,4},{4,0},{8,12},{12,8},{16,20},{20,16},{24,28},{28,24},{1,5},{5... | collective-permute-start | bytes 1572872 | tf_op jit(solution)/shard_map/ppermute | solution.py:240
  61.1 7.8 %collective-permute-start.30 = (bf16[512,128]{1,0:T(8,128)(2,1)S(1)}, bf16[512,128]{1,0:T(8,128)(2,1)S(1)}, u32[]{:S(2)}, u32[]{:S(2)}) collective-permute-start(bf16[512,128]{1,0:T(8,128)(2,1)S(1)} %get-tuple-element.67), channel_id=1, source_target_pairs={{0,1},{1,0},{2,3},{3,2},{4,5},{5,4},{6,7},{7,6},{8,9},{9,8},{10,11... | collective-permute-start | bytes 393224 | tf_op jit(solution)/shard_map/ppermute | solution.py:243
  61.2 9.5 %collective-permute-start.31 = (bf16[512,128]{1,0:T(8,128)(2,1)S(1)}, bf16[512,128]{1,0:T(8,128)(2,1)S(1)}, u32[]{:S(2)}, u32[]{:S(2)}) collective-permute-start(bf16[512,128]{1,0:T(8,128)(2,1)S(1)} %get-tuple-element.68), channel_id=1, source_target_pairs={{0,2},{1,3},{2,0},{3,1},{4,6},{5,7},{6,4},{7,5},{8,10},{9,11},{10,... | collective-permute-start | bytes 393224 | tf_op jit(solution)/shard_map/ppermute | solution.py:243
  62.9 7.8 %collective-permute-start.32 = (bf16[512,128]{1,0:T(8,128)(2,1)S(1)}, bf16[512,128]{1,0:T(8,128)(2,1)S(1)}, u32[]{:S(2)}, u32[]{:S(2)}) collective-permute-start(bf16[512,128]{1,0:T(8,128)(2,1)S(1)} %get-tuple-element.69), channel_id=1, source_target_pairs={{0,3},{1,2},{2,1},{3,0},{4,7},{5,6},{6,5},{7,4},{8,11},{9,10},{10,... | collective-permute-start | bytes 393224 | tf_op jit(solution)/shard_map/ppermute | solution.py:243
  67.2 6.4 %collective-permute-start.24 = (bf16[512,128]{1,0:T(8,128)(2,1)S(1)}, bf16[512,128]{1,0:T(8,128)(2,1)S(1)}, u32[]{:S(2)}, u32[]{:S(2)}) collective-permute-start(bf16[512,128]{1,0:T(8,128)(2,1)S(1)} %get-tuple-element.61), channel_id=1, source_target_pairs={{0,1},{1,0},{2,3},{3,2},{4,5},{5,4},{6,7},{7,6},{8,9},{9,8},{10,11... | collective-permute-start | bytes 393224 | tf_op jit(solution)/shard_map/ppermute | solution.py:243
  67.3 6.5 %collective-permute-start.25 = (bf16[512,128]{1,0:T(8,128)(2,1)S(1)}, bf16[512,128]{1,0:T(8,128)(2,1)S(1)}, u32[]{:S(2)}, u32[]{:S(2)}) collective-permute-start(bf16[512,128]{1,0:T(8,128)(2,1)S(1)} %get-tuple-element.62), channel_id=1, source_target_pairs={{0,2},{1,3},{2,0},{3,1},{4,6},{5,7},{6,4},{7,5},{8,10},{9,11},{10,... | collective-permute-start | bytes 393224 | tf_op jit(solution)/shard_map/ppermute | solution.py:243
  68.9 6.3 %collective-permute-start.26 = (bf16[512,128]{1,0:T(8,128)(2,1)S(1)}, bf16[512,128]{1,0:T(8,128)(2,1)S(1)}, u32[]{:S(2)}, u32[]{:S(2)}) collective-permute-start(bf16[512,128]{1,0:T(8,128)(2,1)S(1)} %get-tuple-element.63), channel_id=1, source_target_pairs={{0,3},{1,2},{2,1},{3,0},{4,7},{5,6},{6,5},{7,4},{8,11},{9,10},{10,... | collective-permute-start | bytes 393224 | tf_op jit(solution)/shard_map/ppermute | solution.py:243
  70.8 7.3 %collective-permute-start.33 = (bf16[256,128]{1,0:T(8,128)(2,1)S(1)}, bf16[256,128]{1,0:T(8,128)(2,1)S(1)}, u32[]{:S(2)}, u32[]{:S(2)}) collective-permute-start(bf16[256,128]{1,0:T(8,128)(2,1)S(1)} %slice.34), channel_id=1, source_target_pairs={{0,16},{4,20},{8,24},{12,28},{16,0},{20,4},{24,8},{28,12},{1,17},{... | collective-permute-start | bytes 196616 | tf_op jit(solution)/shard_map/ppermute | solution.py:240
  (18 other events, 53.3 us)

commit v2 on v0

v2 whole, which is shorter than its diff:
```python
import math

import jax
import jax.numpy as jnp
from jax import lax
from jax.experimental import pallas as pl
from jax.experimental.pallas import tpu as pltpu
from jax.sharding import PartitionSpec as P

F32, BF16 = jnp.float32, jnp.bfloat16
VALUE_GATE, OUTPUT_GATE, VALUE_ROUTE, OUTPUT_ROUTE, LOW_PART = 0, 2, 4, 6, 8


def kernel_call(body, outs, *args, scalars=0, flops=0, where=pltpu.VMEM, scratch=(), vmem=24):
    moved = sum(x.size * x.dtype.itemsize for x in args) + sum(
        math.prod(s) * jnp.dtype(t).itemsize for s, t in outs
    )
    return pl.pallas_call(
        body,
        out_shape=[jax.ShapeDtypeStruct(s, t) for s, t in outs],
        in_specs=[pl.BlockSpec(memory_space=pltpu.SMEM)] * scalars
        + [pl.BlockSpec(memory_space=where)] * (len(args) - scalars),
        out_specs=[pl.BlockSpec(memory_space=pltpu.VMEM)] * len(outs),
        cost_estimate=pl.CostEstimate(flops=flops, bytes_accessed=moved, transcendentals=0),
        scratch_shapes=list(scratch),
        compiler_params=pltpu.CompilerParams(vmem_limit_bytes=vmem * 2**20),
    )(*args)


def dot(left, right):
    return jnp.dot(left, right, preferred_element_type=F32)


def dot_nt(left, right):
    return lax.dot_general(left, right, (((1,), (1,)), ((), ())), preferred_element_type=F32)


def probs_body(q_ref, k_ref, probs_ref, weights_ref, back_ref):
    length = q_ref.shape[0]
    scores = dot_nt(q_ref[...], k_ref[...]) / math.sqrt(q_ref.shape[1])
    row_ids = lax.broadcasted_iota(jnp.int32, (length, length), 0)
    col_ids = lax.broadcasted_iota(jnp.int32, (length, length), 1)
    scores = jnp.where(row_ids >= col_ids, scores, -1e30)
    exponent = jnp.exp(scores - jnp.max(scores, axis=1, keepdims=True))
    probs = exponent / jnp.sum(exponent, axis=1, keepdims=True)
    probs_ref[...] = probs
    weights_ref[...] = probs.astype(BF16)
    back_ref[...] = probs.T.astype(BF16)


def token_table(me, logits, route_v, route_o):
    both, rows = logits.shape
    experts = both // 2
    gates = jax.nn.sigmoid(logits)
    ids = lax.broadcasted_iota(jnp.int32, (both, rows), 0)
    high, low = [], []
    for routes, first in ((route_v, 0), (route_o, experts)):
        for j in range(2):
            gate = jnp.sum(
                jnp.where(ids == routes[j : j + 1] + first, gates, 0.0), axis=0, keepdims=True
            )
            high.append(gate.astype(BF16).astype(F32))
            low.append(gate - high[-1])
    routes = [(routes ^ me).astype(F32) for routes in (route_v, route_o)]
    table = jnp.concatenate(high + routes + low, axis=0)
    return jnp.concatenate([table, jnp.zeros((128 - table.shape[0], rows), F32)], axis=0).T


def quad_table_body(column, *refs):
    out_ref = refs[-1]
    for i, ref in enumerate(refs[:-1]):
        rows = ref.shape[0]
        table = ref[:, column:].astype(F32)
        out_ref[i * rows : (i + 1) * rows, :] = jnp.concatenate(
            [
                table[:, :VALUE_ROUTE] + table[:, LOW_PART : LOW_PART + VALUE_ROUTE],
                table[:, VALUE_ROUTE:],
            ],
            axis=1,
        )


def pack_body(block, quads, at_ref, me_ref, tokens_ref, cotangent_ref, *refs):
    small_refs, out_refs, held_refs, sems = refs[:3], refs[3:7], refs[7:10], refs[10]
    copies = [
        pltpu.make_async_copy(ref, held, sems.at[i])
        for i, (ref, held) in enumerate(zip(small_refs, held_refs))
    ]
    for flip in (3, 2, 1, 0):
        for m, ref in enumerate((tokens_ref, cotangent_ref)):
            for k in range(quads):
                start = pl.multiple_of((at_ref[0] ^ (4 * k + flip)) * block, block)
                to = (m * quads + k) * block
                copies.append(
                    pltpu.make_async_copy(
                        ref.at[:, pl.ds(start, block)],
                        out_refs[flip].at[:, to : to + block],
                        sems.at[len(copies)],
                    )
                )
    for copy in copies:
        copy.start()
    for copy in copies[:3]:
        copy.wait()
    table = token_table(me_ref[0], *[held[...] for held in held_refs]).astype(BF16)
    for flip, out_ref in enumerate(out_refs):
        if flip != 2:
            out_ref[:, 2 * quads * block :] = table
    for copy in copies[3:]:
        copy.wait()


def table_body(me_ref, logits_ref, vr_ref, or_ref, out_ref):
    out_ref[...] = token_table(me_ref[0], logits_ref[...], vr_ref[...], or_ref[...]).astype(BF16)


def unpack_body(block, quads, at_ref, own_ref, core_ref, beside_ref, out_ref):
    half = quads * block
    for flip, (ref, first) in enumerate(
        ((own_ref, 0), (core_ref, 0), (beside_ref, 0), (beside_ref, half))
    ):
        for k in range(quads):
            start = pl.multiple_of((at_ref[0] ^ (4 * k + flip)) * block, block)
            out_ref[:, pl.ds(start, block)] = ref[:, first + k * block : first + (k + 1) * block]


def turn_body(*refs):
    out_ref = refs[-1]
    for i, ref in enumerate(refs[:-1]):
        rows = ref.shape[0]
        out_ref[:, i * rows : (i + 1) * rows] = ref[:, : out_ref.shape[0]].T


def turn_bank_body(experts, chunks, size, *refs):
    for e in range(experts):
        refs[-1][e * size : (e + 1) * size, :] = bank(refs[e * chunks : (e + 1) * chunks], 0).T


def bank(refs, side):
    return jnp.concatenate([ref[side] for ref in refs], axis=0)


def bank_pair(refs, chunks, side, i):
    return jnp.concatenate(
        [bank(refs[e * chunks : (e + 1) * chunks], side) for e in (i, i + 1)], axis=1
    )


def partial_body(experts, chunks, size, half, *refs):
    row_refs, table_ref, weights = refs[:4], refs[4], refs[5 : 5 + experts * chunks]
    keep_ref, send_ref = refs[-2:]
    count = row_refs[0].shape[0]
    for side, route in ((0, VALUE_ROUTE), (1, OUTPUT_ROUTE)):
        left = jnp.concatenate([r[:, side * half : (side + 1) * half] for r in row_refs], axis=0)
        routes = [table_ref[:, route + j : route + j + 1] for j in range(2)]
        slots = [jnp.zeros((4 * count, size), F32) for _ in range(2)]
        for i in range(0, experts, 2):
            product = dot(left, bank_pair(weights, chunks, side, i))
            for p in range(2):
                piece = product[:, p * size : (p + 1) * size]
                for j in range(2):
                    slots[j] = jnp.where(routes[j] == float(i + p), piece, slots[j])
        for j in range(2):
            lanes = slice((2 * side + j) * size, (2 * side + j + 1) * size)
            keep_ref[:, lanes] = slots[j][: 2 * count]
            send_ref[:, lanes] = slots[j][2 * count :].astype(BF16)


def core_sum_body(keep_ref, got_ref, own_ref, send_ref):
    count = own_ref.shape[0]
    own_ref[...] = keep_ref[:count] + got_ref[:count].astype(F32)
    send_ref[...] = (keep_ref[count:] + got_ref[count:].astype(F32)).astype(BF16)


def middle_body(keep_ref, got_ref, table_ref, weights_ref, back_ref, slots_ref, mixed_ref, grad_ref, sent_ref):
    count, size = mixed_ref.shape
    slots = (keep_ref[...] + got_ref[...].astype(F32)).astype(BF16)
    slots_ref[...] = slots
    gated = []
    for gate, base in ((VALUE_GATE, 0), (OUTPUT_GATE, 2)):
        total = jnp.zeros((count, size), F32)
        for j in range(2):
            rows = slots[:, (base + j) * size : (base + j + 1) * size].astype(F32)
            total += table_ref[:count, gate + j : gate + j + 1] * rows
        gated.append(total.astype(BF16))
    mixed_ref[...], grad_ref[...] = gated
    sent_ref[:, :size] = dot(weights_ref[...], gated[0]).astype(BF16)
    sent_ref[:, size:] = dot(back_ref[...], gated[1]).astype(BF16)


def gated_rows(experts, table_ref, gate, route, rows):
    gates = [table_ref[:, gate + j : gate + j + 1] for j in range(2)]
    routes = [table_ref[:, route + j : route + j + 1] for j in range(2)]
    gated = []
    for k in range(experts):
        column = sum(jnp.where(r == float(k), g, 0.0) for g, r in zip(gates, routes))
        gated.append((column * rows).astype(BF16))
    return gated


def weight_grad_body(experts, chunks, size, turned_ref, bank_ref, table_ref, *refs):
    row_refs, out_refs, back_refs = refs[:4], refs[4:-3], refs[-3:]
    half, count = turned_ref.shape[0] // 2, row_refs[0].shape[0]
    for side, gate, route, at in (
        (0, VALUE_GATE, VALUE_ROUTE, 1),
        (1, OUTPUT_GATE, OUTPUT_ROUTE, 0),
    ):
        rows = jnp.concatenate([r[:, at * size : (at + 1) * size] for r in row_refs], axis=0)
        gated = gated_rows(experts, table_ref, gate, route, rows.astype(F32))
        left = turned_ref[side * half : (side + 1) * half, :]
        for i in range(0, experts, 2):
            product = dot(left, jnp.concatenate(gated[i : i + 2], axis=1))
            for p in range(2):
                start = 0
                for out_ref in out_refs[(i + p) * chunks : (i + p + 1) * chunks]:
                    stop = start + out_ref.shape[1]
                    out_ref[side] = product[start:stop, p * size : (p + 1) * size].astype(
                        out_ref.dtype
                    )
                    start = stop
        if side == 0:
            back = dot(jnp.concatenate(gated, axis=1), bank_ref[...]).astype(BF16)
            back_refs[0][...], back_refs[1][...] = back[:count], back[count : 2 * count]
            back_refs[2][...] = back[2 * count :]


def merge_body(beside_ref, got_ref, own_ref, send_ref):
    count, half = beside_ref.shape
    own_ref[...] = got_ref[:count]
    send_ref[:, :half] = beside_ref[...]
    send_ref[:, half:] = got_ref[count:]


def chunk_sum_body(*refs):
    total = refs[0][...]
    for ref in refs[1:-1]:
        total += ref[...].astype(F32)
    refs[-1][...] = total.astype(BF16)


def final_sum_body(groups, *refs):
    total = refs[0][...]
    for ref in refs[1:-2]:
        total += ref[...].astype(F32)
    total = total / groups
    for side in range(2):
        refs[side - 2][0] = total[side]


def attention_back_body(vr_ref, or_ref, table_ref, probs_ref, q_ref, k_ref, mixed_ref, slots_ref, grad_ref, rows_ref, query_grad_ref, key_grad_ref, logit_ref):
    count, size = q_ref.shape
    both = logit_ref.shape[1]
    probs = probs_ref[...]
    prob_grad = dot_nt(grad_ref[...], mixed_ref[...])
    score_grad = probs * (prob_grad - jnp.sum(prob_grad * probs, axis=1, keepdims=True))
    scaled = score_grad / math.sqrt(size)
    query_grad_ref[...] = dot(scaled.astype(BF16), k_ref[...]).astype(BF16)
    key_grad_ref[...] = dot(scaled.T.astype(BF16), q_ref[...]).astype(BF16)
    ids = lax.broadcasted_iota(jnp.int32, (count, both), 1)
    logit = jnp.zeros((count, both), F32)
    for gate_at, route, at, base, first in (
        (VALUE_GATE, vr_ref, 1, 0, 0),
        (OUTPUT_GATE, or_ref, 0, 2, both // 2),
    ):
        rows = rows_ref[:, at * size : (at + 1) * size].astype(F32)
        for j in range(2):
            gate = table_ref[:count, gate_at + j : gate_at + j + 1]
            other = slots_ref[:, (base + j) * size : (base + j + 1) * size].astype(F32)
            gate_grad = jnp.sum(rows * other, axis=1, keepdims=True)
            logit = jnp.where(
                ids == route[:, j : j + 1] + first, gate_grad * gate * (1.0 - gate), logit
            )
    logit_ref[...] = logit


def on_device(
    tokens,
    queries,
    key_vectors,
    gate_logits,
    value_routes,
    output_routes,
    value_weight,
    output_weight,
    cotangent,
):
    count, features = tokens.shape
    size = queries.shape[1]
    experts = gate_logits.shape[1] // 2
    block = value_weight.shape[1]
    groups = lax.axis_size("dp")
    quads = groups // 4
    half = quads * block
    at = lax.axis_index("dp")
    me = lax.axis_index("expert")
    aligned = block % 128 == 0

    def over_dp(x, flip, what):
        with jax.named_scope(f"{what}_dp{flip}"):
            return lax.ppermute(x, "dp", [(i, i ^ flip) for i in range(groups)])

    def over_experts(x, flip, what):
        with jax.named_scope(f"{what}_expert{flip}"):
            return lax.ppermute(x, "expert", [(i, i ^ flip) for i in range(experts)])

    def side_by_side(arrays, axis):
        return arrays[0] if len(arrays) == 1 else jnp.concatenate(arrays, axis=axis)

    own_banks = jnp.concatenate([value_weight, output_weight], axis=0)
    other_banks = side_by_side([over_dp(own_banks, 4 * k, "banks") for k in range(1, quads)], 1)
    first_round = [over_experts(own_banks, k, "banks") for k in range(1, experts)]

    if aligned:
        packed = kernel_call(
            lambda *refs: pack_body(block, quads, *refs),
            [((count, 2 * half + (0 if flip == 2 else 128)), BF16) for flip in range(4)],
            at[None],
            me[None],
            tokens,
            cotangent,
            gate_logits.T,
            value_routes.T,
            output_routes.T,
            scalars=2,
            where=pl.ANY,
            scratch=[
                pltpu.VMEM((2 * experts, count), F32),
                pltpu.VMEM((2, count), jnp.int32),
                pltpu.VMEM((2, count), jnp.int32),
                pltpu.SemaphoreType.DMA((3 + 8 * quads,)),
            ],
            vmem=48,
        )
    else:
        (own_table,) = kernel_call(
            table_body,
            [((count, 128), BF16)],
            me[None],
            gate_logits.T,
            value_routes.T,
            output_routes.T,
            scalars=1,
        )
        packed = [
            jnp.concatenate(
                [
                    lax.dynamic_slice(x, (0, (at ^ (4 * k + flip)) * block), (count, block))
                    for x in (tokens, cotangent)
                    for k in range(quads)
                ]
                + ([] if flip == 2 else [own_table]),
                axis=1,
            )
            for flip in range(4)
        ]
    packed = list(packed)
    far_rows = over_dp(packed[3], 2, "far_rows")
    far_rows, other_banks, first_round, packed[2], packed[1] = lax.optimization_barrier(
        (far_rows, other_banks, first_round, packed[2], packed[1])
    )
    banks = [own_banks, other_banks]
    for k in range(1, experts):
        banks += [first_round[k - 1], over_experts(other_banks, k, "other_banks")]
    near_rows = over_dp(packed[2], 2, "near_rows")
    core_rows, core_far_rows = over_dp(packed[1], 1, "rows"), over_dp(far_rows, 1, "rows")
    rows = [packed[0], near_rows, core_rows, core_far_rows]
    (table,) = kernel_call(
        lambda *refs: quad_table_body(2 * half, *refs),
        [((4 * count, 128), F32)],
        packed[0],
        far_rows,
        core_rows,
        core_far_rows,
    )
    probs, weights, weights_back = kernel_call(
        probs_body,
        [((count, count), F32), ((count, count), BF16), ((count, count), BF16)],
        queries,
        key_vectors,
    )

    def from_quad(x, what):
        beside = over_dp(x, 2, what)
        return [x, beside, over_dp(x, 1, what), over_dp(beside, 1, what)]

    (turned_bank,) = kernel_call(
        lambda *refs: turn_bank_body(experts, 2, size, *refs), [((experts * size, half), BF16)], *banks
    )
    (turned,) = kernel_call(turn_body, [((2 * half, 4 * count), BF16)], *rows)

    product_flops = 2 * 4 * count * half * experts * size
    keep, send = kernel_call(
        lambda *refs: partial_body(experts, 2, size, half, *refs),
        [((2 * count, 4 * size), F32), ((2 * count, 4 * size), BF16)],
        *rows,
        table,
        *banks,
        flops=2 * product_flops,
    )
    keep, send = kernel_call(
        core_sum_body,
        [((count, 4 * size), F32), ((count, 4 * size), BF16)],
        keep,
        over_dp(send, 1, "partials"),
    )
    slots, mixed_value, hidden_grad, head_rows = kernel_call(
        middle_body,
        [((count, 4 * size), BF16), ((count, size), BF16), ((count, size), BF16), ((count, 2 * size), BF16)],
        keep,
        over_dp(send, 2, "partials"),
        table,
        weights,
        weights_back,
    )
    quad_rows = from_quad(head_rows, "head_rows")

    shapes = []
    for k in range(experts):
        kind = F32 if k == 0 else BF16
        shapes += [((2, block, size), kind), ((2, half - block, size), kind)]
    *grads, own_back, beside_back, core_back = kernel_call(
        lambda *refs: weight_grad_body(experts, 2, size, *refs),
        shapes + [((count, half), BF16), ((count, half), BF16), ((2 * count, half), BF16)],
        turned,
        turned_bank,
        table,
        *quad_rows,
        flops=3 * product_flops,
    )
    got_back, beside_back = kernel_call(
        merge_body,
        [((count, half), BF16), ((count, 2 * half), BF16)],
        beside_back,
        over_dp(core_back, 1, "token_back"),
    )
    back = [own_back, got_back, over_dp(beside_back, 2, "token_back")]

    def over_all_experts(chunk):
        return [grads[chunk]] + [
            over_experts(grads[2 * k + chunk], k, "grads") for k in range(1, experts)
        ]

    (others,) = kernel_call(
        chunk_sum_body, [((2, half - block, size), BF16)], *over_all_experts(1)
    )
    sums = over_all_experts(0) + [
        over_dp(others[:, (k - 1) * block : k * block], 4 * k, "grads") for k in range(1, quads)
    ]
    value_weight_grad, output_weight_grad = kernel_call(
        lambda *refs: final_sum_body(groups, *refs), [((1, block, size), F32)] * 2, *sums
    )

    if aligned:
        (token_grad,) = kernel_call(
            lambda *refs: unpack_body(block, quads, *refs),
            [((count, features), BF16)],
            at[None],
            *back,
            scalars=1,
        )
    else:
        back = jnp.concatenate(back, axis=1)
        token_grad = jnp.concatenate(
            [
                lax.dynamic_slice(
                    back,
                    (0, (((at ^ b) & 3) * quads + ((at ^ b) >> 2)) * block),
                    (count, block),
                )
                for b in range(groups)
            ],
            axis=1,
        )

    query_grad, key_grad, logit_grad = kernel_call(
        attention_back_body,
        [((count, size), BF16), ((count, size), BF16), ((count, 2 * experts), F32)],
        value_routes,
        output_routes,
        table,
        probs,
        queries,
        key_vectors,
        mixed_value,
        slots,
        hidden_grad,
        head_rows,
    )
    return (token_grad, query_grad, key_grad, logit_grad, value_weight_grad, output_weight_grad)


def solution(mesh):
    rows, banks = P(("dp", "expert"), None), P("expert", "dp", None)
    return jax.shard_map(
        on_device,
        mesh=mesh,
        in_specs=(rows,) * 6 + (banks, banks, rows),
        out_specs=(rows,) * 4 + (banks, banks),
        check_vma=False,
    )
```

time: 175 us -> 65.6 us (0.37)
  blocking collectives: 32 us -> 0 us
  local copies, waits for them, and re-layouts: 25.8 us -> 3.69 us
  other arithmetic: 20.5 us -> 0 us
  waiting for transfers between devices: 45.2 us -> 24.8 us
  between operations: 14.6 us -> 0.8 us
  matrix products: 11.8 us -> 0 us
  Pallas kernels: 0 us -> 7.48 us
  starting transfers between devices: 24.4 us -> 28.5 us
    all_gather x2 -> x0, blocking collectives: 32 us -> none  [the longest x1 16.1 us: on_device(): lax.all_gather(value_weight, 'dp', axis=1, tiled=True)]
    reduce_scatter x2 -> x0, waiting for transfers between devices: 29.2 us -> none  [the longest x1 21 us: on_device(): lax.psum_scatter(grad_value[None].astype(jnp.bfloat16), 'dp', scatter_dim...]
    ppermute x0 -> x25, starting transfers between devices: none -> 28.5 us  [the longest x13 14.4 us: over_dp(): return lax.ppermute(x, 'dp', [(i, i ^ flip) for i in range(groups)])]
    ppermute x0 -> x25, waiting for transfers between devices: none -> 24.8 us  [the longest x13 14.3 us: over_dp(): return lax.ppermute(x, 'dp', [(i, i ^ flip) for i in range(groups)])]
    all_to_all x6 -> x0, starting transfers between devices: 24.3 us -> none  [the longest x3 12.3 us: to_owners(): lax.all_to_all(buffer, 'expert', split_axis=0, concat_axis=0, tiled=True)]
    gather x17 -> x0, local copies, waits for them, and re-layouts: 17.2 us -> none  [the longest x1 3.02 us: on_device(): jnp.take(cotangent, owner_output // 2, axis=0, mode='fill', fill_value=0)]
    all_to_all x6 -> x0, waiting for transfers between devices: 16 us -> none  [the longest x3 11.4 us: from_owners(): lax.all_to_all(buffer, 'expert', split_axis=0, concat_axis=0, tiled=True)]
    dot_general x11 -> x0, matrix products: 11.8 us -> none  [the longest x2 2.89 us: transpose_product(): lax.dot_general(left, right, (((0,), (0,)), ((), ())), preferred_element_...]
  transfers between devices with their start and end apart: 8 -> 25, of which waited for: 6 -> 14; matrix products, arithmetic and copies ran while one was open for 21% -> 1% of each run, Pallas kernels for 0% -> 4%
where the time goes in v2:
time: 65.6 us; the launch traced here: 65.3 us
  starting transfers between devices  28.5 us (43%)
  waiting for transfers between devices  24.8 us (38%)
  Pallas kernels  7.48 us (11%)
  local copies, waits for them, and re-layouts  3.69 us (6%)
  between operations  0.8 us (1%)
    ppermute x13, starting transfers between devices, over_dp(): return lax.ppermute(x, 'dp', [(i, i ^ flip) for i in range(groups)])  14.4 us
    ppermute x13, waiting for transfers between devices, over_dp(): return lax.ppermute(x, 'dp', [(i, i ^ flip) for i in range(groups)])  14.3 us
    ppermute x12, starting transfers between devices, over_experts(): return lax.ppermute(x, 'expert', [(i, i ^ flip) for i in range(experts)])  14.1 us
    ppermute x12, waiting for transfers between devices, over_experts(): return lax.ppermute(x, 'expert', [(i, i ^ flip) for i in range(experts)])  10.5 us
    pallas_call x14, Pallas kernels, kernel_call(): pl.pallas_call(body, out_shape=[jax.ShapeDtypeStruct(s, t) for s, t in ou...  7.48 us
    unnamed x22, local copies, waits for them, and re-layouts  3.68 us
  transfers between devices with their start and end apart: 25, of which 14 were waited for; matrix products, arithmetic and copies ran while one was open for 1% of the time, Pallas kernels for 4%

profile of v2, /device:TPU:0, one launch (start us, length us, event | category | flops | bytes accessed | tf_op | source)
XLA Modules:
  0.0 65.3 jit_solution(926945960784845847)
XLA Ops:
  2.4 1.0 %copy-done.1 = bf16[128,2048]{1,0:T(8,128)(2,1)S(1)} copy-done((bf16[128,2048]{1,0:T(8,128)(2,1)S(1)}, bf16[128,2048]{1,0:T(8,128)(2,1)}, u32[]{:S(2)}) %copy-start.1) | copy-done | bytes 524312
  3.9 3.1 %collective-permute-start = (bf16[128,1152]{1,0:T(8,128)(2,1)S(1)}, bf16[128,1152]{1,0:T(8,128)(2,1)S(1)}, u32[]{:S(2)}, u32[]{:S(2)}) collective-permute-start(bf16[128,1152]{1,0:T(8,128)(2,1)S(1)} %get-tuple-element.47), channel_id=1, source_target_pairs={{0,8},{4,12},{8,0},{12,4},{16,24},{20,28},{24,16},{28,20},{1,9},{5... | collective-permute-start | bytes 884744 | tf_op jit(solution)/shard_map/far_rows_dp2/ppermute | solution.py:300
  7.1 2.5 %collective-permute-start.4 = (bf16[2,256,128]{2,1,0:T(8,128)(2,1)S(1)}, bf16[2,256,128]{2,1,0:T(8,128)(2,1)S(1)}, u32[]{:S(2)}, u32[]{:S(2)}) collective-permute-start(bf16[2,256,128]{2,1,0:T(8,128)(2,1)S(1)} %constant_dynamic-update-slice_fusion.refs_0_.refs_5_), channel_id=1, source_target_pairs={{0,3},{1,2},{2,1},{3,0},{4,7},{5,6},{6,5},{7,4},{8,11},{9,10},{10,... | collective-permute-start | bytes 393224 | tf_op jit(solution)/shard_map/banks_expert3/ppermute | solution.py:304
  10.6 2.6 %collective-permute-start.1 = (bf16[2,256,128]{2,1,0:T(8,128)(2,1)S(1)}, bf16[2,256,128]{2,1,0:T(8,128)(2,1)S(1)}, u32[]{:S(2)}, u32[]{:S(2)}) collective-permute-start(bf16[2,256,128]{2,1,0:T(8,128)(2,1)S(1)} %constant_dynamic-update-slice_fusion.refs_0_.refs_5_), channel_id=1, source_target_pairs={{0,16},{4,20},{8,24},{12,28},{16,0},{20,4},{24,8},{28,12},{1,17},{... | collective-permute-start | bytes 393224 | tf_op jit(solution)/shard_map/banks_dp4/ppermute | solution.py:300
  13.5 2.3 %collective-permute-done.3.refs_4_.refs_9_ = bf16[2,256,128]{2,1,0:T(8,128)(2,1)S(1)} collective-permute-done((bf16[2,256,128]{2,1,0:T(8,128)(2,1)S(1)}, bf16[2,256,128]{2,1,0:T(8,128)(2,1)S(1)}, u32[]{:S(2)}, u32[]{:S(2)}) %collective-permute-start.3) | collective-permute-done | bytes 131104 | tf_op jit(solution)/shard_map/banks_expert2/ppermute | solution.py:304
  15.9 3.4 %collective-permute-done.1.refs_1_.refs_6_ = bf16[2,256,128]{2,1,0:T(8,128)(2,1)S(1)} collective-permute-done((bf16[2,256,128]{2,1,0:T(8,128)(2,1)S(1)}, bf16[2,256,128]{2,1,0:T(8,128)(2,1)S(1)}, u32[]{:S(2)}, u32[]{:S(2)}) %collective-permute-start.1) | collective-permute-done | bytes 131104 | tf_op jit(solution)/shard_map/banks_dp4/ppermute | solution.py:300
  20.2 2.4 %collective-permute-start.10 = (bf16[2,256,128]{2,1,0:T(8,128)(2,1)S(1)}, bf16[2,256,128]{2,1,0:T(8,128)(2,1)S(1)}, u32[]{:S(2)}, u32[]{:S(2)}) collective-permute-start(bf16[2,256,128]{2,1,0:T(8,128)(2,1)S(1)} %collective-permute-done.1.refs_1_.refs_6_), channel_id=1, source_target_pairs={{0,3},{1,2},{2,1},{3,0},{4,7},{5,6},{6,5},{7,4},{8,11},{9,10},{10,... | collective-permute-start | bytes 393224 | tf_op jit(solution)/shard_map/other_banks_expert3/ppermute | solution.py:304
  23.8 2.8 %collective-permute-done.10.refs_7_.refs_12_ = bf16[2,256,128]{2,1,0:T(8,128)(2,1)S(1)} collective-permute-done((bf16[2,256,128]{2,1,0:T(8,128)(2,1)S(1)}, bf16[2,256,128]{2,1,0:T(8,128)(2,1)S(1)}, u32[]{:S(2)}, u32[]{:S(2)}) %collective-permute-start.10) | collective-permute-done | bytes 131104 | tf_op jit(solution)/shard_map/other_banks_expert3/ppermute | solution.py:304
  26.6 2.5 %collective-permute-done.9.refs_5_.refs_10_ = bf16[2,256,128]{2,1,0:T(8,128)(2,1)S(1)} collective-permute-done((bf16[2,256,128]{2,1,0:T(8,128)(2,1)S(1)}, bf16[2,256,128]{2,1,0:T(8,128)(2,1)S(1)}, u32[]{:S(2)}, u32[]{:S(2)}) %collective-permute-start.9) | collective-permute-done | bytes 131104 | tf_op jit(solution)/shard_map/other_banks_expert2/ppermute | solution.py:304
  29.1 1.2 %shard_map.140 = (f32[256,512]{1,0:T(8,128)S(1)}, bf16[256,512]{1,0:T(8,128)(2,1)S(1)}) custom-call(bf16[128,1152]{1,0:T(8,128)(2,1)S(1)} %get-tuple-element.46.refs_0_, bf16[128,1024]{1,0:T(8,128)(2,1)S(1)} %collective-permute-done.5.refs_1_, bf16[128,1152]{1,0:T(8,128)(2,1)S(1)} %collective-permute-done.6.refs_2_, ...), custom_call_target="tpu_custom_call" | custom-call | flops 536870912 | bytes 3244032 | tf_op jit(solution)/shard_map/pallas_call | solution.py:18
  30.4 1.5 %collective-permute-done.11.got_ref = bf16[256,512]{1,0:T(8,128)(2,1)S(1)} collective-permute-done((bf16[256,512]{1,0:T(8,128)(2,1)S(1)}, bf16[256,512]{1,0:T(8,128)(2,1)S(1)}, u32[]{:S(2)}, u32[]{:S(2)}) %collective-permute-start.11) | collective-permute-done | bytes 262176 | tf_op jit(solution)/shard_map/partials_dp1/ppermute | solution.py:300
  32.0 1.7 %collective-permute-start.12 = (bf16[128,512]{1,0:T(8,128)(2,1)S(1)}, bf16[128,512]{1,0:T(8,128)(2,1)S(1)}, u32[]{:S(2)}, u32[]{:S(2)}) collective-permute-start(bf16[128,512]{1,0:T(8,128)(2,1)S(1)} %get-tuple-element.60), channel_id=1, source_target_pairs={{0,8},{4,12},{8,0},{12,4},{16,24},{20,28},{24,16},{28,20},{1,9},{5... | collective-permute-start | bytes 393224 | tf_op jit(solution)/shard_map/partials_dp2/ppermute | solution.py:300
  34.1 3.5 %collective-permute-done.12.got_ref = bf16[128,512]{1,0:T(8,128)(2,1)S(1)} collective-permute-done((bf16[128,512]{1,0:T(8,128)(2,1)S(1)}, bf16[128,512]{1,0:T(8,128)(2,1)S(1)}, u32[]{:S(2)}, u32[]{:S(2)}) %collective-permute-start.12) | collective-permute-done | bytes 131104 | tf_op jit(solution)/shard_map/partials_dp2/ppermute | solution.py:300
  37.9 1.7 %collective-permute-start.13 = (bf16[128,256]{1,0:T(8,128)(2,1)S(1)}, bf16[128,256]{1,0:T(8,128)(2,1)S(1)}, u32[]{:S(2)}, u32[]{:S(2)}) collective-permute-start(bf16[128,256]{1,0:T(8,128)(2,1)S(1)} %get-tuple-element.63.refs_3_.rows_ref), channel_id=1, source_target_pairs={{0,8},{4,12},{8,0},{12,4},{16,24},{20,28},{24,16},{28,20},{1,9},{5... | collective-permute-start | bytes 196616 | tf_op jit(solution)/shard_map/head_rows_dp2/ppermute | solution.py:300
  39.6 2.6 %collective-permute-done.13.refs_4_ = bf16[128,256]{1,0:T(8,128)(2,1)S(1)} collective-permute-done((bf16[128,256]{1,0:T(8,128)(2,1)S(1)}, bf16[128,256]{1,0:T(8,128)(2,1)S(1)}, u32[]{:S(2)}, u32[]{:S(2)}) %collective-permute-start.13) | collective-permute-done | bytes 65568 | tf_op jit(solution)/shard_map/head_rows_dp2/ppermute | solution.py:300
  43.5 1.6 %shard_map.144 = (f32[2,256,128]{2,1,0:T(8,128)S(1)}, f32[2,256,128]{2,1,0:T(8,128)S(1)}, bf16[2,256,128]{2,1,0:T(8,128)(2,1)S(1)}, bf16[2,256,128]{2,1,0:T(8,12...) custom-call(bf16[1024,512]{1,0:T(8,128)(2,1)S(1)} %shard_map.137.ref, ...), custom_call_target="tpu_custom_call" | custom-call | flops 805306368 | bytes 3932160 | tf_op jit(solution)/shard_map/pallas_call | solution.py:18
  45.4 1.5 %collective-permute-start.21 = (bf16[2,256,128]{2,1,0:T(8,128)(2,1)S(1)}, bf16[2,256,128]{2,1,0:T(8,128)(2,1)S(1)}, u32[]{:S(2)}, u32[]{:S(2)}) collective-permute-start(bf16[2,256,128]{2,1,0:T(8,128)(2,1)S(1)} %get-tuple-element.81), channel_id=1, source_target_pairs={{0,1},{1,0},{2,3},{3,2},{4,5},{5,4},{6,7},{7,6},{8,9},{9,8},{10,11... | collective-permute-start | bytes 393224 | tf_op jit(solution)/shard_map/grads_expert1/ppermute | solution.py:304
  47.6 1.2 %collective-permute-start.23 = (bf16[2,256,128]{2,1,0:T(8,128)(2,1)S(1)}, bf16[2,256,128]{2,1,0:T(8,128)(2,1)S(1)}, u32[]{:S(2)}, u32[]{:S(2)}) collective-permute-start(bf16[2,256,128]{2,1,0:T(8,128)(2,1)S(1)} %get-tuple-element.83), channel_id=1, source_target_pairs={{0,3},{1,2},{2,1},{3,0},{4,7},{5,6},{6,5},{7,4},{8,11},{9,10},{10,... | collective-permute-start | bytes 393224 | tf_op jit(solution)/shard_map/grads_expert3/ppermute | solution.py:304
  48.9 1.7 %collective-permute-start.17 = (bf16[128,1024]{1,0:T(8,128)(2,1)S(1)}, bf16[128,1024]{1,0:T(8,128)(2,1)S(1)}, u32[]{:S(2)}, u32[]{:S(2)}) collective-permute-start(bf16[128,1024]{1,0:T(8,128)(2,1)S(1)} %get-tuple-element.68), channel_id=1, source_target_pairs={{0,8},{4,12},{8,0},{12,4},{16,24},{20,28},{24,16},{28,20},{1,9},{5... | collective-permute-start | bytes 786440 | tf_op jit(solution)/shard_map/token_back_dp2/ppermute | solution.py:300
  50.6 1.5 %collective-permute-start.18 = (bf16[2,256,128]{2,1,0:T(8,128)(2,1)S(1)}, bf16[2,256,128]{2,1,0:T(8,128)(2,1)S(1)}, u32[]{:S(2)}, u32[]{:S(2)}) collective-permute-start(bf16[2,256,128]{2,1,0:T(8,128)(2,1)S(1)} %get-tuple-element.77), channel_id=1, source_target_pairs={{0,1},{1,0},{2,3},{3,2},{4,5},{5,4},{6,7},{7,6},{8,9},{9,8},{10,11... | collective-permute-start | bytes 393224 | tf_op jit(solution)/shard_map/grads_expert1/ppermute | solution.py:304
  53.1 2.2 %collective-permute-done.22.refs_2_ = bf16[2,256,128]{2,1,0:T(8,128)(2,1)S(1)} collective-permute-done((bf16[2,256,128]{2,1,0:T(8,128)(2,1)S(1)}, bf16[2,256,128]{2,1,0:T(8,128)(2,1)S(1)}, u32[]{:S(2)}, u32[]{:S(2)}) %collective-permute-start.22) | collective-permute-done | bytes 131104 | tf_op jit(solution)/shard_map/grads_expert2/ppermute | solution.py:304
  56.3 2.4 %collective-permute-start.24 = (bf16[2,256,128]{2,1,0:T(8,128)(2,1)S(1)}, bf16[2,256,128]{2,1,0:T(8,128)(2,1)S(1)}, u32[]{:S(2)}, u32[]{:S(2)}) collective-permute-start(bf16[2,256,128]{2,1,0:T(8,128)(2,1)S(1)} %shard_map.148), channel_id=1, source_target_pairs={{0,16},{4,20},{8,24},{12,28},{16,0},{20,4},{24,8},{28,12},{1,17},{... | collective-permute-start | bytes 393224 | tf_op jit(solution)/shard_map/grads_dp4/ppermute | solution.py:300
  59.0 1.1 %shard_map.147 = (bf16[128,128]{1,0:T(8,128)(2,1)}, bf16[128,128]{1,0:T(8,128)(2,1)}, f32[128,8]{1,0:T(8,128)S(1)}) custom-call(s32[128,2]{1,0:T(8,128)S(1)} %copy.15.vr_ref, s32[128,2]{1,0:T(8,128)S(1)} %copy.16.or_ref, f32[512,128]{1,0:T(8,128)S(1)} %shard_map.139.refs_4_.table_ref.refs_2_, f32[128,128]{1,0:T(8,128)S(1)} %get-tuple-element.69.probs_ref, ...), custom_call_target="tpu_custom_call" | custom-call | bytes 727040 | tf_op jit(solution)/shard_map/pallas_call | solution.py:18
  61.2 2.5 %collective-permute-done.24.refs_4_ = bf16[2,256,128]{2,1,0:T(8,128)(2,1)S(1)} collective-permute-done((bf16[2,256,128]{2,1,0:T(8,128)(2,1)S(1)}, bf16[2,256,128]{2,1,0:T(8,128)(2,1)S(1)}, u32[]{:S(2)}, u32[]{:S(2)}) %collective-permute-start.24) | collective-permute-done | bytes 131104 | tf_op jit(solution)/shard_map/grads_dp4/ppermute | solution.py:300
  (63 shorter events, 13.8 us)
Async XLA Ops:
  3.9 15.4 %collective-permute-start = (bf16[128,1152]{1,0:T(8,128)(2,1)S(1)}, bf16[128,1152]{1,0:T(8,128)(2,1)S(1)}, u32[]{:S(2)}, u32[]{:S(2)}) collective-permute-start(bf16[128,1152]{1,0:T(8,128)(2,1)S(1)} %get-tuple-element.47), channel_id=1, source_target_pairs={{0,8},{4,12},{8,0},{12,4},{16,24},{20,28},{24,16},{28,20},{1,9},{5... | collective-permute-start | bytes 884744 | tf_op jit(solution)/shard_map/far_rows_dp2/ppermute | solution.py:300
  7.1 6.5 %collective-permute-start.4 = (bf16[2,256,128]{2,1,0:T(8,128)(2,1)S(1)}, bf16[2,256,128]{2,1,0:T(8,128)(2,1)S(1)}, u32[]{:S(2)}, u32[]{:S(2)}) collective-permute-start(bf16[2,256,128]{2,1,0:T(8,128)(2,1)S(1)} %constant_dynamic-update-slice_fusion.refs_0_.refs_5_), channel_id=1, source_target_pairs={{0,3},{1,2},{2,1},{3,0},{4,7},{5,6},{6,5},{7,4},{8,11},{9,10},{10,... | collective-permute-start | bytes 393224 | tf_op jit(solution)/shard_map/banks_expert3/ppermute | solution.py:304
  9.6 6.2 %collective-permute-start.3 = (bf16[2,256,128]{2,1,0:T(8,128)(2,1)S(1)}, bf16[2,256,128]{2,1,0:T(8,128)(2,1)S(1)}, u32[]{:S(2)}, u32[]{:S(2)}) collective-permute-start(bf16[2,256,128]{2,1,0:T(8,128)(2,1)S(1)} %constant_dynamic-update-slice_fusion.refs_0_.refs_5_), channel_id=1, source_target_pairs={{0,2},{1,3},{2,0},{3,1},{4,6},{5,7},{6,4},{7,5},{8,10},{9,11},{10,... | collective-permute-start | bytes 393224 | tf_op jit(solution)/shard_map/banks_expert2/ppermute | solution.py:304
  10.1 5.8 %collective-permute-start.2 = (bf16[2,256,128]{2,1,0:T(8,128)(2,1)S(1)}, bf16[2,256,128]{2,1,0:T(8,128)(2,1)S(1)}, u32[]{:S(2)}, u32[]{:S(2)}) collective-permute-start(bf16[2,256,128]{2,1,0:T(8,128)(2,1)S(1)} %constant_dynamic-update-slice_fusion.refs_0_.refs_5_), channel_id=1, source_target_pairs={{0,1},{1,0},{2,3},{3,2},{4,5},{5,4},{6,7},{7,6},{8,9},{9,8},{10,11... | collective-permute-start | bytes 393224 | tf_op jit(solution)/shard_map/banks_expert1/ppermute | solution.py:304
  10.6 8.7 %collective-permute-start.1 = (bf16[2,256,128]{2,1,0:T(8,128)(2,1)S(1)}, bf16[2,256,128]{2,1,0:T(8,128)(2,1)S(1)}, u32[]{:S(2)}, u32[]{:S(2)}) collective-permute-start(bf16[2,256,128]{2,1,0:T(8,128)(2,1)S(1)} %constant_dynamic-update-slice_fusion.refs_0_.refs_5_), channel_id=1, source_target_pairs={{0,16},{4,20},{8,24},{12,28},{16,0},{20,4},{24,8},{28,12},{1,17},{... | collective-permute-start | bytes 393224 | tf_op jit(solution)/shard_map/banks_dp4/ppermute | solution.py:300
  19.3 3.9 %collective-permute-start.6 = (bf16[128,1152]{1,0:T(8,128)(2,1)S(1)}, bf16[128,1152]{1,0:T(8,128)(2,1)S(1)}, u32[]{:S(2)}, u32[]{:S(2)}) collective-permute-start(bf16[128,1152]{1,0:T(8,128)(2,1)S(1)} %get-tuple-element.51), channel_id=1, source_target_pairs={{0,4},{4,0},{8,12},{12,8},{16,20},{20,16},{24,28},{28,24},{1,5},{5... | collective-permute-start | bytes 884744 | tf_op jit(solution)/shard_map/rows_dp1/ppermute | solution.py:300
  19.3 4.4 %collective-permute-start.7 = (bf16[128,1152]{1,0:T(8,128)(2,1)S(1)}, bf16[128,1152]{1,0:T(8,128)(2,1)S(1)}, u32[]{:S(2)}, u32[]{:S(2)}) collective-permute-start(bf16[128,1152]{1,0:T(8,128)(2,1)S(1)} %collective-permute-done.refs_1_), channel_id=1, source_target_pairs={{0,4},{4,0},{8,12},{12,8},{16,20},{20,16},{24,28},{28,24},{1,5},{5... | collective-permute-start | bytes 884744 | tf_op jit(solution)/shard_map/rows_dp1/ppermute | solution.py:300
  19.8 9.3 %collective-permute-start.5 = (bf16[128,1024]{1,0:T(8,128)(2,1)S(1)}, bf16[128,1024]{1,0:T(8,128)(2,1)S(1)}, u32[]{:S(2)}, u32[]{:S(2)}) collective-permute-start(bf16[128,1024]{1,0:T(8,128)(2,1)S(1)} %get-tuple-element.50), channel_id=1, source_target_pairs={{0,8},{4,12},{8,0},{12,4},{16,24},{20,28},{24,16},{28,20},{1,9},{5... | collective-permute-start | bytes 786440 | tf_op jit(solution)/shard_map/near_rows_dp2/ppermute | solution.py:300
  20.2 6.4 %collective-permute-start.10 = (bf16[2,256,128]{2,1,0:T(8,128)(2,1)S(1)}, bf16[2,256,128]{2,1,0:T(8,128)(2,1)S(1)}, u32[]{:S(2)}, u32[]{:S(2)}) collective-permute-start(bf16[2,256,128]{2,1,0:T(8,128)(2,1)S(1)} %collective-permute-done.1.refs_1_.refs_6_), channel_id=1, source_target_pairs={{0,3},{1,2},{2,1},{3,0},{4,7},{5,6},{6,5},{7,4},{8,11},{9,10},{10,... | collective-permute-start | bytes 393224 | tf_op jit(solution)/shard_map/other_banks_expert3/ppermute | solution.py:304
  22.7 6.4 %collective-permute-start.9 = (bf16[2,256,128]{2,1,0:T(8,128)(2,1)S(1)}, bf16[2,256,128]{2,1,0:T(8,128)(2,1)S(1)}, u32[]{:S(2)}, u32[]{:S(2)}) collective-permute-start(bf16[2,256,128]{2,1,0:T(8,128)(2,1)S(1)} %collective-permute-done.1.refs_1_.refs_6_), channel_id=1, source_target_pairs={{0,2},{1,3},{2,0},{3,1},{4,6},{5,7},{6,4},{7,5},{8,10},{9,11},{10,... | collective-permute-start | bytes 393224 | tf_op jit(solution)/shard_map/other_banks_expert2/ppermute | solution.py:304
  23.2 5.9 %collective-permute-start.8 = (bf16[2,256,128]{2,1,0:T(8,128)(2,1)S(1)}, bf16[2,256,128]{2,1,0:T(8,128)(2,1)S(1)}, u32[]{:S(2)}, u32[]{:S(2)}) collective-permute-start(bf16[2,256,128]{2,1,0:T(8,128)(2,1)S(1)} %collective-permute-done.1.refs_1_.refs_6_), channel_id=1, source_target_pairs={{0,1},{1,0},{2,3},{3,2},{4,5},{5,4},{6,7},{7,6},{8,9},{9,8},{10,11... | collective-permute-start | bytes 393224 | tf_op jit(solution)/shard_map/other_banks_expert1/ppermute | solution.py:304
  30.4 1.6 %collective-permute-start.11 = (bf16[256,512]{1,0:T(8,128)(2,1)S(1)}, bf16[256,512]{1,0:T(8,128)(2,1)S(1)}, u32[]{:S(2)}, u32[]{:S(2)}) collective-permute-start(bf16[256,512]{1,0:T(8,128)(2,1)S(1)} %get-tuple-element.58), channel_id=1, source_target_pairs={{0,4},{4,0},{8,12},{12,8},{16,20},{20,16},{24,28},{28,24},{1,5},{5... | collective-permute-start | bytes 786440 | tf_op jit(solution)/shard_map/partials_dp1/ppermute | solution.py:300
  32.0 5.6 %collective-permute-start.12 = (bf16[128,512]{1,0:T(8,128)(2,1)S(1)}, bf16[128,512]{1,0:T(8,128)(2,1)S(1)}, u32[]{:S(2)}, u32[]{:S(2)}) collective-permute-start(bf16[128,512]{1,0:T(8,128)(2,1)S(1)} %get-tuple-element.60), channel_id=1, source_target_pairs={{0,8},{4,12},{8,0},{12,4},{16,24},{20,28},{24,16},{28,20},{1,9},{5... | collective-permute-start | bytes 393224 | tf_op jit(solution)/shard_map/partials_dp2/ppermute | solution.py:300
  37.9 4.3 %collective-permute-start.13 = (bf16[128,256]{1,0:T(8,128)(2,1)S(1)}, bf16[128,256]{1,0:T(8,128)(2,1)S(1)}, u32[]{:S(2)}, u32[]{:S(2)}) collective-permute-start(bf16[128,256]{1,0:T(8,128)(2,1)S(1)} %get-tuple-element.63.refs_3_.rows_ref), channel_id=1, source_target_pairs={{0,8},{4,12},{8,0},{12,4},{16,24},{20,28},{24,16},{28,20},{1,9},{5... | collective-permute-start | bytes 196616 | tf_op jit(solution)/shard_map/head_rows_dp2/ppermute | solution.py:300
  39.6 3.2 %collective-permute-start.14 = (bf16[128,256]{1,0:T(8,128)(2,1)S(1)}, bf16[128,256]{1,0:T(8,128)(2,1)S(1)}, u32[]{:S(2)}, u32[]{:S(2)}) collective-permute-start(bf16[128,256]{1,0:T(8,128)(2,1)S(1)} %get-tuple-element.63.refs_3_.rows_ref), channel_id=1, source_target_pairs={{0,4},{4,0},{8,12},{12,8},{16,20},{20,16},{24,28},{28,24},{1,5},{5... | collective-permute-start | bytes 196616 | tf_op jit(solution)/shard_map/head_rows_dp1/ppermute | solution.py:300
  45.1 3.7 %collective-permute-start.16 = (bf16[256,512]{1,0:T(8,128)(2,1)S(1)}, bf16[256,512]{1,0:T(8,128)(2,1)S(1)}, u32[]{:S(2)}, u32[]{:S(2)}) collective-permute-start(bf16[256,512]{1,0:T(8,128)(2,1)S(1)} %get-tuple-element.66), channel_id=1, source_target_pairs={{0,4},{4,0},{8,12},{12,8},{16,20},{20,16},{24,28},{28,24},{1,5},{5... | collective-permute-start | bytes 786440 | tf_op jit(solution)/shard_map/token_back_dp1/ppermute | solution.py:300
  45.4 6.7 %collective-permute-start.21 = (bf16[2,256,128]{2,1,0:T(8,128)(2,1)S(1)}, bf16[2,256,128]{2,1,0:T(8,128)(2,1)S(1)}, u32[]{:S(2)}, u32[]{:S(2)}) collective-permute-start(bf16[2,256,128]{2,1,0:T(8,128)(2,1)S(1)} %get-tuple-element.81), channel_id=1, source_target_pairs={{0,1},{1,0},{2,3},{3,2},{4,5},{5,4},{6,7},{7,6},{8,9},{9,8},{10,11... | collective-permute-start | bytes 393224 | tf_op jit(solution)/shard_map/grads_expert1/ppermute | solution.py:304
  46.9 8.4 %collective-permute-start.22 = (bf16[2,256,128]{2,1,0:T(8,128)(2,1)S(1)}, bf16[2,256,128]{2,1,0:T(8,128)(2,1)S(1)}, u32[]{:S(2)}, u32[]{:S(2)}) collective-permute-start(bf16[2,256,128]{2,1,0:T(8,128)(2,1)S(1)} %get-tuple-element.82), channel_id=1, source_target_pairs={{0,2},{1,3},{2,0},{3,1},{4,6},{5,7},{6,4},{7,5},{8,10},{9,11},{10,... | collective-permute-start | bytes 393224 | tf_op jit(solution)/shard_map/grads_expert2/ppermute | solution.py:304
  47.6 8.6 %collective-permute-start.23 = (bf16[2,256,128]{2,1,0:T(8,128)(2,1)S(1)}, bf16[2,256,128]{2,1,0:T(8,128)(2,1)S(1)}, u32[]{:S(2)}, u32[]{:S(2)}) collective-permute-start(bf16[2,256,128]{2,1,0:T(8,128)(2,1)S(1)} %get-tuple-element.83), channel_id=1, source_target_pairs={{0,3},{1,2},{2,1},{3,0},{4,7},{5,6},{6,5},{7,4},{8,11},{9,10},{10,... | collective-permute-start | bytes 393224 | tf_op jit(solution)/shard_map/grads_expert3/ppermute | solution.py:304
  48.9 15.5 %collective-permute-start.17 = (bf16[128,1024]{1,0:T(8,128)(2,1)S(1)}, bf16[128,1024]{1,0:T(8,128)(2,1)S(1)}, u32[]{:S(2)}, u32[]{:S(2)}) collective-permute-start(bf16[128,1024]{1,0:T(8,128)(2,1)S(1)} %get-tuple-element.68), channel_id=1, source_target_pairs={{0,8},{4,12},{8,0},{12,4},{16,24},{20,28},{24,16},{28,20},{1,9},{5... | collective-permute-start | bytes 786440 | tf_op jit(solution)/shard_map/token_back_dp2/ppermute | solution.py:300
  50.6 10.2 %collective-permute-start.18 = (bf16[2,256,128]{2,1,0:T(8,128)(2,1)S(1)}, bf16[2,256,128]{2,1,0:T(8,128)(2,1)S(1)}, u32[]{:S(2)}, u32[]{:S(2)}) collective-permute-start(bf16[2,256,128]{2,1,0:T(8,128)(2,1)S(1)} %get-tuple-element.77), channel_id=1, source_target_pairs={{0,1},{1,0},{2,3},{3,2},{4,5},{5,4},{6,7},{7,6},{8,9},{9,8},{10,11... | collective-permute-start | bytes 393224 | tf_op jit(solution)/shard_map/grads_expert1/ppermute | solution.py:304
  52.1 8.6 %collective-permute-start.19 = (bf16[2,256,128]{2,1,0:T(8,128)(2,1)S(1)}, bf16[2,256,128]{2,1,0:T(8,128)(2,1)S(1)}, u32[]{:S(2)}, u32[]{:S(2)}) collective-permute-start(bf16[2,256,128]{2,1,0:T(8,128)(2,1)S(1)} %get-tuple-element.78), channel_id=1, source_target_pairs={{0,2},{1,3},{2,0},{3,1},{4,6},{5,7},{6,4},{7,5},{8,10},{9,11},{10,... | collective-permute-start | bytes 393224 | tf_op jit(solution)/shard_map/grads_expert2/ppermute | solution.py:304
  55.3 5.9 %collective-permute-start.20 = (bf16[2,256,128]{2,1,0:T(8,128)(2,1)S(1)}, bf16[2,256,128]{2,1,0:T(8,128)(2,1)S(1)}, u32[]{:S(2)}, u32[]{:S(2)}) collective-permute-start(bf16[2,256,128]{2,1,0:T(8,128)(2,1)S(1)} %get-tuple-element.79), channel_id=1, source_target_pairs={{0,3},{1,2},{2,1},{3,0},{4,7},{5,6},{6,5},{7,4},{8,11},{9,10},{10,... | collective-permute-start | bytes 393224 | tf_op jit(solution)/shard_map/grads_expert3/ppermute | solution.py:304
  56.3 7.3 %collective-permute-start.24 = (bf16[2,256,128]{2,1,0:T(8,128)(2,1)S(1)}, bf16[2,256,128]{2,1,0:T(8,128)(2,1)S(1)}, u32[]{:S(2)}, u32[]{:S(2)}) collective-permute-start(bf16[2,256,128]{2,1,0:T(8,128)(2,1)S(1)} %shard_map.148), channel_id=1, source_target_pairs={{0,16},{4,20},{8,24},{12,28},{16,0},{20,4},{24,8},{28,12},{1,17},{... | collective-permute-start | bytes 393224 | tf_op jit(solution)/shard_map/grads_dp4/ppermute | solution.py:300
  (10 other events, 15.6 us)

commit v3 on v2

--- a/solution.py
+++ b/solution.py
@@ -35,7 +35,7 @@
     return lax.dot_general(left, right, (((1,), (1,)), ((), ())), preferred_element_type=F32)
 
 
-def probs_body(q_ref, k_ref, probs_ref, weights_ref, back_ref):
+def probs_body(q_ref, k_ref, probs_ref, weights_ref):
     length = q_ref.shape[0]
     scores = dot_nt(q_ref[...], k_ref[...]) / math.sqrt(q_ref.shape[1])
     row_ids = lax.broadcasted_iota(jnp.int32, (length, length), 0)
@@ -45,7 +45,6 @@
     probs = exponent / jnp.sum(exponent, axis=1, keepdims=True)
     probs_ref[...] = probs
     weights_ref[...] = probs.astype(BF16)
-    back_ref[...] = probs.T.astype(BF16)
 
 
 def token_table(me, logits, route_v, route_o):
@@ -121,7 +120,9 @@
     ):
         for k in range(quads):
             start = pl.multiple_of((at_ref[0] ^ (4 * k + flip)) * block, block)
-            out_ref[:, pl.ds(start, block)] = ref[:, first + k * block : first + (k + 1) * block]
+            out_ref[:, pl.ds(start, block)] = ref[
+                : out_ref.shape[0], first + k * block : first + (k + 1) * block
+            ]
 
 
 def turn_body(*refs):
@@ -148,9 +149,9 @@
 
 def partial_body(experts, chunks, size, half, *refs):
     row_refs, table_ref, weights = refs[:4], refs[4], refs[5 : 5 + experts * chunks]
-    keep_ref, send_ref = refs[-2:]
+    slots_ref, keep_ref, send_ref = refs[-3:]
     count = row_refs[0].shape[0]
-    for side, route in ((0, VALUE_ROUTE), (1, OUTPUT_ROUTE)):
+    for side, gate, route in ((0, VALUE_GATE, VALUE_ROUTE), (1, OUTPUT_GATE, OUTPUT_ROUTE)):
         left = jnp.concatenate([r[:, side * half : (side + 1) * half] for r in row_refs], axis=0)
         routes = [table_ref[:, route + j : route + j + 1] for j in range(2)]
         slots = [jnp.zeros((4 * count, size), F32) for _ in range(2)]
@@ -160,32 +161,55 @@
                 piece = product[:, p * size : (p + 1) * size]
                 for j in range(2):
                     slots[j] = jnp.where(routes[j] == float(i + p), piece, slots[j])
+        mixed = sum(table_ref[:, gate + j : gate + j + 1] * slots[j] for j in range(2))
         for j in range(2):
-            lanes = slice((2 * side + j) * size, (2 * side + j + 1) * size)
-            keep_ref[:, lanes] = slots[j][: 2 * count]
-            send_ref[:, lanes] = slots[j][2 * count :].astype(BF16)
-
-
-def core_sum_body(keep_ref, got_ref, own_ref, send_ref):
-    count = own_ref.shape[0]
-    own_ref[...] = keep_ref[:count] + got_ref[:count].astype(F32)
-    send_ref[...] = (keep_ref[count:] + got_ref[count:].astype(F32)).astype(BF16)
-
-
-def middle_body(keep_ref, got_ref, table_ref, weights_ref, back_ref, slots_ref, mixed_ref, grad_ref, sent_ref):
+            slots_ref[:, (2 * side + j) * size : (2 * side + j + 1) * size] = slots[j].astype(BF16)
+        lanes = slice(side * size, (side + 1) * size)
+        keep_ref[:, lanes] = mixed[: 2 * count]
+        send_ref[:, lanes] = mixed[2 * count :].astype(BF16)
+
+
+def core_sum_body(keep_ref, got_ref, weights_ref, sum_ref, send_ref):
+    both, count = keep_ref.shape[0], weights_ref.shape[0]
+    total = keep_ref[...] + got_ref[...].astype(F32)
+    sum_ref[...] = total
+    send_ref[:both, :] = total.astype(BF16)
+    send_ref[both:, :count] = weights_ref[: count // 2, :]
+    send_ref[both:, count:] = weights_ref[count // 2 :, :]
+
+
+def middle_body(sum_ref, got_ref, weights_ref, mixed_ref, grad_ref, rows_ref):
     count, size = mixed_ref.shape
-    slots = (keep_ref[...] + got_ref[...].astype(F32)).astype(BF16)
-    slots_ref[...] = slots
-    gated = []
-    for gate, base in ((VALUE_GATE, 0), (OUTPUT_GATE, 2)):
-        total = jnp.zeros((count, size), F32)
-        for j in range(2):
-            rows = slots[:, (base + j) * size : (base + j + 1) * size].astype(F32)
-            total += table_ref[:count, gate + j : gate + j + 1] * rows
-        gated.append(total.astype(BF16))
-    mixed_ref[...], grad_ref[...] = gated
-    sent_ref[:, :size] = dot(weights_ref[...], gated[0]).astype(BF16)
-    sent_ref[:, size:] = dot(back_ref[...], gated[1]).astype(BF16)
+    far_weights = jnp.concatenate(
+        [got_ref[2 * count :, :count], got_ref[2 * count :, count:]], axis=0
+    )
+    for i, weights in enumerate((weights_ref[...], far_weights)):
+        total = sum_ref[i * count : (i + 1) * count, :] + got_ref[
+            (1 - i) * count : (2 - i) * count, :
+        ].astype(F32)
+        total = total.astype(BF16)
+        if i == 0:
+            mixed_ref[...], grad_ref[...] = total[:, :size], total[:, size:]
+        rows_ref[i * count : (i + 1) * count, :size] = dot(weights, total[:, :size]).astype(BF16)
+        rows_ref[i * count : (i + 1) * count, size:] = lax.dot_general(
+            weights, total[:, size:], (((0,), (0,)), ((), ())), preferred_element_type=F32
+        ).astype(BF16)
+
+
+def two_parts(columns):
+    rows = columns[0].shape[0]
+    lane = lax.broadcasted_iota(jnp.int32, (rows, 128), 1)
+    block = jnp.zeros((rows, 128), F32)
+    for j, column in enumerate(columns):
+        high = column.astype(BF16).astype(F32)
+        block = jnp.where(lane == j, high, block)
+        block = jnp.where(lane == 4 + j, column - high, block)
+    return block.astype(BF16)
+
+
+def whole_columns(block):
+    block = block.astype(F32)
+    return [block[:, j : j + 1] + block[:, 4 + j : 5 + j] for j in range(4)]
 
 
 def gated_rows(experts, table_ref, gate, route, rows):
@@ -198,15 +222,17 @@
     return gated
 
 
-def weight_grad_body(experts, chunks, size, turned_ref, bank_ref, table_ref, *refs):
-    row_refs, out_refs, back_refs = refs[:4], refs[4:-3], refs[-3:]
-    half, count = turned_ref.shape[0] // 2, row_refs[0].shape[0]
+def weight_grad_body(experts, chunks, size, turned_ref, bank_ref, table_ref, slots_ref, *refs):
+    row_refs, out_refs, back_refs = refs[:2], refs[2:-3], refs[-3:]
+    half, count = turned_ref.shape[0] // 2, row_refs[0].shape[0] // 2
+    gate_grads = []
     for side, gate, route, at in (
         (0, VALUE_GATE, VALUE_ROUTE, 1),
         (1, OUTPUT_GATE, OUTPUT_ROUTE, 0),
     ):
         rows = jnp.concatenate([r[:, at * size : (at + 1) * size] for r in row_refs], axis=0)
-        gated = gated_rows(experts, table_ref, gate, route, rows.astype(F32))
+        rows = rows.astype(F32)
+        gated = gated_rows(experts, table_ref, gate, route, rows)
         left = turned_ref[side * half : (side + 1) * half, :]
         for i in range(0, experts, 2):
             product = dot(left, jnp.concatenate(gated[i : i + 2], axis=1))
@@ -220,15 +246,51 @@
                     start = stop
         if side == 0:
             back = dot(jnp.concatenate(gated, axis=1), bank_ref[...]).astype(BF16)
-            back_refs[0][...], back_refs[1][...] = back[:count], back[count : 2 * count]
-            back_refs[2][...] = back[2 * count :]
-
-
-def merge_body(beside_ref, got_ref, own_ref, send_ref):
-    count, half = beside_ref.shape
-    own_ref[...] = got_ref[:count]
-    send_ref[:, :half] = beside_ref[...]
-    send_ref[:, half:] = got_ref[count:]
+        for j in range(2):
+            slot = slots_ref[:, (2 * side + j) * size : (2 * side + j + 1) * size].astype(F32)
+            gate_grads.append(jnp.sum(rows * slot, axis=1, keepdims=True))
+    gate_block = two_parts(gate_grads)
+    for i, back_ref in enumerate(back_refs):
+        start, stop = (i * count, (i + 1) * count) if i < 2 else (2 * count, 4 * count)
+        back_ref[:, :half] = back[start:stop]
+        back_ref[:, half:] = gate_block[start:stop]
+
+
+def merge_body(own_ref, beside_ref, got_ref, gate_ref, send_ref):
+    count, half = beside_ref.shape[0], beside_ref.shape[1] - 128
+    sums = [
+        two_parts(
+            [
+                near + far
+                for near, far in zip(whole_columns(ref[:, half:]), whole_columns(got))
+            ]
+        )
+        for ref, got in ((own_ref, got_ref[:count, half:]), (beside_ref, got_ref[count:, half:]))
+    ]
+    gate_ref[...] = sums[0]
+    send_ref[:, :half] = beside_ref[:, :half]
+    send_ref[:, half : 2 * half] = got_ref[count:, :half]
+    send_ref[:, 2 * half :] = sums[1]
+
+
+def logit_body(gate_ref, got_ref, table_ref, vr_ref, or_ref, out_ref):
+    both, count = out_ref.shape
+    got = got_ref[:, got_ref.shape[1] - 128 :]
+    near, far = gate_ref[...].astype(F32).T, got.astype(F32).T
+    gates = table_ref[:count, :].T
+    ids = lax.broadcasted_iota(jnp.int32, (both, count), 0)
+    logit = jnp.zeros((both, count), F32)
+    for side, (route_ref, first) in enumerate(((vr_ref, 0), (or_ref, both // 2))):
+        for j in range(2):
+            at = 2 * side + j
+            grad = (near[at : at + 1] + near[4 + at : 5 + at]) + (
+                far[at : at + 1] + far[4 + at : 5 + at]
+            )
+            gate = gates[at : at + 1]
+            logit = jnp.where(
+                ids == route_ref[j : j + 1, :] + first, grad * gate * (1.0 - gate), logit
+            )
+    out_ref[...] = logit
 
 
 def chunk_sum_body(*refs):
@@ -247,30 +309,13 @@
         refs[side - 2][0] = total[side]
 
 
-def attention_back_body(vr_ref, or_ref, table_ref, probs_ref, q_ref, k_ref, mixed_ref, slots_ref, grad_ref, rows_ref, query_grad_ref, key_grad_ref, logit_ref):
-    count, size = q_ref.shape
-    both = logit_ref.shape[1]
+def attention_back_body(probs_ref, q_ref, k_ref, mixed_ref, grad_ref, query_grad_ref, key_grad_ref):
     probs = probs_ref[...]
     prob_grad = dot_nt(grad_ref[...], mixed_ref[...])
     score_grad = probs * (prob_grad - jnp.sum(prob_grad * probs, axis=1, keepdims=True))
-    scaled = score_grad / math.sqrt(size)
+    scaled = score_grad / math.sqrt(q_ref.shape[1])
     query_grad_ref[...] = dot(scaled.astype(BF16), k_ref[...]).astype(BF16)
     key_grad_ref[...] = dot(scaled.T.astype(BF16), q_ref[...]).astype(BF16)
-    ids = lax.broadcasted_iota(jnp.int32, (count, both), 1)
-    logit = jnp.zeros((count, both), F32)
-    for gate_at, route, at, base, first in (
-        (VALUE_GATE, vr_ref, 1, 0, 0),
-        (OUTPUT_GATE, or_ref, 0, 2, both // 2),
-    ):
-        rows = rows_ref[:, at * size : (at + 1) * size].astype(F32)
-        for j in range(2):
-            gate = table_ref[:count, gate_at + j : gate_at + j + 1]
-            other = slots_ref[:, (base + j) * size : (base + j + 1) * size].astype(F32)
-            gate_grad = jnp.sum(rows * other, axis=1, keepdims=True)
-            logit = jnp.where(
-                ids == route[:, j : j + 1] + first, gate_grad * gate * (1.0 - gate), logit
-            )
-    logit_ref[...] = logit
 
 
 def on_device(
@@ -307,8 +352,8 @@
         return arrays[0] if len(arrays) == 1 else jnp.concatenate(arrays, axis=axis)
 
     own_banks = jnp.concatenate([value_weight, output_weight], axis=0)
+    first_round = [over_experts(own_banks, k, "banks") for k in range(1, experts)]
     other_banks = side_by_side([over_dp(own_banks, 4 * k, "banks") for k in range(1, quads)], 1)
-    first_round = [over_experts(own_banks, k, "banks") for k in range(1, experts)]
 
     if aligned:
         packed = kernel_call(
@@ -329,7 +374,7 @@
                 pltpu.VMEM((2, count), jnp.int32),
                 pltpu.SemaphoreType.DMA((3 + 8 * quads,)),
             ],
-            vmem=48,
+            vmem=60,
         )
     else:
         (own_table,) = kernel_call(
@@ -355,8 +400,8 @@
         ]
     packed = list(packed)
     far_rows = over_dp(packed[3], 2, "far_rows")
-    far_rows, other_banks, first_round, packed[2], packed[1] = lax.optimization_barrier(
-        (far_rows, other_banks, first_round, packed[2], packed[1])
+    far_rows, first_round, other_banks, packed[2], packed[1] = lax.optimization_barrier(
+        (far_rows, first_round, other_banks, packed[2], packed[1])
     )
     banks = [own_banks, other_banks]
     for k in range(1, experts):
@@ -372,47 +417,44 @@
         core_rows,
         core_far_rows,
     )
-    probs, weights, weights_back = kernel_call(
+    probs, weights = kernel_call(
         probs_body,
-        [((count, count), F32), ((count, count), BF16), ((count, count), BF16)],
+        [((count, count), F32), ((count, count), BF16)],
         queries,
         key_vectors,
     )
 
-    def from_quad(x, what):
-        beside = over_dp(x, 2, what)
-        return [x, beside, over_dp(x, 1, what), over_dp(beside, 1, what)]
-
     (turned_bank,) = kernel_call(
         lambda *refs: turn_bank_body(experts, 2, size, *refs), [((experts * size, half), BF16)], *banks
     )
     (turned,) = kernel_call(turn_body, [((2 * half, 4 * count), BF16)], *rows)
 
     product_flops = 2 * 4 * count * half * experts * size
-    keep, send = kernel_call(
+    slots, keep, send = kernel_call(
         lambda *refs: partial_body(experts, 2, size, half, *refs),
-        [((2 * count, 4 * size), F32), ((2 * count, 4 * size), BF16)],
+        [((4 * count, 4 * size), BF16), ((2 * count, 2 * size), F32), ((2 * count, 2 * size), BF16)],
         *rows,
         table,
         *banks,
         flops=2 * product_flops,
     )
-    keep, send = kernel_call(
+    chip_sum, send = kernel_call(
         core_sum_body,
-        [((count, 4 * size), F32), ((count, 4 * size), BF16)],
+        [((2 * count, 2 * size), F32), ((2 * count + count // 2, 2 * size), BF16)],
         keep,
         over_dp(send, 1, "partials"),
-    )
-    slots, mixed_value, hidden_grad, head_rows = kernel_call(
+        weights,
+    )
+    got_sum, turned, turned_bank = lax.optimization_barrier(
+        (over_dp(send, 2, "partials"), turned, turned_bank)
+    )
+    mixed_value, hidden_grad, head_rows = kernel_call(
         middle_body,
-        [((count, 4 * size), BF16), ((count, size), BF16), ((count, size), BF16), ((count, 2 * size), BF16)],
-        keep,
-        over_dp(send, 2, "partials"),
-        table,
+        [((count, size), BF16), ((count, size), BF16), ((2 * count, 2 * size), BF16)],
+        chip_sum,
+        got_sum,
         weights,
-        weights_back,
-    )
-    quad_rows = from_quad(head_rows, "head_rows")
+    )
 
     shapes = []
     for k in range(experts):
@@ -420,35 +462,37 @@
         shapes += [((2, block, size), kind), ((2, half - block, size), kind)]
     *grads, own_back, beside_back, core_back = kernel_call(
         lambda *refs: weight_grad_body(experts, 2, size, *refs),
-        shapes + [((count, half), BF16), ((count, half), BF16), ((2 * count, half), BF16)],
+        shapes + [((n * count, half + 128), BF16) for n in (1, 1, 2)],
         turned,
         turned_bank,
         table,
-        *quad_rows,
+        slots,
+        head_rows,
+        over_dp(head_rows, 1, "head_rows"),
         flops=3 * product_flops,
     )
-    got_back, beside_back = kernel_call(
-        merge_body,
-        [((count, half), BF16), ((count, 2 * half), BF16)],
-        beside_back,
-        over_dp(core_back, 1, "token_back"),
-    )
-    back = [own_back, got_back, over_dp(beside_back, 2, "token_back")]
-
     def over_all_experts(chunk):
         return [grads[chunk]] + [
             over_experts(grads[2 * k + chunk], k, "grads") for k in range(1, experts)
         ]
 
+    far_chunk = over_all_experts(1)
+    got_back = over_dp(core_back, 1, "token_back")
+    gate_sums, beside_back = kernel_call(
+        merge_body,
+        [((count, 128), BF16), ((count, 2 * half + 128), BF16)],
+        own_back,
+        beside_back,
+        got_back,
+    )
+    back = [own_back, got_back, over_dp(beside_back, 2, "token_back")]
+
     (others,) = kernel_call(
-        chunk_sum_body, [((2, half - block, size), BF16)], *over_all_experts(1)
+        chunk_sum_body, [((2, half - block, size), BF16)], *far_chunk, flops=10**9
     )
     sums = over_all_experts(0) + [
         over_dp(others[:, (k - 1) * block : k * block], 4 * k, "grads") for k in range(1, quads)
     ]
-    value_weight_grad, output_weight_grad = kernel_call(
-        lambda *refs: final_sum_body(groups, *refs), [((1, block, size), F32)] * 2, *sums
-    )
 
     if aligned:
         (token_grad,) = kernel_call(
@@ -459,11 +503,13 @@
             scalars=1,
         )
     else:
-        back = jnp.concatenate(back, axis=1)
+        parts = jnp.concatenate(
+            [back[0][:, :half], back[1][:count, :half], back[2][:, : 2 * half]], axis=1
+        )
         token_grad = jnp.concatenate(
             [
                 lax.dynamic_slice(
-                    back,
+                    parts,
                     (0, (((at ^ b) & 3) * quads + ((at ^ b) >> 2)) * block),
                     (count, block),
                 )
@@ -472,21 +518,30 @@
             axis=1,
         )
 
-    query_grad, key_grad, logit_grad = kernel_call(
+    (logit_grad,) = kernel_call(
+        logit_body,
+        [((2 * experts, count), F32)],
+        gate_sums,
+        back[2],
+        table,
+        value_routes.T,
+        output_routes.T,
+    )
+    token_grad, logit_grad, sums = lax.optimization_barrier((token_grad, logit_grad, sums))
+    value_weight_grad, output_weight_grad = kernel_call(
+        lambda *refs: final_sum_body(groups, *refs), [((1, block, size), F32)] * 2, *sums
+    )
+
+    query_grad, key_grad = kernel_call(
         attention_back_body,
-        [((count, size), BF16), ((count, size), BF16), ((count, 2 * experts), F32)],
-        value_routes,
-        output_routes,
-        table,
+        [((count, size), BF16), ((count, size), BF16)],
         probs,
         queries,
         key_vectors,
         mixed_value,
-        slots,
         hidden_grad,
-        head_rows,
-    )
-    return (token_grad, query_grad, key_grad, logit_grad, value_weight_grad, output_weight_grad)
+    )
+    return (token_grad, query_grad, key_grad, logit_grad.T, value_weight_grad, output_weight_grad)
 
 
 def solution(mesh):

time: 65.6 us -> 60.7 us (0.925)
  Pallas kernels: 7.48 us -> 10.8 us
  starting transfers between devices: 28.5 us -> 25.2 us
  waiting for transfers between devices: 24.8 us -> 21.5 us
  local copies, waits for them, and re-layouts: 3.69 us -> 2.1 us
    ppermute x13 -> x11, starting transfers between devices: 14.4 us -> 10.5 us  [over_dp(): return lax.ppermute(x, 'dp', [(i, i ^ flip) for i in range(groups)])]
    pallas_call x14 -> x15, Pallas kernels: 7.48 us -> 10.8 us  [kernel_call(): pl.pallas_call(body, out_shape=[jax.ShapeDtypeStruct(s, t) for s, t in ou...]
    ppermute x12, waiting for transfers between devices: 10.5 us -> 8.65 us  [over_experts(): return lax.ppermute(x, 'expert', [(i, i ^ flip) for i in range(experts)])]
    unnamed x22 -> x17, local copies, waits for them, and re-layouts: 3.68 us -> 2.09 us
    ppermute x13 -> x11, waiting for transfers between devices: 14.3 us -> 12.9 us  [over_dp(): return lax.ppermute(x, 'dp', [(i, i ^ flip) for i in range(groups)])]
    ppermute x12, starting transfers between devices: 14.1 us -> 14.7 us  [over_experts(): return lax.ppermute(x, 'expert', [(i, i ^ flip) for i in range(experts)])]
  transfers between devices with their start and end apart: 25 -> 23, of which waited for: 14 -> 12; matrix products, arithmetic and copies ran while one was open for 1% -> 0% of each run, Pallas kernels for 4% -> 7%
where the time goes in v3:
time: 60.7 us; the launch traced here: 60.4 us
  starting transfers between devices  25.2 us (42%)
  waiting for transfers between devices  21.5 us (35%)
  Pallas kernels  10.8 us (18%)
  local copies, waits for them, and re-layouts  2.1 us (3%)
  between operations  0.82 us (1%)
    ppermute x12, starting transfers between devices, over_experts(): return lax.ppermute(x, 'expert', [(i, i ^ flip) for i in range(experts)])  14.7 us
    ppermute x11, waiting for transfers between devices, over_dp(): return lax.ppermute(x, 'dp', [(i, i ^ flip) for i in range(groups)])  12.9 us
    pallas_call x15, Pallas kernels, kernel_call(): pl.pallas_call(body, out_shape=[jax.ShapeDtypeStruct(s, t) for s, t in ou...  10.8 us
    ppermute x11, starting transfers between devices, over_dp(): return lax.ppermute(x, 'dp', [(i, i ^ flip) for i in range(groups)])  10.5 us
    ppermute x12, waiting for transfers between devices, over_experts(): return lax.ppermute(x, 'expert', [(i, i ^ flip) for i in range(experts)])  8.65 us
    unnamed x17, local copies, waits for them, and re-layouts  2.09 us
  transfers between devices with their start and end apart: 23, of which 12 were waited for; matrix products, arithmetic and copies ran while one was open for 0% of the time, Pallas kernels for 7%

profile of v3, /device:TPU:0, one launch (start us, length us, event | category | flops | bytes accessed | tf_op | source)
XLA Modules:
  0.0 60.4 jit_solution(326190587169185352)
XLA Ops:
  0.6 2.5 %shard_map.136 = (bf16[128,1152]{1,0:T(8,128)(2,1)}, bf16[128,1152]{1,0:T(8,128)(2,1)}, bf16[128,1024]{1,0:T(8,128)(2,1)}, bf16[128,1152]{1,0:T(8,128)(2,1)}) custom-call(s32[1]{0:T(128)} %bitcast.refs_0_, s32[1]{0:T(128)} %bitcast.1.refs_1_, bf16[128,2048]{1,0:T(8,128)(2,1)} %refs_2_.1, bf16[128,2048]{1,0:T(8,128)(2,1)} %refs_3_.1, f32[8,128]{1,0:T(8,128)} %bitcast.10, ...), custom_call_target="tpu_custom_call" | custom-call | bytes 2201608 | tf_op jit(solution)/shard_map/pallas_call | solution.py:18
  3.1 3.1 %collective-permute-start = (bf16[128,1152]{1,0:T(8,128)(2,1)}, bf16[128,1152]{1,0:T(8,128)(2,1)S(1)}, u32[]{:S(2)}, u32[]{:S(2)}) collective-permute-start(bf16[128,1152]{1,0:T(8,128)(2,1)} %get-tuple-element.55), channel_id=1, source_target_pairs={{0,8},{4,12},{8,0},{12,4},{16,24},{20,28},{24,16},{28,20},{1,9},{5... | collective-permute-start | bytes 884744 | tf_op jit(solution)/shard_map/far_rows_dp2/ppermute | solution.py:345
  6.3 2.7 %collective-permute-start.4 = (bf16[2,256,128]{2,1,0:T(8,128)(2,1)S(1)}, bf16[2,256,128]{2,1,0:T(8,128)(2,1)S(1)}, u32[]{:S(2)}, u32[]{:S(2)}) collective-permute-start(bf16[2,256,128]{2,1,0:T(8,128)(2,1)S(1)} %constant_dynamic-update-slice_fusion.refs_5_.refs_0_), channel_id=1, source_target_pairs={{0,16},{4,20},{8,24},{12,28},{16,0},{20,4},{24,8},{28,12},{1,17},{... | collective-permute-start | bytes 393224 | tf_op jit(solution)/shard_map/banks_dp4/ppermute | solution.py:345
  8.9 2.4 %collective-permute-start.3 = (bf16[2,256,128]{2,1,0:T(8,128)(2,1)S(1)}, bf16[2,256,128]{2,1,0:T(8,128)(2,1)S(1)}, u32[]{:S(2)}, u32[]{:S(2)}) collective-permute-start(bf16[2,256,128]{2,1,0:T(8,128)(2,1)S(1)} %constant_dynamic-update-slice_fusion.refs_5_.refs_0_), channel_id=1, source_target_pairs={{0,3},{1,2},{2,1},{3,0},{4,7},{5,6},{6,5},{7,4},{8,11},{9,10},{10,... | collective-permute-start | bytes 393224 | tf_op jit(solution)/shard_map/banks_expert3/ppermute | solution.py:349
  12.4 3.1 %collective-permute-done.4.refs_6_.refs_1_ = bf16[2,256,128]{2,1,0:T(8,128)(2,1)S(1)} collective-permute-done((bf16[2,256,128]{2,1,0:T(8,128)(2,1)S(1)}, bf16[2,256,128]{2,1,0:T(8,128)(2,1)S(1)}, u32[]{:S(2)}, u32[]{:S(2)}) %collective-permute-start.4) | collective-permute-done | bytes 131104 | tf_op jit(solution)/shard_map/banks_dp4/ppermute | solution.py:345
  15.5 1.8 %collective-permute-done.2.refs_9_.refs_4_ = bf16[2,256,128]{2,1,0:T(8,128)(2,1)S(1)} collective-permute-done((bf16[2,256,128]{2,1,0:T(8,128)(2,1)S(1)}, bf16[2,256,128]{2,1,0:T(8,128)(2,1)S(1)}, u32[]{:S(2)}, u32[]{:S(2)}) %collective-permute-start.2) | collective-permute-done | bytes 131104 | tf_op jit(solution)/shard_map/banks_expert2/ppermute | solution.py:349
  17.9 1.7 %collective-permute-start.5 = (bf16[128,1024]{1,0:T(8,128)(2,1)}, bf16[128,1024]{1,0:T(8,128)(2,1)S(1)}, u32[]{:S(2)}, u32[]{:S(2)}) collective-permute-start(bf16[128,1024]{1,0:T(8,128)(2,1)} %get-tuple-element.58), channel_id=1, source_target_pairs={{0,8},{4,12},{8,0},{12,4},{16,24},{20,28},{24,16},{28,20},{1,9},{5... | collective-permute-start | bytes 786440 | tf_op jit(solution)/shard_map/near_rows_dp2/ppermute | solution.py:345
  19.6 2.4 %collective-permute-start.10 = (bf16[2,256,128]{2,1,0:T(8,128)(2,1)S(1)}, bf16[2,256,128]{2,1,0:T(8,128)(2,1)S(1)}, u32[]{:S(2)}, u32[]{:S(2)}) collective-permute-start(bf16[2,256,128]{2,1,0:T(8,128)(2,1)S(1)} %collective-permute-done.4.refs_6_.refs_1_), channel_id=1, source_target_pairs={{0,3},{1,2},{2,1},{3,0},{4,7},{5,6},{6,5},{7,4},{8,11},{9,10},{10,... | collective-permute-start | bytes 393224 | tf_op jit(solution)/shard_map/other_banks_expert3/ppermute | solution.py:349
  24.2 1.8 %collective-permute-done.10.refs_12_.refs_7_ = bf16[2,256,128]{2,1,0:T(8,128)(2,1)S(1)} collective-permute-done((bf16[2,256,128]{2,1,0:T(8,128)(2,1)S(1)}, bf16[2,256,128]{2,1,0:T(8,128)(2,1)S(1)}, u32[]{:S(2)}, u32[]{:S(2)}) %collective-permute-start.10) | collective-permute-done | bytes 131104 | tf_op jit(solution)/shard_map/other_banks_expert3/ppermute | solution.py:349
  26.0 2.5 %collective-permute-done.9.refs_10_.refs_5_ = bf16[2,256,128]{2,1,0:T(8,128)(2,1)S(1)} collective-permute-done((bf16[2,256,128]{2,1,0:T(8,128)(2,1)S(1)}, bf16[2,256,128]{2,1,0:T(8,128)(2,1)S(1)}, u32[]{:S(2)}, u32[]{:S(2)}) %collective-permute-start.9) | collective-permute-done | bytes 131104 | tf_op jit(solution)/shard_map/other_banks_expert2/ppermute | solution.py:349
  28.6 1.5 %shard_map.138 = (bf16[512,512]{1,0:T(8,128)(2,1)S(1)}, f32[256,256]{1,0:T(8,128)S(1)}, bf16[256,256]{1,0:T(8,128)(2,1)S(1)}) custom-call(bf16[128,1152]{1,0:T(8,128)(2,1)S(1)} %copy-done, bf16[128,1024]{1,0:T(8,128)(2,1)S(1)} %collective-permute-done.5.refs_1_, bf16[128,1152]{1,0:T(8,128)(2,1)S(1)} %collective-permute-done.6.refs_2_, ...), custom_call_target="tpu_custom_call" | custom-call | flops 536870912 | bytes 3375104 | tf_op jit(solution)/shard_map/pallas_call | solution.py:18
  30.5 1.0 %collective-permute-done.11.got_ref = bf16[256,256]{1,0:T(8,128)(2,1)S(1)} collective-permute-done((bf16[256,256]{1,0:T(8,128)(2,1)S(1)}, bf16[256,256]{1,0:T(8,128)(2,1)S(1)}, u32[]{:S(2)}, u32[]{:S(2)}) %collective-permute-start.11) | collective-permute-done | bytes 131104 | tf_op jit(solution)/shard_map/partials_dp1/ppermute | solution.py:345
  32.8 5.0 %collective-permute-done.12.got_ref = bf16[320,256]{1,0:T(8,128)(2,1)S(1)} collective-permute-done((bf16[320,256]{1,0:T(8,128)(2,1)S(1)}, bf16[320,256]{1,0:T(8,128)(2,1)S(1)}, u32[]{:S(2)}, u32[]{:S(2)}) %collective-permute-start.12) | collective-permute-done | bytes 163872 | tf_op jit(solution)/shard_map/partials_dp2/ppermute | solution.py:345
  38.2 1.3 %collective-permute-done.13.refs_5_ = bf16[256,256]{1,0:T(8,128)(2,1)S(1)} collective-permute-done((bf16[256,256]{1,0:T(8,128)(2,1)S(1)}, bf16[256,256]{1,0:T(8,128)(2,1)S(1)}, u32[]{:S(2)}, u32[]{:S(2)}) %collective-permute-start.13) | collective-permute-done | bytes 131104 | tf_op jit(solution)/shard_map/head_rows_dp1/ppermute | solution.py:345
  39.5 1.8 %shard_map.144 = (f32[2,256,128]{2,1,0:T(8,128)S(1)}, f32[2,256,128]{2,1,0:T(8,128)S(1)}, bf16[2,256,128]{2,1,0:T(8,128)(2,1)S(1)}, bf16[2,256,128]{2,1,0:T(8,12...) custom-call(bf16[1024,512]{1,0:T(8,128)(2,1)S(1)} %shard_map.141.ref, ...), custom_call_target="tpu_custom_call" | custom-call | flops 805306368 | bytes 4587520 | tf_op jit(solution)/shard_map/pallas_call | solution.py:18
  41.5 1.5 %collective-permute-start.19 = (bf16[2,256,128]{2,1,0:T(8,128)(2,1)S(1)}, bf16[2,256,128]{2,1,0:T(8,128)(2,1)S(1)}, u32[]{:S(2)}, u32[]{:S(2)}) collective-permute-start(bf16[2,256,128]{2,1,0:T(8,128)(2,1)S(1)} %get-tuple-element.85), channel_id=1, source_target_pairs={{0,1},{1,0},{2,3},{3,2},{4,5},{5,4},{6,7},{7,6},{8,9},{9,8},{10,11... | collective-permute-start | bytes 393224 | tf_op jit(solution)/shard_map/grads_expert1/ppermute | solution.py:349
  43.8 1.2 %collective-permute-start.21 = (bf16[2,256,128]{2,1,0:T(8,128)(2,1)S(1)}, bf16[2,256,128]{2,1,0:T(8,128)(2,1)S(1)}, u32[]{:S(2)}, u32[]{:S(2)}) collective-permute-start(bf16[2,256,128]{2,1,0:T(8,128)(2,1)S(1)} %get-tuple-element.87), channel_id=1, source_target_pairs={{0,3},{1,2},{2,1},{3,0},{4,7},{5,6},{6,5},{7,4},{8,11},{9,10},{10,... | collective-permute-start | bytes 393224 | tf_op jit(solution)/shard_map/grads_expert3/ppermute | solution.py:349
  45.8 1.5 %collective-permute-start.16 = (bf16[2,256,128]{2,1,0:T(8,128)(2,1)S(1)}, bf16[2,256,128]{2,1,0:T(8,128)(2,1)S(1)}, u32[]{:S(2)}, u32[]{:S(2)}) collective-permute-start(bf16[2,256,128]{2,1,0:T(8,128)(2,1)S(1)} %get-tuple-element.81), channel_id=1, source_target_pairs={{0,1},{1,0},{2,3},{3,2},{4,5},{5,4},{6,7},{7,6},{8,9},{9,8},{10,11... | collective-permute-start | bytes 393224 | tf_op jit(solution)/shard_map/grads_expert1/ppermute | solution.py:349
  47.6 1.7 %collective-permute-start.17 = (bf16[2,256,128]{2,1,0:T(8,128)(2,1)S(1)}, bf16[2,256,128]{2,1,0:T(8,128)(2,1)S(1)}, u32[]{:S(2)}, u32[]{:S(2)}) collective-permute-start(bf16[2,256,128]{2,1,0:T(8,128)(2,1)S(1)} %get-tuple-element.82), channel_id=1, source_target_pairs={{0,2},{1,3},{2,0},{3,1},{4,6},{5,7},{6,4},{7,5},{8,10},{9,11},{10,... | collective-permute-start | bytes 393224 | tf_op jit(solution)/shard_map/grads_expert2/ppermute | solution.py:349
  49.3 2.1 %collective-permute-done.20.refs_2_ = bf16[2,256,128]{2,1,0:T(8,128)(2,1)S(1)} collective-permute-done((bf16[2,256,128]{2,1,0:T(8,128)(2,1)S(1)}, bf16[2,256,128]{2,1,0:T(8,128)(2,1)S(1)}, u32[]{:S(2)}, u32[]{:S(2)}) %collective-permute-start.20) | collective-permute-done | bytes 131104 | tf_op jit(solution)/shard_map/grads_expert2/ppermute | solution.py:349
  51.4 1.0 %collective-permute-start.18 = (bf16[2,256,128]{2,1,0:T(8,128)(2,1)S(1)}, bf16[2,256,128]{2,1,0:T(8,128)(2,1)S(1)}, u32[]{:S(2)}, u32[]{:S(2)}) collective-permute-start(bf16[2,256,128]{2,1,0:T(8,128)(2,1)S(1)} %get-tuple-element.83), channel_id=1, source_target_pairs={{0,3},{1,2},{2,1},{3,0},{4,7},{5,6},{6,5},{7,4},{8,11},{9,10},{10,... | collective-permute-start | bytes 393224 | tf_op jit(solution)/shard_map/grads_expert3/ppermute | solution.py:349
  52.5 1.5 %collective-permute-start.22 = (bf16[2,256,128]{2,1,0:T(8,128)(2,1)S(1)}, bf16[2,256,128]{2,1,0:T(8,128)(2,1)S(1)}, u32[]{:S(2)}, u32[]{:S(2)}) collective-permute-start(bf16[2,256,128]{2,1,0:T(8,128)(2,1)S(1)} %shard_map.148), channel_id=1, source_target_pairs={{0,16},{4,20},{8,24},{12,28},{16,0},{20,4},{24,8},{28,12},{1,17},{... | collective-permute-start | bytes 393224 | tf_op jit(solution)/shard_map/grads_dp4/ppermute | solution.py:345
  54.0 1.1 %shard_map.149 = (bf16[128,128]{1,0:T(8,128)(2,1)}, bf16[128,128]{1,0:T(8,128)(2,1)}) custom-call(f32[128,128]{1,0:T(8,128)S(1)} %get-tuple-element.89.probs_ref, bf16[128,128]{1,0:T(8,128)(2,1)S(1)} %copy-done.2, bf16[128,128]{1,0:T(8,128)(2,1)S(1)} %copy-done.3, bf16[128,128]{1,0:T(8,128)(2,1)S(1)} %get-tuple-element.90.mixed_ref, ...), custom_call_target="tpu_custom_call" | custom-call | bytes 262144 | tf_op jit(solution)/shard_map/pallas_call | solution.py:18
  57.3 2.4 %collective-permute-done.22.refs_4_ = bf16[2,256,128]{2,1,0:T(8,128)(2,1)S(1)} collective-permute-done((bf16[2,256,128]{2,1,0:T(8,128)(2,1)S(1)}, bf16[2,256,128]{2,1,0:T(8,128)(2,1)S(1)}, u32[]{:S(2)}, u32[]{:S(2)}) %collective-permute-start.22) | collective-permute-done | bytes 131104 | tf_op jit(solution)/shard_map/grads_dp4/ppermute | solution.py:345
  (55 shorter events, 10.9 us)
Async XLA Ops:
  3.1 14.3 %collective-permute-start = (bf16[128,1152]{1,0:T(8,128)(2,1)}, bf16[128,1152]{1,0:T(8,128)(2,1)S(1)}, u32[]{:S(2)}, u32[]{:S(2)}) collective-permute-start(bf16[128,1152]{1,0:T(8,128)(2,1)} %get-tuple-element.55), channel_id=1, source_target_pairs={{0,8},{4,12},{8,0},{12,4},{16,24},{20,28},{24,16},{28,20},{1,9},{5... | collective-permute-start | bytes 884744 | tf_op jit(solution)/shard_map/far_rows_dp2/ppermute | solution.py:345
  6.3 9.2 %collective-permute-start.4 = (bf16[2,256,128]{2,1,0:T(8,128)(2,1)S(1)}, bf16[2,256,128]{2,1,0:T(8,128)(2,1)S(1)}, u32[]{:S(2)}, u32[]{:S(2)}) collective-permute-start(bf16[2,256,128]{2,1,0:T(8,128)(2,1)S(1)} %constant_dynamic-update-slice_fusion.refs_5_.refs_0_), channel_id=1, source_target_pairs={{0,16},{4,20},{8,24},{12,28},{16,0},{20,4},{24,8},{28,12},{1,17},{... | collective-permute-start | bytes 393224 | tf_op jit(solution)/shard_map/banks_dp4/ppermute | solution.py:345
  8.9 6.6 %collective-permute-start.3 = (bf16[2,256,128]{2,1,0:T(8,128)(2,1)S(1)}, bf16[2,256,128]{2,1,0:T(8,128)(2,1)S(1)}, u32[]{:S(2)}, u32[]{:S(2)}) collective-permute-start(bf16[2,256,128]{2,1,0:T(8,128)(2,1)S(1)} %constant_dynamic-update-slice_fusion.refs_5_.refs_0_), channel_id=1, source_target_pairs={{0,3},{1,2},{2,1},{3,0},{4,7},{5,6},{6,5},{7,4},{8,11},{9,10},{10,... | collective-permute-start | bytes 393224 | tf_op jit(solution)/shard_map/banks_expert3/ppermute | solution.py:349
  11.4 5.9 %collective-permute-start.2 = (bf16[2,256,128]{2,1,0:T(8,128)(2,1)S(1)}, bf16[2,256,128]{2,1,0:T(8,128)(2,1)S(1)}, u32[]{:S(2)}, u32[]{:S(2)}) collective-permute-start(bf16[2,256,128]{2,1,0:T(8,128)(2,1)S(1)} %constant_dynamic-update-slice_fusion.refs_5_.refs_0_), channel_id=1, source_target_pairs={{0,2},{1,3},{2,0},{3,1},{4,6},{5,7},{6,4},{7,5},{8,10},{9,11},{10,... | collective-permute-start | bytes 393224 | tf_op jit(solution)/shard_map/banks_expert2/ppermute | solution.py:349
  11.9 5.5 %collective-permute-start.1 = (bf16[2,256,128]{2,1,0:T(8,128)(2,1)S(1)}, bf16[2,256,128]{2,1,0:T(8,128)(2,1)S(1)}, u32[]{:S(2)}, u32[]{:S(2)}) collective-permute-start(bf16[2,256,128]{2,1,0:T(8,128)(2,1)S(1)} %constant_dynamic-update-slice_fusion.refs_5_.refs_0_), channel_id=1, source_target_pairs={{0,1},{1,0},{2,3},{3,2},{4,5},{5,4},{6,7},{7,6},{8,9},{9,8},{10,11... | collective-permute-start | bytes 393224 | tf_op jit(solution)/shard_map/banks_expert1/ppermute | solution.py:349
  17.4 5.2 %collective-permute-start.6 = (bf16[128,1152]{1,0:T(8,128)(2,1)}, bf16[128,1152]{1,0:T(8,128)(2,1)S(1)}, u32[]{:S(2)}, u32[]{:S(2)}) collective-permute-start(bf16[128,1152]{1,0:T(8,128)(2,1)} %get-tuple-element.59), channel_id=1, source_target_pairs={{0,4},{4,0},{8,12},{12,8},{16,20},{20,16},{24,28},{28,24},{1,5},{5... | collective-permute-start | bytes 884744 | tf_op jit(solution)/shard_map/rows_dp1/ppermute | solution.py:345
  17.4 5.7 %collective-permute-start.7 = (bf16[128,1152]{1,0:T(8,128)(2,1)S(1)}, bf16[128,1152]{1,0:T(8,128)(2,1)S(1)}, u32[]{:S(2)}, u32[]{:S(2)}) collective-permute-start(bf16[128,1152]{1,0:T(8,128)(2,1)S(1)} %collective-permute-done.refs_1_), channel_id=1, source_target_pairs={{0,4},{4,0},{8,12},{12,8},{16,20},{20,16},{24,28},{28,24},{1,5},{5... | collective-permute-start | bytes 884744 | tf_op jit(solution)/shard_map/rows_dp1/ppermute | solution.py:345
  17.9 10.7 %collective-permute-start.5 = (bf16[128,1024]{1,0:T(8,128)(2,1)}, bf16[128,1024]{1,0:T(8,128)(2,1)S(1)}, u32[]{:S(2)}, u32[]{:S(2)}) collective-permute-start(bf16[128,1024]{1,0:T(8,128)(2,1)} %get-tuple-element.58), channel_id=1, source_target_pairs={{0,8},{4,12},{8,0},{12,4},{16,24},{20,28},{24,16},{28,20},{1,9},{5... | collective-permute-start | bytes 786440 | tf_op jit(solution)/shard_map/near_rows_dp2/ppermute | solution.py:345
  19.6 6.4 %collective-permute-start.10 = (bf16[2,256,128]{2,1,0:T(8,128)(2,1)S(1)}, bf16[2,256,128]{2,1,0:T(8,128)(2,1)S(1)}, u32[]{:S(2)}, u32[]{:S(2)}) collective-permute-start(bf16[2,256,128]{2,1,0:T(8,128)(2,1)S(1)} %collective-permute-done.4.refs_6_.refs_1_), channel_id=1, source_target_pairs={{0,3},{1,2},{2,1},{3,0},{4,7},{5,6},{6,5},{7,4},{8,11},{9,10},{10,... | collective-permute-start | bytes 393224 | tf_op jit(solution)/shard_map/other_banks_expert3/ppermute | solution.py:349
  22.1 6.5 %collective-permute-start.9 = (bf16[2,256,128]{2,1,0:T(8,128)(2,1)S(1)}, bf16[2,256,128]{2,1,0:T(8,128)(2,1)S(1)}, u32[]{:S(2)}, u32[]{:S(2)}) collective-permute-start(bf16[2,256,128]{2,1,0:T(8,128)(2,1)S(1)} %collective-permute-done.4.refs_6_.refs_1_), channel_id=1, source_target_pairs={{0,2},{1,3},{2,0},{3,1},{4,6},{5,7},{6,4},{7,5},{8,10},{9,11},{10,... | collective-permute-start | bytes 393224 | tf_op jit(solution)/shard_map/other_banks_expert2/ppermute | solution.py:349
  22.6 6.0 %collective-permute-start.8 = (bf16[2,256,128]{2,1,0:T(8,128)(2,1)S(1)}, bf16[2,256,128]{2,1,0:T(8,128)(2,1)S(1)}, u32[]{:S(2)}, u32[]{:S(2)}) collective-permute-start(bf16[2,256,128]{2,1,0:T(8,128)(2,1)S(1)} %collective-permute-done.4.refs_6_.refs_1_), channel_id=1, source_target_pairs={{0,1},{1,0},{2,3},{3,2},{4,5},{5,4},{6,7},{7,6},{8,9},{9,8},{10,11... | collective-permute-start | bytes 393224 | tf_op jit(solution)/shard_map/other_banks_expert1/ppermute | solution.py:349
  24.2 6.0 %copy-start.2 = (bf16[128,128]{1,0:T(8,128)(2,1)S(1)}, bf16[128,128]{1,0:T(8,128)(2,1)}, u32[]{:S(2)}) copy-start(bf16[128,128]{1,0:T(8,128)(2,1)} %q_ref.3) | copy-start | bytes 98308
  30.1 1.4 %collective-permute-start.11 = (bf16[256,256]{1,0:T(8,128)(2,1)S(1)}, bf16[256,256]{1,0:T(8,128)(2,1)S(1)}, u32[]{:S(2)}, u32[]{:S(2)}) collective-permute-start(bf16[256,256]{1,0:T(8,128)(2,1)S(1)} %get-tuple-element.66), channel_id=1, source_target_pairs={{0,4},{4,0},{8,12},{12,8},{16,20},{20,16},{24,28},{28,24},{1,5},{5... | collective-permute-start | bytes 393224 | tf_op jit(solution)/shard_map/partials_dp1/ppermute | solution.py:345
  31.5 6.3 %collective-permute-start.12 = (bf16[320,256]{1,0:T(8,128)(2,1)S(1)}, bf16[320,256]{1,0:T(8,128)(2,1)S(1)}, u32[]{:S(2)}, u32[]{:S(2)}) collective-permute-start(bf16[320,256]{1,0:T(8,128)(2,1)S(1)} %get-tuple-element.68), channel_id=1, source_target_pairs={{0,8},{4,12},{8,0},{12,4},{16,24},{20,28},{24,16},{28,20},{1,9},{5... | collective-permute-start | bytes 491528 | tf_op jit(solution)/shard_map/partials_dp2/ppermute | solution.py:345
  38.1 1.4 %collective-permute-start.13 = (bf16[256,256]{1,0:T(8,128)(2,1)S(1)}, bf16[256,256]{1,0:T(8,128)(2,1)S(1)}, u32[]{:S(2)}, u32[]{:S(2)}) collective-permute-start(bf16[256,256]{1,0:T(8,128)(2,1)S(1)} %get-tuple-element.74.refs_4_), channel_id=1, source_target_pairs={{0,4},{4,0},{8,12},{12,8},{16,20},{20,16},{24,28},{28,24},{1,5},{5... | collective-permute-start | bytes 393224 | tf_op jit(solution)/shard_map/head_rows_dp1/ppermute | solution.py:345
  41.3 3.7 %collective-permute-start.14 = (bf16[256,640]{1,0:T(8,128)(2,1)S(1)}, bf16[256,640]{1,0:T(8,128)(2,1)S(1)}, u32[]{:S(2)}, u32[]{:S(2)}) collective-permute-start(bf16[256,640]{1,0:T(8,128)(2,1)S(1)} %get-tuple-element.76), channel_id=1, source_target_pairs={{0,4},{4,0},{8,12},{12,8},{16,20},{20,16},{24,28},{28,24},{1,5},{5... | collective-permute-start | bytes 983048 | tf_op jit(solution)/shard_map/token_back_dp1/ppermute | solution.py:345
  41.5 6.1 %collective-permute-start.19 = (bf16[2,256,128]{2,1,0:T(8,128)(2,1)S(1)}, bf16[2,256,128]{2,1,0:T(8,128)(2,1)S(1)}, u32[]{:S(2)}, u32[]{:S(2)}) collective-permute-start(bf16[2,256,128]{2,1,0:T(8,128)(2,1)S(1)} %get-tuple-element.85), channel_id=1, source_target_pairs={{0,1},{1,0},{2,3},{3,2},{4,5},{5,4},{6,7},{7,6},{8,9},{9,8},{10,11... | collective-permute-start | bytes 393224 | tf_op jit(solution)/shard_map/grads_expert1/ppermute | solution.py:349
  43.0 8.4 %collective-permute-start.20 = (bf16[2,256,128]{2,1,0:T(8,128)(2,1)S(1)}, bf16[2,256,128]{2,1,0:T(8,128)(2,1)S(1)}, u32[]{:S(2)}, u32[]{:S(2)}) collective-permute-start(bf16[2,256,128]{2,1,0:T(8,128)(2,1)S(1)} %get-tuple-element.86), channel_id=1, source_target_pairs={{0,2},{1,3},{2,0},{3,1},{4,6},{5,7},{6,4},{7,5},{8,10},{9,11},{10,... | collective-permute-start | bytes 393224 | tf_op jit(solution)/shard_map/grads_expert2/ppermute | solution.py:349
  43.8 8.7 %collective-permute-start.21 = (bf16[2,256,128]{2,1,0:T(8,128)(2,1)S(1)}, bf16[2,256,128]{2,1,0:T(8,128)(2,1)S(1)}, u32[]{:S(2)}, u32[]{:S(2)}) collective-permute-start(bf16[2,256,128]{2,1,0:T(8,128)(2,1)S(1)} %get-tuple-element.87), channel_id=1, source_target_pairs={{0,3},{1,2},{2,1},{3,0},{4,7},{5,6},{6,5},{7,4},{8,11},{9,10},{10,... | collective-permute-start | bytes 393224 | tf_op jit(solution)/shard_map/grads_expert3/ppermute | solution.py:349
  45.4 9.6 %collective-permute-start.15 = (bf16[128,1152]{1,0:T(8,128)(2,1)S(1)}, bf16[128,1152]{1,0:T(8,128)(2,1)S(1)}, u32[]{:S(2)}, u32[]{:S(2)}) collective-permute-start(bf16[128,1152]{1,0:T(8,128)(2,1)S(1)} %get-tuple-element.78), channel_id=1, source_target_pairs={{0,8},{4,12},{8,0},{12,4},{16,24},{20,28},{24,16},{28,20},{1,9},{5... | collective-permute-start | bytes 884744 | tf_op jit(solution)/shard_map/token_back_dp2/ppermute | solution.py:345
  45.8 11.5 %collective-permute-start.16 = (bf16[2,256,128]{2,1,0:T(8,128)(2,1)S(1)}, bf16[2,256,128]{2,1,0:T(8,128)(2,1)S(1)}, u32[]{:S(2)}, u32[]{:S(2)}) collective-permute-start(bf16[2,256,128]{2,1,0:T(8,128)(2,1)S(1)} %get-tuple-element.81), channel_id=1, source_target_pairs={{0,1},{1,0},{2,3},{3,2},{4,5},{5,4},{6,7},{7,6},{8,9},{9,8},{10,11... | collective-permute-start | bytes 393224 | tf_op jit(solution)/shard_map/grads_expert1/ppermute | solution.py:349
  47.6 9.7 %collective-permute-start.17 = (bf16[2,256,128]{2,1,0:T(8,128)(2,1)S(1)}, bf16[2,256,128]{2,1,0:T(8,128)(2,1)S(1)}, u32[]{:S(2)}, u32[]{:S(2)}) collective-permute-start(bf16[2,256,128]{2,1,0:T(8,128)(2,1)S(1)} %get-tuple-element.82), channel_id=1, source_target_pairs={{0,2},{1,3},{2,0},{3,1},{4,6},{5,7},{6,4},{7,5},{8,10},{9,11},{10,... | collective-permute-start | bytes 393224 | tf_op jit(solution)/shard_map/grads_expert2/ppermute | solution.py:349
  51.4 5.9 %collective-permute-start.18 = (bf16[2,256,128]{2,1,0:T(8,128)(2,1)S(1)}, bf16[2,256,128]{2,1,0:T(8,128)(2,1)S(1)}, u32[]{:S(2)}, u32[]{:S(2)}) collective-permute-start(bf16[2,256,128]{2,1,0:T(8,128)(2,1)S(1)} %get-tuple-element.83), channel_id=1, source_target_pairs={{0,3},{1,2},{2,1},{3,0},{4,7},{5,6},{6,5},{7,4},{8,11},{9,10},{10,... | collective-permute-start | bytes 393224 | tf_op jit(solution)/shard_map/grads_expert3/ppermute | solution.py:349
  52.5 7.2 %collective-permute-start.22 = (bf16[2,256,128]{2,1,0:T(8,128)(2,1)S(1)}, bf16[2,256,128]{2,1,0:T(8,128)(2,1)S(1)}, u32[]{:S(2)}, u32[]{:S(2)}) collective-permute-start(bf16[2,256,128]{2,1,0:T(8,128)(2,1)S(1)} %shard_map.148), channel_id=1, source_target_pairs={{0,16},{4,20},{8,24},{12,28},{16,0},{20,4},{24,8},{28,12},{1,17},{... | collective-permute-start | bytes 393224 | tf_op jit(solution)/shard_map/grads_dp4/ppermute | solution.py:345
  (7 other events, 18.2 us)

commit v4 on v3

--- a/solution.py
+++ b/solution.py
@@ -8,11 +8,11 @@
 from jax.sharding import PartitionSpec as P
 
 F32, BF16 = jnp.float32, jnp.bfloat16
-VALUE_GATE, OUTPUT_GATE, VALUE_ROUTE, OUTPUT_ROUTE, LOW_PART = 0, 2, 4, 6, 8
-
-
-def kernel_call(body, outs, *args, scalars=0, flops=0, where=pltpu.VMEM, scratch=(), vmem=24):
-    moved = sum(x.size * x.dtype.itemsize for x in args) + sum(
+VALUE_GATE, OUTPUT_GATE, VALUE_ROUTE, OUTPUT_ROUTE, LOW_PART, DENSE = 0, 2, 4, 6, 8, 16
+
+
+def kernel_call(body, outs, *args, scalars=0, flops=0, moved=None, where=pltpu.VMEM, scratch=(), vmem=24):
+    moved = moved or sum(x.size * x.dtype.itemsize for x in args) + sum(
         math.prod(s) * jnp.dtype(t).itemsize for s, t in outs
     )
     return pl.pallas_call(
@@ -65,47 +65,56 @@
     return jnp.concatenate([table, jnp.zeros((128 - table.shape[0], rows), F32)], axis=0).T
 
 
-def quad_table_body(column, *refs):
+def quad_table_body(experts, *refs):
     out_ref = refs[-1]
     for i, ref in enumerate(refs[:-1]):
         rows = ref.shape[0]
-        table = ref[:, column:].astype(F32)
-        out_ref[i * rows : (i + 1) * rows, :] = jnp.concatenate(
-            [
-                table[:, :VALUE_ROUTE] + table[:, LOW_PART : LOW_PART + VALUE_ROUTE],
-                table[:, VALUE_ROUTE:],
-            ],
-            axis=1,
-        )
-
-
-def pack_body(block, quads, at_ref, me_ref, tokens_ref, cotangent_ref, *refs):
-    small_refs, out_refs, held_refs, sems = refs[:3], refs[3:7], refs[7:10], refs[10]
-    copies = [
+        table = ref[:, ref.shape[1] - 128 :].astype(F32)
+        gates = table[:, :VALUE_ROUTE] + table[:, LOW_PART : LOW_PART + VALUE_ROUTE]
+        lane = lax.broadcasted_iota(jnp.int32, (rows, 128), 1).astype(F32)
+        table = jnp.concatenate([gates, table[:, VALUE_ROUTE:LOW_PART], table[:, LOW_PART:]], axis=1)
+        for gate, route, first in (
+            (VALUE_GATE, VALUE_ROUTE, DENSE),
+            (OUTPUT_GATE, OUTPUT_ROUTE, DENSE + experts),
+        ):
+            for j in range(2):
+                at = table[:, route + j : route + j + 1] + float(first)
+                table = jnp.where(lane == at, table[:, gate + j : gate + j + 1], table)
+        out_ref[i * rows : (i + 1) * rows, :] = table
+
+
+def pack_body(block, quads, groups, at_ref, me_ref, tokens_ref, cotangent_ref, value_ref, output_ref, *refs):
+    small_refs, bank_ref, out_refs, held_refs, sems = refs[:3], refs[3], refs[4:7], refs[7:10], refs[10]
+    small = [
         pltpu.make_async_copy(ref, held, sems.at[i])
         for i, (ref, held) in enumerate(zip(small_refs, held_refs))
     ]
-    for flip in (3, 2, 1, 0):
-        for m, ref in enumerate((tokens_ref, cotangent_ref)):
-            for k in range(quads):
-                start = pl.multiple_of((at_ref[0] ^ (4 * k + flip)) * block, block)
-                to = (m * quads + k) * block
-                copies.append(
-                    pltpu.make_async_copy(
-                        ref.at[:, pl.ds(start, block)],
-                        out_refs[flip].at[:, to : to + block],
-                        sems.at[len(copies)],
+    copies = [
+        pltpu.make_async_copy(ref.at[0], bank_ref.at[i], sems.at[3 + i])
+        for i, ref in enumerate((value_ref, output_ref))
+    ]
+    for group, out_ref in zip(groups, out_refs):
+        to = 0
+        for flip in group:
+            for ref in (tokens_ref, cotangent_ref):
+                for k in range(quads):
+                    start = pl.multiple_of((at_ref[0] ^ (4 * k + flip)) * block, block)
+                    copies.append(
+                        pltpu.make_async_copy(
+                            ref.at[:, pl.ds(start, block)],
+                            out_ref.at[:, to : to + block],
+                            sems.at[3 + len(copies)],
+                        )
                     )
-                )
-    for copy in copies:
+                    to += block
+    for copy in small + copies:
         copy.start()
-    for copy in copies[:3]:
+    for copy in small:
         copy.wait()
     table = token_table(me_ref[0], *[held[...] for held in held_refs]).astype(BF16)
-    for flip, out_ref in enumerate(out_refs):
-        if flip != 2:
-            out_ref[:, 2 * quads * block :] = table
-    for copy in copies[3:]:
+    for out_ref in out_refs:
+        out_ref[:, out_ref.shape[1] - 128 :] = table
+    for copy in copies:
         copy.wait()
 
 
@@ -132,9 +141,17 @@
         out_ref[:, i * rows : (i + 1) * rows] = ref[:, : out_ref.shape[0]].T
 
 
-def turn_bank_body(experts, chunks, size, *refs):
-    for e in range(experts):
-        refs[-1][e * size : (e + 1) * size, :] = bank(refs[e * chunks : (e + 1) * chunks], 0).T
+def copy_body(in_ref, out_ref):
+    out_ref[...] = in_ref[...]
+
+
+def tail_body(in_ref, out_ref):
+    out_ref[...] = in_ref[:, in_ref.shape[1] - out_ref.shape[1] :]
+
+
+def turn_bank_body(size, *refs):
+    for e, ref in enumerate(refs[:-1]):
+        refs[-1][e * size : (e + 1) * size, :] = ref[0].T
 
 
 def bank(refs, side):
@@ -147,26 +164,41 @@
     )
 
 
+def expert_products(experts, chunks, half, side, row_refs, weights):
+    left = jnp.concatenate([r[:, side * half : (side + 1) * half] for r in row_refs], axis=0)
+    for i in range(0, experts, 2):
+        product = dot(left, bank_pair(weights, chunks, side, i))
+        size = product.shape[1] // 2
+        yield i, product[:, :size]
+        yield i + 1, product[:, size:]
+
+
 def partial_body(experts, chunks, size, half, *refs):
     row_refs, table_ref, weights = refs[:4], refs[4], refs[5 : 5 + experts * chunks]
-    slots_ref, keep_ref, send_ref = refs[-3:]
+    keep_ref, send_ref = refs[-2:]
     count = row_refs[0].shape[0]
-    for side, gate, route in ((0, VALUE_GATE, VALUE_ROUTE), (1, OUTPUT_GATE, OUTPUT_ROUTE)):
-        left = jnp.concatenate([r[:, side * half : (side + 1) * half] for r in row_refs], axis=0)
-        routes = [table_ref[:, route + j : route + j + 1] for j in range(2)]
-        slots = [jnp.zeros((4 * count, size), F32) for _ in range(2)]
-        for i in range(0, experts, 2):
-            product = dot(left, bank_pair(weights, chunks, side, i))
-            for p in range(2):
-                piece = product[:, p * size : (p + 1) * size]
-                for j in range(2):
-                    slots[j] = jnp.where(routes[j] == float(i + p), piece, slots[j])
-        mixed = sum(table_ref[:, gate + j : gate + j + 1] * slots[j] for j in range(2))
-        for j in range(2):
-            slots_ref[:, (2 * side + j) * size : (2 * side + j + 1) * size] = slots[j].astype(BF16)
+    for side in range(2):
+        mixed = jnp.zeros((4 * count, size), F32)
+        for e, product in expert_products(experts, chunks, half, side, row_refs, weights):
+            at = DENSE + side * experts + e
+            mixed += table_ref[:, at : at + 1] * product
         lanes = slice(side * size, (side + 1) * size)
         keep_ref[:, lanes] = mixed[: 2 * count]
         send_ref[:, lanes] = mixed[2 * count :].astype(BF16)
+
+
+def slots_body(experts, chunks, size, half, *refs):
+    row_refs, table_ref, weights = refs[:4], refs[4], refs[5 : 5 + experts * chunks]
+    slots_ref = refs[-1]
+    count = row_refs[0].shape[0]
+    for side, route in ((0, VALUE_ROUTE), (1, OUTPUT_ROUTE)):
+        routes = [table_ref[:, route + j : route + j + 1] for j in range(2)]
+        slots = [jnp.zeros((4 * count, size), F32) for _ in range(2)]
+        for e, product in expert_products(experts, chunks, half, side, row_refs, weights):
+            for j in range(2):
+                slots[j] = jnp.where(routes[j] == float(e), product, slots[j])
+        for j in range(2):
+            slots_ref[:, (2 * side + j) * size : (2 * side + j + 1) * size] = slots[j].astype(BF16)
 
 
 def core_sum_body(keep_ref, got_ref, weights_ref, sum_ref, send_ref):
@@ -212,27 +244,22 @@
     return [block[:, j : j + 1] + block[:, 4 + j : 5 + j] for j in range(4)]
 
 
-def gated_rows(experts, table_ref, gate, route, rows):
-    gates = [table_ref[:, gate + j : gate + j + 1] for j in range(2)]
-    routes = [table_ref[:, route + j : route + j + 1] for j in range(2)]
-    gated = []
-    for k in range(experts):
-        column = sum(jnp.where(r == float(k), g, 0.0) for g, r in zip(gates, routes))
-        gated.append((column * rows).astype(BF16))
-    return gated
-
-
-def weight_grad_body(experts, chunks, size, turned_ref, bank_ref, table_ref, slots_ref, *refs):
+def gated_rows(experts, side, table_ref, rows):
+    first = DENSE + side * experts
+    return [
+        (table_ref[:, e : e + 1] * rows).astype(BF16) for e in range(first, first + experts)
+    ]
+
+
+def weight_grad_body(experts, chunks, size, turned_ref, *refs):
+    bank_refs, (table_ref, slots_ref), refs = refs[:2], refs[2:4], refs[4:]
     row_refs, out_refs, back_refs = refs[:2], refs[2:-3], refs[-3:]
     half, count = turned_ref.shape[0] // 2, row_refs[0].shape[0] // 2
     gate_grads = []
-    for side, gate, route, at in (
-        (0, VALUE_GATE, VALUE_ROUTE, 1),
-        (1, OUTPUT_GATE, OUTPUT_ROUTE, 0),
-    ):
+    for side, at in ((0, 1), (1, 0)):
         rows = jnp.concatenate([r[:, at * size : (at + 1) * size] for r in row_refs], axis=0)
         rows = rows.astype(F32)
-        gated = gated_rows(experts, table_ref, gate, route, rows)
+        gated = gated_rows(experts, side, table_ref, rows)
         left = turned_ref[side * half : (side + 1) * half, :]
         for i in range(0, experts, 2):
             product = dot(left, jnp.concatenate(gated[i : i + 2], axis=1))
@@ -245,7 +272,8 @@
                     )
                     start = stop
         if side == 0:
-            back = dot(jnp.concatenate(gated, axis=1), bank_ref[...]).astype(BF16)
+            bank_rows = jnp.concatenate([ref[...] for ref in bank_refs], axis=1)
+            back = dot(jnp.concatenate(gated, axis=1), bank_rows).astype(BF16)
         for j in range(2):
             slot = slots_ref[:, (2 * side + j) * size : (2 * side + j + 1) * size].astype(F32)
             gate_grads.append(jnp.sum(rows * slot, axis=1, keepdims=True))
@@ -351,71 +379,67 @@
     def side_by_side(arrays, axis):
         return arrays[0] if len(arrays) == 1 else jnp.concatenate(arrays, axis=axis)
 
-    own_banks = jnp.concatenate([value_weight, output_weight], axis=0)
-    first_round = [over_experts(own_banks, k, "banks") for k in range(1, experts)]
-    other_banks = side_by_side([over_dp(own_banks, 4 * k, "banks") for k in range(1, quads)], 1)
-
+    routing = (gate_logits.T, value_routes.T, output_routes.T)
+    flips = ((2, 3), (1,), (0,))
     if aligned:
-        packed = kernel_call(
-            lambda *refs: pack_body(block, quads, *refs),
-            [((count, 2 * half + (0 if flip == 2 else 128)), BF16) for flip in range(4)],
+        own_banks, sent_rows, core_rows, own_rows = kernel_call(
+            lambda *refs: pack_body(block, quads, flips, *refs),
+            [((2, block, size), BF16)]
+            + [((count, 2 * half * len(group) + 128), BF16) for group in flips],
             at[None],
             me[None],
             tokens,
             cotangent,
-            gate_logits.T,
-            value_routes.T,
-            output_routes.T,
+            value_weight,
+            output_weight,
+            *routing,
             scalars=2,
             where=pl.ANY,
-            scratch=[
-                pltpu.VMEM((2 * experts, count), F32),
-                pltpu.VMEM((2, count), jnp.int32),
-                pltpu.VMEM((2, count), jnp.int32),
-                pltpu.SemaphoreType.DMA((3 + 8 * quads,)),
-            ],
+            scratch=[pltpu.VMEM(x.shape, x.dtype) for x in routing]
+            + [pltpu.SemaphoreType.DMA((5 + 8 * quads,))],
             vmem=60,
         )
     else:
+        own_banks = jnp.concatenate([value_weight, output_weight], axis=0)
         (own_table,) = kernel_call(
-            table_body,
-            [((count, 128), BF16)],
-            me[None],
-            gate_logits.T,
-            value_routes.T,
-            output_routes.T,
-            scalars=1,
+            table_body, [((count, 128), BF16)], me[None], *routing, scalars=1
         )
-        packed = [
+        sent_rows, core_rows, own_rows = [
             jnp.concatenate(
                 [
                     lax.dynamic_slice(x, (0, (at ^ (4 * k + flip)) * block), (count, block))
+                    for flip in group
                     for x in (tokens, cotangent)
                     for k in range(quads)
                 ]
-                + ([] if flip == 2 else [own_table]),
+                + [own_table],
                 axis=1,
             )
-            for flip in range(4)
+            for group in flips
         ]
-    packed = list(packed)
-    far_rows = over_dp(packed[3], 2, "far_rows")
-    far_rows, first_round, other_banks, packed[2], packed[1] = lax.optimization_barrier(
-        (far_rows, first_round, other_banks, packed[2], packed[1])
+    first_round = [over_experts(own_banks, k, "banks") for k in range(1, experts)]
+    other_banks = side_by_side([over_dp(own_banks, 4 * k, "banks") for k in range(1, quads)], 1)
+    beside_rows = over_dp(sent_rows, 2, "rows")
+    (other_banks,) = kernel_call(
+        copy_body, [(other_banks.shape, BF16)], other_banks, flops=5000000000
+    )
+    other_banks, core_rows = lax.optimization_barrier(
+        (other_banks, core_rows)
+    )
+    (far_rows,) = kernel_call(
+        tail_body, [((count, 2 * half + 128), BF16)], beside_rows, flops=1000000000
     )
     banks = [own_banks, other_banks]
     for k in range(1, experts):
         banks += [first_round[k - 1], over_experts(other_banks, k, "other_banks")]
-    near_rows = over_dp(packed[2], 2, "near_rows")
-    core_rows, core_far_rows = over_dp(packed[1], 1, "rows"), over_dp(far_rows, 1, "rows")
-    rows = [packed[0], near_rows, core_rows, core_far_rows]
+    rows = [
+        own_rows,
+        beside_rows,
+        over_dp(core_rows, 1, "rows"),
+        over_dp(far_rows, 1, "far_rows"),
+    ]
     (table,) = kernel_call(
-        lambda *refs: quad_table_body(2 * half, *refs),
-        [((4 * count, 128), F32)],
-        packed[0],
-        far_rows,
-        core_rows,
-        core_far_rows,
+        lambda *refs: quad_table_body(experts, *refs), [((4 * count, 128), F32)], *rows
     )
     probs, weights = kernel_call(
         probs_body,
@@ -424,15 +448,30 @@
         key_vectors,
     )
 
-    (turned_bank,) = kernel_call(
-        lambda *refs: turn_bank_body(experts, 2, size, *refs), [((experts * size, half), BF16)], *banks
-    )
+    turned_bank = [
+        kernel_call(
+            lambda *refs: turn_bank_body(size, *refs),
+            [((experts * size, banks[chunk].shape[1]), BF16)],
+            *banks[chunk::2],
+            flops=flops,
+        )[0]
+        for chunk, flops in enumerate((0, 4000000000))
+    ]
     (turned,) = kernel_call(turn_body, [((2 * half, 4 * count), BF16)], *rows)
 
     product_flops = 2 * 4 * count * half * experts * size
-    slots, keep, send = kernel_call(
+    table, turned_bank = lax.optimization_barrier((table, turned_bank))
+    keep, send = kernel_call(
         lambda *refs: partial_body(experts, 2, size, half, *refs),
-        [((4 * count, 4 * size), BF16), ((2 * count, 2 * size), F32), ((2 * count, 2 * size), BF16)],
+        [((2 * count, 2 * size), F32), ((2 * count, 2 * size), BF16)],
+        *rows,
+        table,
+        *banks,
+        flops=2 * product_flops,
+    )
+    (slots,) = kernel_call(
+        lambda *refs: slots_body(experts, 2, size, half, *refs),
+        [((4 * count, 4 * size), BF16)],
         *rows,
         table,
         *banks,
@@ -445,8 +484,8 @@
         over_dp(send, 1, "partials"),
         weights,
     )
-    got_sum, turned, turned_bank = lax.optimization_barrier(
-        (over_dp(send, 2, "partials"), turned, turned_bank)
+    got_sum, turned, turned_bank, slots = lax.optimization_barrier(
+        (over_dp(send, 2, "partials"), turned, turned_bank, slots)
     )
     mixed_value, hidden_grad, head_rows = kernel_call(
         middle_body,
@@ -464,7 +503,7 @@
         lambda *refs: weight_grad_body(experts, 2, size, *refs),
         shapes + [((n * count, half + 128), BF16) for n in (1, 1, 2)],
         turned,
-        turned_bank,
+        *turned_bank,
         table,
         slots,
         head_rows,
@@ -488,7 +527,7 @@
     back = [own_back, got_back, over_dp(beside_back, 2, "token_back")]
 
     (others,) = kernel_call(
-        chunk_sum_body, [((2, half - block, size), BF16)], *far_chunk, flops=10**9
+        chunk_sum_body, [((2, half - block, size), BF16)], *far_chunk, flops=1000000000
     )
     sums = over_all_experts(0) + [
         over_dp(others[:, (k - 1) * block : k * block], 4 * k, "grads") for k in range(1, quads)

time: 60.7 us -> 58.4 us (0.962)
  local copies, waits for them, and re-layouts: 2.1 us -> 0.7 us
  Pallas kernels: 10.8 us -> 12 us
  waiting for transfers between devices: 21.5 us -> 20.3 us
  starting transfers between devices: 25.2 us -> 24.2 us
    ppermute x11 -> x10, starting transfers between devices: 10.5 us -> 7.28 us  [over_dp(): return lax.ppermute(x, 'dp', [(i, i ^ flip) for i in range(groups)])]
    ppermute x12, starting transfers between devices: 14.7 us -> 16.9 us  [over_experts(): return lax.ppermute(x, 'expert', [(i, i ^ flip) for i in range(experts)])]
    unnamed x17 -> x14, local copies, waits for them, and re-layouts: 2.09 us -> 0.7 us
    pallas_call x15 -> x19, Pallas kernels: 10.8 us -> 12 us  [kernel_call(): pl.pallas_call(body, out_shape=[jax.ShapeDtypeStruct(s, t) for s, t in ou...]
    ppermute x11 -> x10, waiting for transfers between devices: 12.9 us -> 11.8 us  [over_dp(): return lax.ppermute(x, 'dp', [(i, i ^ flip) for i in range(groups)])]
  transfers between devices with their start and end apart: 23 -> 22, of which waited for: 12 -> 11; matrix products, arithmetic and copies ran while one was open for 0% -> 0% of each run, Pallas kernels for 7% -> 9%
where the time goes in v4:
time: 58.4 us; the launch traced here: 58.1 us
  starting transfers between devices  24.2 us (41%)
  waiting for transfers between devices  20.3 us (35%)
  Pallas kernels  12 us (21%)
  between operations  0.86 us (1%)
  local copies, waits for them, and re-layouts  0.7 us (1%)
    ppermute x12, starting transfers between devices, over_experts(): return lax.ppermute(x, 'expert', [(i, i ^ flip) for i in range(experts)])  16.9 us
    pallas_call x19, Pallas kernels, kernel_call(): pl.pallas_call(body, out_shape=[jax.ShapeDtypeStruct(s, t) for s, t in ou...  12 us
    ppermute x10, waiting for transfers between devices, over_dp(): return lax.ppermute(x, 'dp', [(i, i ^ flip) for i in range(groups)])  11.8 us
    ppermute x12, waiting for transfers between devices, over_experts(): return lax.ppermute(x, 'expert', [(i, i ^ flip) for i in range(experts)])  8.56 us
    ppermute x10, starting transfers between devices, over_dp(): return lax.ppermute(x, 'dp', [(i, i ^ flip) for i in range(groups)])  7.28 us
  transfers between devices with their start and end apart: 22, of which 11 were waited for; matrix products, arithmetic and copies ran while one was open for 0% of the time, Pallas kernels for 9%

profile of v4, /device:TPU:0, one launch (start us, length us, event | category | flops | bytes accessed | tf_op | source)
XLA Modules:
  0.0 58.1 jit_solution(9903718231701860598)
XLA Ops:
  0.6 2.6 %shard_map.136 = (bf16[2,256,128]{2,1,0:T(8,128)(2,1)}, bf16[128,2176]{1,0:T(8,128)(2,1)}, bf16[128,1152]{1,0:T(8,128)(2,1)}, bf16[128,1152]{1,0:T(8,128)(2,1)}) custom-call(s32[1]{0:T(128)} %bitcast.refs_0_, s32[1]{0:T(128)} %bitcast.1.refs_1_, bf16[128,2048]{1,0:T(8,128)(2,1)} %refs_2_.1, bf16[128,2048]{1,0:T(8,128)(2,1)} %refs_3_.1, ...), custom_call_target="tpu_custom_call" | custom-call | bytes 2463752 | tf_op jit(solution)/shard_map/pallas_call | solution.py:18
  3.2 4.1 %collective-permute-start.1 = (bf16[2,256,128]{2,1,0:T(8,128)(2,1)}, bf16[2,256,128]{2,1,0:T(8,128)(2,1)S(1)}, u32[]{:S(2)}, u32[]{:S(2)}) collective-permute-start(bf16[2,256,128]{2,1,0:T(8,128)(2,1)} %get-tuple-element.55.refs_0_.refs_5_), channel_id=1, source_target_pairs={{0,16},{4,20},{8,24},{12,28},{16,0},{20,4},{24,8},{28,12},{1,17},{... | collective-permute-start | bytes 393224 | tf_op jit(solution)/shard_map/banks_dp4/ppermute | solution.py:373
  7.3 1.6 %collective-permute-start = (bf16[128,2176]{1,0:T(8,128)(2,1)}, bf16[128,2176]{1,0:T(8,128)(2,1)S(1)}, u32[]{:S(2)}, u32[]{:S(2)}) collective-permute-start(bf16[128,2176]{1,0:T(8,128)(2,1)} %get-tuple-element.54), channel_id=1, source_target_pairs={{0,8},{4,12},{8,0},{12,4},{16,24},{20,28},{24,16},{28,20},{1,9},{5... | collective-permute-start | bytes 1671176 | tf_op jit(solution)/shard_map/rows_dp2/ppermute | solution.py:373
  8.9 2.4 %collective-permute-start.6 = (bf16[2,256,128]{2,1,0:T(8,128)(2,1)}, bf16[2,256,128]{2,1,0:T(8,128)(2,1)S(1)}, u32[]{:S(2)}, u32[]{:S(2)}) collective-permute-start(bf16[2,256,128]{2,1,0:T(8,128)(2,1)} %get-tuple-element.55.refs_0_.refs_5_), channel_id=1, source_target_pairs={{0,3},{1,2},{2,1},{3,0},{4,7},{5,6},{6,5},{7,4},{8,11},{9,10},{10,... | collective-permute-start | bytes 393224 | tf_op jit(solution)/shard_map/banks_expert3/ppermute | solution.py:377
  12.4 1.5 %collective-permute-done.1.in_ref = bf16[2,256,128]{2,1,0:T(8,128)(2,1)S(1)} collective-permute-done((bf16[2,256,128]{2,1,0:T(8,128)(2,1)}, bf16[2,256,128]{2,1,0:T(8,128)(2,1)S(1)}, u32[]{:S(2)}, u32[]{:S(2)}) %collective-permute-start.1) | collective-permute-done | bytes 131104 | tf_op jit(solution)/shard_map/banks_dp4/ppermute | solution.py:373
  13.9 2.6 %collective-permute-start.9 = (bf16[2,256,128]{2,1,0:T(8,128)(2,1)S(1)}, bf16[2,256,128]{2,1,0:T(8,128)(2,1)S(1)}, u32[]{:S(2)}, u32[]{:S(2)}) collective-permute-start(bf16[2,256,128]{2,1,0:T(8,128)(2,1)S(1)} %shard_map.137.refs_0_.refs_6_), channel_id=1, source_target_pairs={{0,3},{1,2},{2,1},{3,0},{4,7},{5,6},{6,5},{7,4},{8,11},{9,10},{10,... | collective-permute-start | bytes 393224 | tf_op jit(solution)/shard_map/other_banks_expert3/ppermute | solution.py:377
  16.5 1.3 %collective-permute-start.8 = (bf16[2,256,128]{2,1,0:T(8,128)(2,1)S(1)}, bf16[2,256,128]{2,1,0:T(8,128)(2,1)S(1)}, u32[]{:S(2)}, u32[]{:S(2)}) collective-permute-start(bf16[2,256,128]{2,1,0:T(8,128)(2,1)S(1)} %shard_map.137.refs_0_.refs_6_), channel_id=1, source_target_pairs={{0,2},{1,3},{2,0},{3,1},{4,6},{5,7},{6,4},{7,5},{8,10},{9,11},{10,... | collective-permute-start | bytes 393224 | tf_op jit(solution)/shard_map/other_banks_expert2/ppermute | solution.py:377
  17.8 3.2 %collective-permute-done.5.refs_2_.refs_9_ = bf16[2,256,128]{2,1,0:T(8,128)(2,1)S(1)} collective-permute-done((bf16[2,256,128]{2,1,0:T(8,128)(2,1)}, bf16[2,256,128]{2,1,0:T(8,128)(2,1)S(1)}, u32[]{:S(2)}, u32[]{:S(2)}) %collective-permute-start.5) | collective-permute-done | bytes 131104 | tf_op jit(solution)/shard_map/banks_expert2/ppermute | solution.py:377
  21.0 1.5 %collective-permute-start.7 = (bf16[2,256,128]{2,1,0:T(8,128)(2,1)S(1)}, bf16[2,256,128]{2,1,0:T(8,128)(2,1)S(1)}, u32[]{:S(2)}, u32[]{:S(2)}) collective-permute-start(bf16[2,256,128]{2,1,0:T(8,128)(2,1)S(1)} %shard_map.137.refs_0_.refs_6_), channel_id=1, source_target_pairs={{0,1},{1,0},{2,3},{3,2},{4,5},{5,4},{6,7},{7,6},{8,9},{9,8},{10,11... | collective-permute-start | bytes 393224 | tf_op jit(solution)/shard_map/other_banks_expert1/ppermute | solution.py:377
  23.4 2.5 %collective-permute-done.7.refs_1_.refs_8_ = bf16[2,256,128]{2,1,0:T(8,128)(2,1)S(1)} collective-permute-done((bf16[2,256,128]{2,1,0:T(8,128)(2,1)S(1)}, bf16[2,256,128]{2,1,0:T(8,128)(2,1)S(1)}, u32[]{:S(2)}, u32[]{:S(2)}) %collective-permute-start.7) | collective-permute-done | bytes 131104 | tf_op jit(solution)/shard_map/other_banks_expert1/ppermute | solution.py:377
  26.1 1.3 %shard_map.139.refs_4_.refs_3_.table_ref = f32[512,128]{1,0:T(8,128)S(1)} custom-call(bf16[128,1152]{1,0:T(8,128)(2,1)S(1)} %copy-done, bf16[128,2176]{1,0:T(8,128)(2,1)S(1)} %collective-permute-done.in_ref.refs_1_, bf16[128,1152]{1,0:T(8,128)(2,1)S(1)} %collective-permute-done.2.refs_2_, bf16[128,1152]{1,0:T(8,128)(2,1)S(1)} %collective-permute-done.3.refs_3_), custom_call_target="tpu_custom_call" | custom-call | bytes 1703936 | tf_op jit(solution)/shard_map/pallas_call | solution.py:18
  28.5 1.0 %collective-permute-done.10.got_ref = bf16[256,256]{1,0:T(8,128)(2,1)S(1)} collective-permute-done((bf16[256,256]{1,0:T(8,128)(2,1)S(1)}, bf16[256,256]{1,0:T(8,128)(2,1)S(1)}, u32[]{:S(2)}, u32[]{:S(2)}) %collective-permute-start.10) | collective-permute-done | bytes 131104 | tf_op jit(solution)/shard_map/partials_dp1/ppermute | solution.py:373
  30.2 1.2 %shard_map.146.refs_4_ = bf16[512,512]{1,0:T(8,128)(2,1)S(1)} custom-call(bf16[128,1152]{1,0:T(8,128)(2,1)S(1)} %copy-done, bf16[128,2176]{1,0:T(8,128)(2,1)S(1)} %collective-permute-done.in_ref.refs_1_, bf16[128,1152]{1,0:T(8,128)(2,1)S(1)} %collective-permute-done.2.refs_2_, bf16[128,1152]{1,0:T(8,128)(2,1)S(1)} %collective-permute-done.3.refs_3_, ...), custom_call_target="tpu_custom_call" | custom-call | flops 536870912 | bytes 3276800 | tf_op jit(solution)/shard_map/pallas_call | solution.py:18
  31.5 4.4 %collective-permute-done.11.got_ref = bf16[320,256]{1,0:T(8,128)(2,1)S(1)} collective-permute-done((bf16[320,256]{1,0:T(8,128)(2,1)S(1)}, bf16[320,256]{1,0:T(8,128)(2,1)S(1)}, u32[]{:S(2)}, u32[]{:S(2)}) %collective-permute-start.11) | collective-permute-done | bytes 163872 | tf_op jit(solution)/shard_map/partials_dp2/ppermute | solution.py:373
  36.2 1.3 %collective-permute-done.12.refs_6_ = bf16[256,256]{1,0:T(8,128)(2,1)S(1)} collective-permute-done((bf16[256,256]{1,0:T(8,128)(2,1)S(1)}, bf16[256,256]{1,0:T(8,128)(2,1)S(1)}, u32[]{:S(2)}, u32[]{:S(2)}) %collective-permute-start.12) | collective-permute-done | bytes 131104 | tf_op jit(solution)/shard_map/head_rows_dp1/ppermute | solution.py:373
  37.5 1.3 %shard_map.148 = (f32[2,256,128]{2,1,0:T(8,128)S(1)}, f32[2,256,128]{2,1,0:T(8,128)S(1)}, bf16[2,256,128]{2,1,0:T(8,128)(2,1)S(1)}, bf16[2,256,128]{2,1,0:T(8,12...) custom-call(bf16[1024,512]{1,0:T(8,128)(2,1)S(1)} %shard_map.145.ref, ...), custom_call_target="tpu_custom_call" | custom-call | flops 805306368 | bytes 4587520 | tf_op jit(solution)/shard_map/pallas_call | solution.py:18
  39.0 1.5 %collective-permute-start.18 = (bf16[2,256,128]{2,1,0:T(8,128)(2,1)S(1)}, bf16[2,256,128]{2,1,0:T(8,128)(2,1)S(1)}, u32[]{:S(2)}, u32[]{:S(2)}) collective-permute-start(bf16[2,256,128]{2,1,0:T(8,128)(2,1)S(1)} %get-tuple-element.83), channel_id=1, source_target_pairs={{0,1},{1,0},{2,3},{3,2},{4,5},{5,4},{6,7},{7,6},{8,9},{9,8},{10,11... | collective-permute-start | bytes 393224 | tf_op jit(solution)/shard_map/grads_expert1/ppermute | solution.py:377
  40.9 1.6 %collective-permute-start.20 = (bf16[2,256,128]{2,1,0:T(8,128)(2,1)S(1)}, bf16[2,256,128]{2,1,0:T(8,128)(2,1)S(1)}, u32[]{:S(2)}, u32[]{:S(2)}) collective-permute-start(bf16[2,256,128]{2,1,0:T(8,128)(2,1)S(1)} %get-tuple-element.85), channel_id=1, source_target_pairs={{0,3},{1,2},{2,1},{3,0},{4,7},{5,6},{6,5},{7,4},{8,11},{9,10},{10,... | collective-permute-start | bytes 393224 | tf_op jit(solution)/shard_map/grads_expert3/ppermute | solution.py:377
  43.3 1.5 %collective-permute-start.15 = (bf16[2,256,128]{2,1,0:T(8,128)(2,1)S(1)}, bf16[2,256,128]{2,1,0:T(8,128)(2,1)S(1)}, u32[]{:S(2)}, u32[]{:S(2)}) collective-permute-start(bf16[2,256,128]{2,1,0:T(8,128)(2,1)S(1)} %get-tuple-element.79), channel_id=1, source_target_pairs={{0,1},{1,0},{2,3},{3,2},{4,5},{5,4},{6,7},{7,6},{8,9},{9,8},{10,11... | collective-permute-start | bytes 393224 | tf_op jit(solution)/shard_map/grads_expert1/ppermute | solution.py:377
  45.1 1.7 %collective-permute-start.16 = (bf16[2,256,128]{2,1,0:T(8,128)(2,1)S(1)}, bf16[2,256,128]{2,1,0:T(8,128)(2,1)S(1)}, u32[]{:S(2)}, u32[]{:S(2)}) collective-permute-start(bf16[2,256,128]{2,1,0:T(8,128)(2,1)S(1)} %get-tuple-element.80), channel_id=1, source_target_pairs={{0,2},{1,3},{2,0},{3,1},{4,6},{5,7},{6,4},{7,5},{8,10},{9,11},{10,... | collective-permute-start | bytes 393224 | tf_op jit(solution)/shard_map/grads_expert2/ppermute | solution.py:377
  46.8 1.9 %collective-permute-done.19.refs_2_ = bf16[2,256,128]{2,1,0:T(8,128)(2,1)S(1)} collective-permute-done((bf16[2,256,128]{2,1,0:T(8,128)(2,1)S(1)}, bf16[2,256,128]{2,1,0:T(8,128)(2,1)S(1)}, u32[]{:S(2)}, u32[]{:S(2)}) %collective-permute-start.19) | collective-permute-done | bytes 131104 | tf_op jit(solution)/shard_map/grads_expert2/ppermute | solution.py:377
  48.7 1.4 %collective-permute-start.17 = (bf16[2,256,128]{2,1,0:T(8,128)(2,1)S(1)}, bf16[2,256,128]{2,1,0:T(8,128)(2,1)S(1)}, u32[]{:S(2)}, u32[]{:S(2)}) collective-permute-start(bf16[2,256,128]{2,1,0:T(8,128)(2,1)S(1)} %get-tuple-element.81), channel_id=1, source_target_pairs={{0,3},{1,2},{2,1},{3,0},{4,7},{5,6},{6,5},{7,4},{8,11},{9,10},{10,... | collective-permute-start | bytes 393224 | tf_op jit(solution)/shard_map/grads_expert3/ppermute | solution.py:377
  50.6 1.1 %shard_map.153 = (bf16[128,128]{1,0:T(8,128)(2,1)}, bf16[128,128]{1,0:T(8,128)(2,1)}) custom-call(f32[128,128]{1,0:T(8,128)S(1)} %get-tuple-element.87.probs_ref, bf16[128,128]{1,0:T(8,128)(2,1)S(1)} %copy-done.2, bf16[128,128]{1,0:T(8,128)(2,1)S(1)} %copy-done.3, bf16[128,128]{1,0:T(8,128)(2,1)S(1)} %get-tuple-element.88.mixed_ref, ...), custom_call_target="tpu_custom_call" | custom-call | bytes 262144 | tf_op jit(solution)/shard_map/pallas_call | solution.py:18
  54.6 2.8 %collective-permute-done.21.refs_4_ = bf16[2,256,128]{2,1,0:T(8,128)(2,1)S(1)} collective-permute-done((bf16[2,256,128]{2,1,0:T(8,128)(2,1)S(1)}, bf16[2,256,128]{2,1,0:T(8,128)(2,1)S(1)}, u32[]{:S(2)}, u32[]{:S(2)}) %collective-permute-start.21) | collective-permute-done | bytes 131104 | tf_op jit(solution)/shard_map/grads_dp4/ppermute | solution.py:373
  (53 shorter events, 10.1 us)
Async XLA Ops:
  3.2 10.7 %collective-permute-start.1 = (bf16[2,256,128]{2,1,0:T(8,128)(2,1)}, bf16[2,256,128]{2,1,0:T(8,128)(2,1)S(1)}, u32[]{:S(2)}, u32[]{:S(2)}) collective-permute-start(bf16[2,256,128]{2,1,0:T(8,128)(2,1)} %get-tuple-element.55.refs_0_.refs_5_), channel_id=1, source_target_pairs={{0,16},{4,20},{8,24},{12,28},{16,0},{20,4},{24,8},{28,12},{1,17},{... | collective-permute-start | bytes 393224 | tf_op jit(solution)/shard_map/banks_dp4/ppermute | solution.py:373
  7.3 15.1 %copy-start.6 = (bf16[128,1152]{1,0:T(8,128)(2,1)S(1)}, bf16[128,1152]{1,0:T(8,128)(2,1)}, u32[]{:S(2)}) copy-start(bf16[128,1152]{1,0:T(8,128)(2,1)} %get-tuple-element.57) | copy-start | bytes 884740
  7.3 15.1 %copy-start.1 = (bf16[2,256,128]{2,1,0:T(8,128)(2,1)S(1)}, bf16[2,256,128]{2,1,0:T(8,128)(2,1)}, u32[]{:S(2)}) copy-start(bf16[2,256,128]{2,1,0:T(8,128)(2,1)} %get-tuple-element.55.refs_0_.refs_5_) | copy-start | bytes 393220
  7.3 15.9 %collective-permute-start = (bf16[128,2176]{1,0:T(8,128)(2,1)}, bf16[128,2176]{1,0:T(8,128)(2,1)S(1)}, u32[]{:S(2)}, u32[]{:S(2)}) collective-permute-start(bf16[128,2176]{1,0:T(8,128)(2,1)} %get-tuple-element.54), channel_id=1, source_target_pairs={{0,8},{4,12},{8,0},{12,4},{16,24},{20,28},{24,16},{28,20},{1,9},{5... | collective-permute-start | bytes 1671176 | tf_op jit(solution)/shard_map/rows_dp2/ppermute | solution.py:373
  8.9 7.6 %collective-permute-start.6 = (bf16[2,256,128]{2,1,0:T(8,128)(2,1)}, bf16[2,256,128]{2,1,0:T(8,128)(2,1)S(1)}, u32[]{:S(2)}, u32[]{:S(2)}) collective-permute-start(bf16[2,256,128]{2,1,0:T(8,128)(2,1)} %get-tuple-element.55.refs_0_.refs_5_), channel_id=1, source_target_pairs={{0,3},{1,2},{2,1},{3,0},{4,7},{5,6},{6,5},{7,4},{8,11},{9,10},{10,... | collective-permute-start | bytes 393224 | tf_op jit(solution)/shard_map/banks_expert3/ppermute | solution.py:377
  11.3 9.6 %collective-permute-start.5 = (bf16[2,256,128]{2,1,0:T(8,128)(2,1)}, bf16[2,256,128]{2,1,0:T(8,128)(2,1)S(1)}, u32[]{:S(2)}, u32[]{:S(2)}) collective-permute-start(bf16[2,256,128]{2,1,0:T(8,128)(2,1)} %get-tuple-element.55.refs_0_.refs_5_), channel_id=1, source_target_pairs={{0,2},{1,3},{2,0},{3,1},{4,6},{5,7},{6,4},{7,5},{8,10},{9,11},{10,... | collective-permute-start | bytes 393224 | tf_op jit(solution)/shard_map/banks_expert2/ppermute | solution.py:377
  11.8 10.6 %collective-permute-start.4 = (bf16[2,256,128]{2,1,0:T(8,128)(2,1)}, bf16[2,256,128]{2,1,0:T(8,128)(2,1)S(1)}, u32[]{:S(2)}, u32[]{:S(2)}) collective-permute-start(bf16[2,256,128]{2,1,0:T(8,128)(2,1)} %get-tuple-element.55.refs_0_.refs_5_), channel_id=1, source_target_pairs={{0,1},{1,0},{2,3},{3,2},{4,5},{5,4},{6,7},{7,6},{8,9},{9,8},{10,11... | collective-permute-start | bytes 393224 | tf_op jit(solution)/shard_map/banks_expert1/ppermute | solution.py:377
  13.9 9.4 %collective-permute-start.9 = (bf16[2,256,128]{2,1,0:T(8,128)(2,1)S(1)}, bf16[2,256,128]{2,1,0:T(8,128)(2,1)S(1)}, u32[]{:S(2)}, u32[]{:S(2)}) collective-permute-start(bf16[2,256,128]{2,1,0:T(8,128)(2,1)S(1)} %shard_map.137.refs_0_.refs_6_), channel_id=1, source_target_pairs={{0,3},{1,2},{2,1},{3,0},{4,7},{5,6},{6,5},{7,4},{8,11},{9,10},{10,... | collective-permute-start | bytes 393224 | tf_op jit(solution)/shard_map/other_banks_expert3/ppermute | solution.py:377
  16.5 6.9 %collective-permute-start.8 = (bf16[2,256,128]{2,1,0:T(8,128)(2,1)S(1)}, bf16[2,256,128]{2,1,0:T(8,128)(2,1)S(1)}, u32[]{:S(2)}, u32[]{:S(2)}) collective-permute-start(bf16[2,256,128]{2,1,0:T(8,128)(2,1)S(1)} %shard_map.137.refs_0_.refs_6_), channel_id=1, source_target_pairs={{0,2},{1,3},{2,0},{3,1},{4,6},{5,7},{6,4},{7,5},{8,10},{9,11},{10,... | collective-permute-start | bytes 393224 | tf_op jit(solution)/shard_map/other_banks_expert2/ppermute | solution.py:377
  21.0 5.0 %collective-permute-start.7 = (bf16[2,256,128]{2,1,0:T(8,128)(2,1)S(1)}, bf16[2,256,128]{2,1,0:T(8,128)(2,1)S(1)}, u32[]{:S(2)}, u32[]{:S(2)}) collective-permute-start(bf16[2,256,128]{2,1,0:T(8,128)(2,1)S(1)} %shard_map.137.refs_0_.refs_6_), channel_id=1, source_target_pairs={{0,1},{1,0},{2,3},{3,2},{4,5},{5,4},{6,7},{7,6},{8,9},{9,8},{10,11... | collective-permute-start | bytes 393224 | tf_op jit(solution)/shard_map/other_banks_expert1/ppermute | solution.py:377
  22.4 3.6 %collective-permute-start.2 = (bf16[128,1152]{1,0:T(8,128)(2,1)S(1)}, bf16[128,1152]{1,0:T(8,128)(2,1)S(1)}, u32[]{:S(2)}, u32[]{:S(2)}) collective-permute-start(bf16[128,1152]{1,0:T(8,128)(2,1)S(1)} %copy-done.6), channel_id=1, source_target_pairs={{0,4},{4,0},{8,12},{12,8},{16,20},{20,16},{24,28},{28,24},{1,5},{5... | collective-permute-start | bytes 884744 | tf_op jit(solution)/shard_map/rows_dp1/ppermute | solution.py:373
  23.3 2.8 %collective-permute-start.3 = (bf16[128,1152]{1,0:T(8,128)(2,1)S(1)}, bf16[128,1152]{1,0:T(8,128)(2,1)S(1)}, u32[]{:S(2)}, u32[]{:S(2)}) collective-permute-start(bf16[128,1152]{1,0:T(8,128)(2,1)S(1)} %shard_map.138), channel_id=1, source_target_pairs={{0,4},{4,0},{8,12},{12,8},{16,20},{20,16},{24,28},{28,24},{1,5},{5... | collective-permute-start | bytes 884744 | tf_op jit(solution)/shard_map/far_rows_dp1/ppermute | solution.py:373
  28.1 1.4 %collective-permute-start.10 = (bf16[256,256]{1,0:T(8,128)(2,1)S(1)}, bf16[256,256]{1,0:T(8,128)(2,1)S(1)}, u32[]{:S(2)}, u32[]{:S(2)}) collective-permute-start(bf16[256,256]{1,0:T(8,128)(2,1)S(1)} %get-tuple-element.61), channel_id=1, source_target_pairs={{0,4},{4,0},{8,12},{12,8},{16,20},{20,16},{24,28},{28,24},{1,5},{5... | collective-permute-start | bytes 393224 | tf_op jit(solution)/shard_map/partials_dp1/ppermute | solution.py:373
  29.6 6.3 %collective-permute-start.11 = (bf16[320,256]{1,0:T(8,128)(2,1)S(1)}, bf16[320,256]{1,0:T(8,128)(2,1)S(1)}, u32[]{:S(2)}, u32[]{:S(2)}) collective-permute-start(bf16[320,256]{1,0:T(8,128)(2,1)S(1)} %get-tuple-element.63), channel_id=1, source_target_pairs={{0,8},{4,12},{8,0},{12,4},{16,24},{20,28},{24,16},{28,20},{1,9},{5... | collective-permute-start | bytes 491528 | tf_op jit(solution)/shard_map/partials_dp2/ppermute | solution.py:373
  36.1 1.4 %collective-permute-start.12 = (bf16[256,256]{1,0:T(8,128)(2,1)S(1)}, bf16[256,256]{1,0:T(8,128)(2,1)S(1)}, u32[]{:S(2)}, u32[]{:S(2)}) collective-permute-start(bf16[256,256]{1,0:T(8,128)(2,1)S(1)} %get-tuple-element.72.refs_5_), channel_id=1, source_target_pairs={{0,4},{4,0},{8,12},{12,8},{16,20},{20,16},{24,28},{28,24},{1,5},{5... | collective-permute-start | bytes 393224 | tf_op jit(solution)/shard_map/head_rows_dp1/ppermute | solution.py:373
  38.8 3.7 %collective-permute-start.13 = (bf16[256,640]{1,0:T(8,128)(2,1)S(1)}, bf16[256,640]{1,0:T(8,128)(2,1)S(1)}, u32[]{:S(2)}, u32[]{:S(2)}) collective-permute-start(bf16[256,640]{1,0:T(8,128)(2,1)S(1)} %get-tuple-element.74), channel_id=1, source_target_pairs={{0,4},{4,0},{8,12},{12,8},{16,20},{20,16},{24,28},{28,24},{1,5},{5... | collective-permute-start | bytes 983048 | tf_op jit(solution)/shard_map/token_back_dp1/ppermute | solution.py:373
  39.0 6.1 %collective-permute-start.18 = (bf16[2,256,128]{2,1,0:T(8,128)(2,1)S(1)}, bf16[2,256,128]{2,1,0:T(8,128)(2,1)S(1)}, u32[]{:S(2)}, u32[]{:S(2)}) collective-permute-start(bf16[2,256,128]{2,1,0:T(8,128)(2,1)S(1)} %get-tuple-element.83), channel_id=1, source_target_pairs={{0,1},{1,0},{2,3},{3,2},{4,5},{5,4},{6,7},{7,6},{8,9},{9,8},{10,11... | collective-permute-start | bytes 393224 | tf_op jit(solution)/shard_map/grads_expert1/ppermute | solution.py:377
  40.5 8.2 %collective-permute-start.19 = (bf16[2,256,128]{2,1,0:T(8,128)(2,1)S(1)}, bf16[2,256,128]{2,1,0:T(8,128)(2,1)S(1)}, u32[]{:S(2)}, u32[]{:S(2)}) collective-permute-start(bf16[2,256,128]{2,1,0:T(8,128)(2,1)S(1)} %get-tuple-element.84), channel_id=1, source_target_pairs={{0,2},{1,3},{2,0},{3,1},{4,6},{5,7},{6,4},{7,5},{8,10},{9,11},{10,... | collective-permute-start | bytes 393224 | tf_op jit(solution)/shard_map/grads_expert2/ppermute | solution.py:377
  40.9 9.2 %collective-permute-start.20 = (bf16[2,256,128]{2,1,0:T(8,128)(2,1)S(1)}, bf16[2,256,128]{2,1,0:T(8,128)(2,1)S(1)}, u32[]{:S(2)}, u32[]{:S(2)}) collective-permute-start(bf16[2,256,128]{2,1,0:T(8,128)(2,1)S(1)} %get-tuple-element.85), channel_id=1, source_target_pairs={{0,3},{1,2},{2,1},{3,0},{4,7},{5,6},{6,5},{7,4},{8,11},{9,10},{10,... | collective-permute-start | bytes 393224 | tf_op jit(solution)/shard_map/grads_expert3/ppermute | solution.py:377
  42.9 8.7 %collective-permute-start.14 = (bf16[128,1152]{1,0:T(8,128)(2,1)S(1)}, bf16[128,1152]{1,0:T(8,128)(2,1)S(1)}, u32[]{:S(2)}, u32[]{:S(2)}) collective-permute-start(bf16[128,1152]{1,0:T(8,128)(2,1)S(1)} %get-tuple-element.76), channel_id=1, source_target_pairs={{0,8},{4,12},{8,0},{12,4},{16,24},{20,28},{24,16},{28,20},{1,9},{5... | collective-permute-start | bytes 884744 | tf_op jit(solution)/shard_map/token_back_dp2/ppermute | solution.py:373
  43.3 10.6 %collective-permute-start.15 = (bf16[2,256,128]{2,1,0:T(8,128)(2,1)S(1)}, bf16[2,256,128]{2,1,0:T(8,128)(2,1)S(1)}, u32[]{:S(2)}, u32[]{:S(2)}) collective-permute-start(bf16[2,256,128]{2,1,0:T(8,128)(2,1)S(1)} %get-tuple-element.79), channel_id=1, source_target_pairs={{0,1},{1,0},{2,3},{3,2},{4,5},{5,4},{6,7},{7,6},{8,9},{9,8},{10,11... | collective-permute-start | bytes 393224 | tf_op jit(solution)/shard_map/grads_expert1/ppermute | solution.py:377
  45.1 8.8 %collective-permute-start.16 = (bf16[2,256,128]{2,1,0:T(8,128)(2,1)S(1)}, bf16[2,256,128]{2,1,0:T(8,128)(2,1)S(1)}, u32[]{:S(2)}, u32[]{:S(2)}) collective-permute-start(bf16[2,256,128]{2,1,0:T(8,128)(2,1)S(1)} %get-tuple-element.80), channel_id=1, source_target_pairs={{0,2},{1,3},{2,0},{3,1},{4,6},{5,7},{6,4},{7,5},{8,10},{9,11},{10,... | collective-permute-start | bytes 393224 | tf_op jit(solution)/shard_map/grads_expert2/ppermute | solution.py:377
  48.7 5.9 %collective-permute-start.17 = (bf16[2,256,128]{2,1,0:T(8,128)(2,1)S(1)}, bf16[2,256,128]{2,1,0:T(8,128)(2,1)S(1)}, u32[]{:S(2)}, u32[]{:S(2)}) collective-permute-start(bf16[2,256,128]{2,1,0:T(8,128)(2,1)S(1)} %get-tuple-element.81), channel_id=1, source_target_pairs={{0,3},{1,2},{2,1},{3,0},{4,7},{5,6},{6,5},{7,4},{8,11},{9,10},{10,... | collective-permute-start | bytes 393224 | tf_op jit(solution)/shard_map/grads_expert3/ppermute | solution.py:377
  50.2 7.2 %collective-permute-start.21 = (bf16[2,256,128]{2,1,0:T(8,128)(2,1)S(1)}, bf16[2,256,128]{2,1,0:T(8,128)(2,1)S(1)}, u32[]{:S(2)}, u32[]{:S(2)}) collective-permute-start(bf16[2,256,128]{2,1,0:T(8,128)(2,1)S(1)} %shard_map.152), channel_id=1, source_target_pairs={{0,16},{4,20},{8,24},{12,28},{16,0},{20,4},{24,8},{28,12},{1,17},{... | collective-permute-start | bytes 393224 | tf_op jit(solution)/shard_map/grads_dp4/ppermute | solution.py:373
  (5 other events, 6.0 us)

commit v5 on v4

--- a/solution.py
+++ b/solution.py
@@ -8,8 +8,6 @@
 from jax.sharding import PartitionSpec as P
 
 F32, BF16 = jnp.float32, jnp.bfloat16
-VALUE_GATE, OUTPUT_GATE, VALUE_ROUTE, OUTPUT_ROUTE, LOW_PART, DENSE = 0, 2, 4, 6, 8, 16
-
 
 def kernel_call(body, outs, *args, scalars=0, flops=0, moved=None, where=pltpu.VMEM, scratch=(), vmem=24):
     moved = moved or sum(x.size * x.dtype.itemsize for x in args) + sum(
@@ -49,38 +47,29 @@
 
 def token_table(me, logits, route_v, route_o):
     both, rows = logits.shape
-    experts = both // 2
     gates = jax.nn.sigmoid(logits)
     ids = lax.broadcasted_iota(jnp.int32, (both, rows), 0)
-    high, low = [], []
-    for routes, first in ((route_v, 0), (route_o, experts)):
+    dense = jnp.zeros((both, rows), F32)
+    for routes, first in ((route_v, 0), (route_o, both // 2)):
         for j in range(2):
-            gate = jnp.sum(
-                jnp.where(ids == routes[j : j + 1] + first, gates, 0.0), axis=0, keepdims=True
-            )
-            high.append(gate.astype(BF16).astype(F32))
-            low.append(gate - high[-1])
+            route = routes[j : j + 1]
+            gate = jnp.sum(jnp.where(ids == route + first, gates, 0.0), axis=0, keepdims=True)
+            dense = jnp.where(ids == (route ^ me) + first, gate, dense)
+    high = dense.astype(BF16).astype(F32)
     routes = [(routes ^ me).astype(F32) for routes in (route_v, route_o)]
-    table = jnp.concatenate(high + routes + low, axis=0)
+    table = jnp.concatenate([high, dense - high] + routes, axis=0)
     return jnp.concatenate([table, jnp.zeros((128 - table.shape[0], rows), F32)], axis=0).T
 
 
 def quad_table_body(experts, *refs):
     out_ref = refs[-1]
+    both = 2 * experts
     for i, ref in enumerate(refs[:-1]):
         rows = ref.shape[0]
         table = ref[:, ref.shape[1] - 128 :].astype(F32)
-        gates = table[:, :VALUE_ROUTE] + table[:, LOW_PART : LOW_PART + VALUE_ROUTE]
-        lane = lax.broadcasted_iota(jnp.int32, (rows, 128), 1).astype(F32)
-        table = jnp.concatenate([gates, table[:, VALUE_ROUTE:LOW_PART], table[:, LOW_PART:]], axis=1)
-        for gate, route, first in (
-            (VALUE_GATE, VALUE_ROUTE, DENSE),
-            (OUTPUT_GATE, OUTPUT_ROUTE, DENSE + experts),
-        ):
-            for j in range(2):
-                at = table[:, route + j : route + j + 1] + float(first)
-                table = jnp.where(lane == at, table[:, gate + j : gate + j + 1], table)
-        out_ref[i * rows : (i + 1) * rows, :] = table
+        out_ref[i * rows : (i + 1) * rows, :] = jnp.concatenate(
+            [table[:, :both] + table[:, both : 2 * both], table[:, both:]], axis=1
+        )
 
 
 def pack_body(block, quads, groups, at_ref, me_ref, tokens_ref, cotangent_ref, value_ref, output_ref, *refs):
@@ -180,7 +169,7 @@
     for side in range(2):
         mixed = jnp.zeros((4 * count, size), F32)
         for e, product in expert_products(experts, chunks, half, side, row_refs, weights):
-            at = DENSE + side * experts + e
+            at = side * experts + e
             mixed += table_ref[:, at : at + 1] * product
         lanes = slice(side * size, (side + 1) * size)
         keep_ref[:, lanes] = mixed[: 2 * count]
@@ -191,7 +180,8 @@
     row_refs, table_ref, weights = refs[:4], refs[4], refs[5 : 5 + experts * chunks]
     slots_ref = refs[-1]
     count = row_refs[0].shape[0]
-    for side, route in ((0, VALUE_ROUTE), (1, OUTPUT_ROUTE)):
+    for side in range(2):
+        route = 4 * experts + 2 * side
         routes = [table_ref[:, route + j : route + j + 1] for j in range(2)]
         slots = [jnp.zeros((4 * count, size), F32) for _ in range(2)]
         for e, product in expert_products(experts, chunks, half, side, row_refs, weights):
@@ -201,21 +191,15 @@
             slots_ref[:, (2 * side + j) * size : (2 * side + j + 1) * size] = slots[j].astype(BF16)
 
 
-def core_sum_body(keep_ref, got_ref, weights_ref, sum_ref, send_ref):
-    both, count = keep_ref.shape[0], weights_ref.shape[0]
+def core_sum_body(keep_ref, got_ref, sum_ref, send_ref):
     total = keep_ref[...] + got_ref[...].astype(F32)
     sum_ref[...] = total
-    send_ref[:both, :] = total.astype(BF16)
-    send_ref[both:, :count] = weights_ref[: count // 2, :]
-    send_ref[both:, count:] = weights_ref[count // 2 :, :]
-
-
-def middle_body(sum_ref, got_ref, weights_ref, mixed_ref, grad_ref, rows_ref):
+    send_ref[...] = total.astype(BF16)
+
+
+def middle_body(sum_ref, got_ref, weights_ref, far_weights_ref, mixed_ref, grad_ref, rows_ref):
     count, size = mixed_ref.shape
-    far_weights = jnp.concatenate(
-        [got_ref[2 * count :, :count], got_ref[2 * count :, count:]], axis=0
-    )
-    for i, weights in enumerate((weights_ref[...], far_weights)):
+    for i, weights in enumerate((weights_ref[...], far_weights_ref[...])):
         total = sum_ref[i * count : (i + 1) * count, :] + got_ref[
             (1 - i) * count : (2 - i) * count, :
         ].astype(F32)
@@ -245,7 +229,7 @@
 
 
 def gated_rows(experts, side, table_ref, rows):
-    first = DENSE + side * experts
+    first = side * experts
     return [
         (table_ref[:, e : e + 1] * rows).astype(BF16) for e in range(first, first + experts)
     ]
@@ -305,16 +289,18 @@
     both, count = out_ref.shape
     got = got_ref[:, got_ref.shape[1] - 128 :]
     near, far = gate_ref[...].astype(F32).T, got.astype(F32).T
-    gates = table_ref[:count, :].T
+    table = table_ref[:count, :].T
     ids = lax.broadcasted_iota(jnp.int32, (both, count), 0)
     logit = jnp.zeros((both, count), F32)
-    for side, (route_ref, first) in enumerate(((vr_ref, 0), (or_ref, both // 2))):
+    for side, route_ref in enumerate((vr_ref, or_ref)):
+        first = side * (both // 2)
         for j in range(2):
             at = 2 * side + j
             grad = (near[at : at + 1] + near[4 + at : 5 + at]) + (
                 far[at : at + 1] + far[4 + at : 5 + at]
             )
-            gate = gates[at : at + 1]
+            here = ids.astype(F32) == table[2 * both + at : 2 * both + at + 1] + float(first)
+            gate = jnp.sum(jnp.where(here, table[:both], 0.0), axis=0, keepdims=True)
             logit = jnp.where(
                 ids == route_ref[j : j + 1, :] + first, grad * gate * (1.0 - gate), logit
             )
@@ -438,14 +424,18 @@
         over_dp(core_rows, 1, "rows"),
         over_dp(far_rows, 1, "far_rows"),
     ]
-    (table,) = kernel_call(
-        lambda *refs: quad_table_body(experts, *refs), [((4 * count, 128), F32)], *rows
-    )
     probs, weights = kernel_call(
         probs_body,
         [((count, count), F32), ((count, count), BF16)],
         queries,
         key_vectors,
+    )
+    far_weights = over_dp(weights, 2, "weights")
+    (table,) = kernel_call(
+        lambda *refs: quad_table_body(experts, *refs[:4], refs[-1]),
+        [((4 * count, 128), F32)],
+        *rows,
+        far_weights,
     )
 
     turned_bank = [
@@ -479,10 +469,9 @@
     )
     chip_sum, send = kernel_call(
         core_sum_body,
-        [((2 * count, 2 * size), F32), ((2 * count + count // 2, 2 * size), BF16)],
+        [((2 * count, 2 * size), F32), ((2 * count, 2 * size), BF16)],
         keep,
         over_dp(send, 1, "partials"),
-        weights,
     )
     got_sum, turned, turned_bank, slots = lax.optimization_barrier(
         (over_dp(send, 2, "partials"), turned, turned_bank, slots)
@@ -493,6 +482,7 @@
         chip_sum,
         got_sum,
         weights,
+        far_weights,
     )
 
     shapes = []

time: 58.4 us -> 56.6 us (0.969)
  waiting for transfers between devices: 20.3 us -> 19 us
  Pallas kernels: 12 us -> 10.9 us
  starting transfers between devices: 24.2 us -> 24.8 us
    ppermute x12, waiting for transfers between devices: 8.56 us -> 6.89 us  [over_experts(): return lax.ppermute(x, 'expert', [(i, i ^ flip) for i in range(experts)])]
    ppermute x10 -> x11, starting transfers between devices: 7.28 us -> 8.66 us  [over_dp(): return lax.ppermute(x, 'dp', [(i, i ^ flip) for i in range(groups)])]
    pallas_call x19, Pallas kernels: 12 us -> 10.9 us  [kernel_call(): pl.pallas_call(body, out_shape=[jax.ShapeDtypeStruct(s, t) for s, t in ou...]
    ppermute x12, starting transfers between devices: 16.9 us -> 16.2 us  [over_experts(): return lax.ppermute(x, 'expert', [(i, i ^ flip) for i in range(experts)])]
    ppermute x10 -> x11, waiting for transfers between devices: 11.8 us -> 12.1 us  [over_dp(): return lax.ppermute(x, 'dp', [(i, i ^ flip) for i in range(groups)])]
  transfers between devices with their start and end apart: 22 -> 23, of which waited for: 11 -> 12; matrix products, arithmetic and copies ran while one was open for 0% -> 0% of each run, Pallas kernels for 9% -> 9%
where the time goes in v5:
time: 56.6 us; the launch traced here: 56.4 us
  starting transfers between devices  24.8 us (44%)
  waiting for transfers between devices  19 us (34%)
  Pallas kernels  10.9 us (19%)
  local copies, waits for them, and re-layouts  0.85 us (2%)
  between operations  0.82 us (1%)
    ppermute x12, starting transfers between devices, over_experts(): return lax.ppermute(x, 'expert', [(i, i ^ flip) for i in range(experts)])  16.2 us
    ppermute x11, waiting for transfers between devices, over_dp(): return lax.ppermute(x, 'dp', [(i, i ^ flip) for i in range(groups)])  12.1 us
    pallas_call x19, Pallas kernels, kernel_call(): pl.pallas_call(body, out_shape=[jax.ShapeDtypeStruct(s, t) for s, t in ou...  10.9 us
    ppermute x11, starting transfers between devices, over_dp(): return lax.ppermute(x, 'dp', [(i, i ^ flip) for i in range(groups)])  8.66 us
    ppermute x12, waiting for transfers between devices, over_experts(): return lax.ppermute(x, 'expert', [(i, i ^ flip) for i in range(experts)])  6.89 us
  transfers between devices with their start and end apart: 23, of which 12 were waited for; matrix products, arithmetic and copies ran while one was open for 0% of the time, Pallas kernels for 9%

profile of v5, /device:TPU:0, one launch (start us, length us, event | category | flops | bytes accessed | tf_op | source)
XLA Modules:
  0.0 56.4 jit_solution(9949662712222289000)
XLA Ops:
  0.6 2.6 %shard_map.136 = (bf16[2,256,128]{2,1,0:T(8,128)(2,1)}, bf16[128,2176]{1,0:T(8,128)(2,1)}, bf16[128,1152]{1,0:T(8,128)(2,1)}, bf16[128,1152]{1,0:T(8,128)(2,1)}) custom-call(s32[1]{0:T(128)} %bitcast.refs_0_, s32[1]{0:T(128)} %bitcast.1.refs_1_, bf16[128,2048]{1,0:T(8,128)(2,1)} %refs_2_.1, bf16[128,2048]{1,0:T(8,128)(2,1)} %refs_3_.1, ...), custom_call_target="tpu_custom_call" | custom-call | bytes 2463752 | tf_op jit(solution)/shard_map/pallas_call | solution.py:16
  3.2 4.1 %collective-permute-start.1 = (bf16[2,256,128]{2,1,0:T(8,128)(2,1)}, bf16[2,256,128]{2,1,0:T(8,128)(2,1)S(1)}, u32[]{:S(2)}, u32[]{:S(2)}) collective-permute-start(bf16[2,256,128]{2,1,0:T(8,128)(2,1)} %get-tuple-element.55.refs_0_.refs_5_), channel_id=1, source_target_pairs={{0,16},{4,20},{8,24},{12,28},{16,0},{20,4},{24,8},{28,12},{1,17},{... | collective-permute-start | bytes 393224 | tf_op jit(solution)/shard_map/banks_dp4/ppermute | solution.py:359
  7.3 1.6 %collective-permute-start = (bf16[128,2176]{1,0:T(8,128)(2,1)}, bf16[128,2176]{1,0:T(8,128)(2,1)S(1)}, u32[]{:S(2)}, u32[]{:S(2)}) collective-permute-start(bf16[128,2176]{1,0:T(8,128)(2,1)} %get-tuple-element.54), channel_id=1, source_target_pairs={{0,8},{4,12},{8,0},{12,4},{16,24},{20,28},{24,16},{28,20},{1,9},{5... | collective-permute-start | bytes 1671176 | tf_op jit(solution)/shard_map/rows_dp2/ppermute | solution.py:359
  8.9 2.4 %collective-permute-start.7 = (bf16[2,256,128]{2,1,0:T(8,128)(2,1)}, bf16[2,256,128]{2,1,0:T(8,128)(2,1)S(1)}, u32[]{:S(2)}, u32[]{:S(2)}) collective-permute-start(bf16[2,256,128]{2,1,0:T(8,128)(2,1)} %get-tuple-element.55.refs_0_.refs_5_), channel_id=1, source_target_pairs={{0,3},{1,2},{2,1},{3,0},{4,7},{5,6},{6,5},{7,4},{8,11},{9,10},{10,... | collective-permute-start | bytes 393224 | tf_op jit(solution)/shard_map/banks_expert3/ppermute | solution.py:363
  12.4 1.5 %collective-permute-done.1.in_ref = bf16[2,256,128]{2,1,0:T(8,128)(2,1)S(1)} collective-permute-done((bf16[2,256,128]{2,1,0:T(8,128)(2,1)}, bf16[2,256,128]{2,1,0:T(8,128)(2,1)S(1)}, u32[]{:S(2)}, u32[]{:S(2)}) %collective-permute-start.1) | collective-permute-done | bytes 131104 | tf_op jit(solution)/shard_map/banks_dp4/ppermute | solution.py:359
  13.9 2.6 %collective-permute-start.10 = (bf16[2,256,128]{2,1,0:T(8,128)(2,1)S(1)}, bf16[2,256,128]{2,1,0:T(8,128)(2,1)S(1)}, u32[]{:S(2)}, u32[]{:S(2)}) collective-permute-start(bf16[2,256,128]{2,1,0:T(8,128)(2,1)S(1)} %shard_map.137.refs_0_.refs_6_), channel_id=1, source_target_pairs={{0,3},{1,2},{2,1},{3,0},{4,7},{5,6},{6,5},{7,4},{8,11},{9,10},{10,... | collective-permute-start | bytes 393224 | tf_op jit(solution)/shard_map/other_banks_expert3/ppermute | solution.py:363
  16.5 1.3 %collective-permute-start.9 = (bf16[2,256,128]{2,1,0:T(8,128)(2,1)S(1)}, bf16[2,256,128]{2,1,0:T(8,128)(2,1)S(1)}, u32[]{:S(2)}, u32[]{:S(2)}) collective-permute-start(bf16[2,256,128]{2,1,0:T(8,128)(2,1)S(1)} %shard_map.137.refs_0_.refs_6_), channel_id=1, source_target_pairs={{0,2},{1,3},{2,0},{3,1},{4,6},{5,7},{6,4},{7,5},{8,10},{9,11},{10,... | collective-permute-start | bytes 393224 | tf_op jit(solution)/shard_map/other_banks_expert2/ppermute | solution.py:363
  17.8 3.2 %collective-permute-done.6.refs_2_.refs_9_ = bf16[2,256,128]{2,1,0:T(8,128)(2,1)S(1)} collective-permute-done((bf16[2,256,128]{2,1,0:T(8,128)(2,1)}, bf16[2,256,128]{2,1,0:T(8,128)(2,1)S(1)}, u32[]{:S(2)}, u32[]{:S(2)}) %collective-permute-start.6) | collective-permute-done | bytes 131104 | tf_op jit(solution)/shard_map/banks_expert2/ppermute | solution.py:363
  20.9 1.5 %collective-permute-start.8 = (bf16[2,256,128]{2,1,0:T(8,128)(2,1)S(1)}, bf16[2,256,128]{2,1,0:T(8,128)(2,1)S(1)}, u32[]{:S(2)}, u32[]{:S(2)}) collective-permute-start(bf16[2,256,128]{2,1,0:T(8,128)(2,1)S(1)} %shard_map.137.refs_0_.refs_6_), channel_id=1, source_target_pairs={{0,1},{1,0},{2,3},{3,2},{4,5},{5,4},{6,7},{7,6},{8,9},{9,8},{10,11... | collective-permute-start | bytes 393224 | tf_op jit(solution)/shard_map/other_banks_expert1/ppermute | solution.py:363
  24.4 1.5 %collective-permute-done.8.refs_1_.refs_8_ = bf16[2,256,128]{2,1,0:T(8,128)(2,1)S(1)} collective-permute-done((bf16[2,256,128]{2,1,0:T(8,128)(2,1)S(1)}, bf16[2,256,128]{2,1,0:T(8,128)(2,1)S(1)}, u32[]{:S(2)}, u32[]{:S(2)}) %collective-permute-start.8) | collective-permute-done | bytes 131104 | tf_op jit(solution)/shard_map/other_banks_expert1/ppermute | solution.py:363
  27.7 1.3 %collective-permute-done.11.got_ref = bf16[256,256]{1,0:T(8,128)(2,1)S(1)} collective-permute-done((bf16[256,256]{1,0:T(8,128)(2,1)S(1)}, bf16[256,256]{1,0:T(8,128)(2,1)S(1)}, u32[]{:S(2)}, u32[]{:S(2)}) %collective-permute-start.11) | collective-permute-done | bytes 131104 | tf_op jit(solution)/shard_map/partials_dp1/ppermute | solution.py:359
  29.8 1.2 %shard_map.146.refs_4_ = bf16[512,512]{1,0:T(8,128)(2,1)S(1)} custom-call(bf16[128,1152]{1,0:T(8,128)(2,1)S(1)} %copy-done, bf16[128,2176]{1,0:T(8,128)(2,1)S(1)} %collective-permute-done.in_ref.refs_1_, bf16[128,1152]{1,0:T(8,128)(2,1)S(1)} %collective-permute-done.2.refs_2_, bf16[128,1152]{1,0:T(8,128)(2,1)S(1)} %collective-permute-done.3.refs_3_, ...), custom_call_target="tpu_custom_call" | custom-call | flops 536870912 | bytes 3276800 | tf_op jit(solution)/shard_map/pallas_call | solution.py:16
  31.0 3.7 %collective-permute-done.12.got_ref = bf16[256,256]{1,0:T(8,128)(2,1)S(1)} collective-permute-done((bf16[256,256]{1,0:T(8,128)(2,1)S(1)}, bf16[256,256]{1,0:T(8,128)(2,1)S(1)}, u32[]{:S(2)}, u32[]{:S(2)}) %collective-permute-start.12) | collective-permute-done | bytes 131104 | tf_op jit(solution)/shard_map/partials_dp2/ppermute | solution.py:359
  35.0 1.3 %collective-permute-done.13.refs_6_ = bf16[256,256]{1,0:T(8,128)(2,1)S(1)} collective-permute-done((bf16[256,256]{1,0:T(8,128)(2,1)S(1)}, bf16[256,256]{1,0:T(8,128)(2,1)S(1)}, u32[]{:S(2)}, u32[]{:S(2)}) %collective-permute-start.13) | collective-permute-done | bytes 131104 | tf_op jit(solution)/shard_map/head_rows_dp1/ppermute | solution.py:359
  36.3 1.3 %shard_map.148 = (f32[2,256,128]{2,1,0:T(8,128)S(1)}, f32[2,256,128]{2,1,0:T(8,128)S(1)}, bf16[2,256,128]{2,1,0:T(8,128)(2,1)S(1)}, bf16[2,256,128]{2,1,0:T(8,12...) custom-call(bf16[1024,512]{1,0:T(8,128)(2,1)S(1)} %shard_map.145.ref, ...), custom_call_target="tpu_custom_call" | custom-call | flops 805306368 | bytes 4587520 | tf_op jit(solution)/shard_map/pallas_call | solution.py:16
  38.6 1.2 %collective-permute-start.20 = (bf16[2,256,128]{2,1,0:T(8,128)(2,1)S(1)}, bf16[2,256,128]{2,1,0:T(8,128)(2,1)S(1)}, u32[]{:S(2)}, u32[]{:S(2)}) collective-permute-start(bf16[2,256,128]{2,1,0:T(8,128)(2,1)S(1)} %get-tuple-element.84), channel_id=1, source_target_pairs={{0,2},{1,3},{2,0},{3,1},{4,6},{5,7},{6,4},{7,5},{8,10},{9,11},{10,... | collective-permute-start | bytes 393224 | tf_op jit(solution)/shard_map/grads_expert2/ppermute | solution.py:363
  39.9 1.5 %collective-permute-start.21 = (bf16[2,256,128]{2,1,0:T(8,128)(2,1)S(1)}, bf16[2,256,128]{2,1,0:T(8,128)(2,1)S(1)}, u32[]{:S(2)}, u32[]{:S(2)}) collective-permute-start(bf16[2,256,128]{2,1,0:T(8,128)(2,1)S(1)} %get-tuple-element.85), channel_id=1, source_target_pairs={{0,3},{1,2},{2,1},{3,0},{4,7},{5,6},{6,5},{7,4},{8,11},{9,10},{10,... | collective-permute-start | bytes 393224 | tf_op jit(solution)/shard_map/grads_expert3/ppermute | solution.py:363
  42.2 1.4 %collective-permute-start.16 = (bf16[2,256,128]{2,1,0:T(8,128)(2,1)S(1)}, bf16[2,256,128]{2,1,0:T(8,128)(2,1)S(1)}, u32[]{:S(2)}, u32[]{:S(2)}) collective-permute-start(bf16[2,256,128]{2,1,0:T(8,128)(2,1)S(1)} %get-tuple-element.79), channel_id=1, source_target_pairs={{0,1},{1,0},{2,3},{3,2},{4,5},{5,4},{6,7},{7,6},{8,9},{9,8},{10,11... | collective-permute-start | bytes 393224 | tf_op jit(solution)/shard_map/grads_expert1/ppermute | solution.py:363
  44.2 1.0 %collective-permute-start.17 = (bf16[2,256,128]{2,1,0:T(8,128)(2,1)S(1)}, bf16[2,256,128]{2,1,0:T(8,128)(2,1)S(1)}, u32[]{:S(2)}, u32[]{:S(2)}) collective-permute-start(bf16[2,256,128]{2,1,0:T(8,128)(2,1)S(1)} %get-tuple-element.80), channel_id=1, source_target_pairs={{0,2},{1,3},{2,0},{3,1},{4,6},{5,7},{6,4},{7,5},{8,10},{9,11},{10,... | collective-permute-start | bytes 393224 | tf_op jit(solution)/shard_map/grads_expert2/ppermute | solution.py:363
  45.2 1.7 %collective-permute-done.20.refs_2_ = bf16[2,256,128]{2,1,0:T(8,128)(2,1)S(1)} collective-permute-done((bf16[2,256,128]{2,1,0:T(8,128)(2,1)S(1)}, bf16[2,256,128]{2,1,0:T(8,128)(2,1)S(1)}, u32[]{:S(2)}, u32[]{:S(2)}) %collective-permute-start.20) | collective-permute-done | bytes 131104 | tf_op jit(solution)/shard_map/grads_expert2/ppermute | solution.py:363
  46.8 1.4 %collective-permute-start.18 = (bf16[2,256,128]{2,1,0:T(8,128)(2,1)S(1)}, bf16[2,256,128]{2,1,0:T(8,128)(2,1)S(1)}, u32[]{:S(2)}, u32[]{:S(2)}) collective-permute-start(bf16[2,256,128]{2,1,0:T(8,128)(2,1)S(1)} %get-tuple-element.81), channel_id=1, source_target_pairs={{0,3},{1,2},{2,1},{3,0},{4,7},{5,6},{6,5},{7,4},{8,11},{9,10},{10,... | collective-permute-start | bytes 393224 | tf_op jit(solution)/shard_map/grads_expert3/ppermute | solution.py:363
  48.3 1.2 %collective-permute-start.22 = (bf16[2,256,128]{2,1,0:T(8,128)(2,1)S(1)}, bf16[2,256,128]{2,1,0:T(8,128)(2,1)S(1)}, u32[]{:S(2)}, u32[]{:S(2)}) collective-permute-start(bf16[2,256,128]{2,1,0:T(8,128)(2,1)S(1)} %shard_map.152), channel_id=1, source_target_pairs={{0,16},{4,20},{8,24},{12,28},{16,0},{20,4},{24,8},{28,12},{1,17},{... | collective-permute-start | bytes 393224 | tf_op jit(solution)/shard_map/grads_dp4/ppermute | solution.py:359
  49.5 1.1 %shard_map.153 = (bf16[128,128]{1,0:T(8,128)(2,1)}, bf16[128,128]{1,0:T(8,128)(2,1)}) custom-call(f32[128,128]{1,0:T(8,128)S(1)} %get-tuple-element.87.probs_ref, bf16[128,128]{1,0:T(8,128)(2,1)S(1)} %copy-done.2, bf16[128,128]{1,0:T(8,128)(2,1)S(1)} %copy-done.3, bf16[128,128]{1,0:T(8,128)(2,1)S(1)} %get-tuple-element.88.mixed_ref, ...), custom_call_target="tpu_custom_call" | custom-call | bytes 262144 | tf_op jit(solution)/shard_map/pallas_call | solution.py:16
  52.9 2.8 %collective-permute-done.22.refs_4_ = bf16[2,256,128]{2,1,0:T(8,128)(2,1)S(1)} collective-permute-done((bf16[2,256,128]{2,1,0:T(8,128)(2,1)S(1)}, bf16[2,256,128]{2,1,0:T(8,128)(2,1)S(1)}, u32[]{:S(2)}, u32[]{:S(2)}) %collective-permute-start.22) | collective-permute-done | bytes 131104 | tf_op jit(solution)/shard_map/grads_dp4/ppermute | solution.py:359
  (55 shorter events, 11.2 us)
Async XLA Ops:
  3.2 10.7 %collective-permute-start.1 = (bf16[2,256,128]{2,1,0:T(8,128)(2,1)}, bf16[2,256,128]{2,1,0:T(8,128)(2,1)S(1)}, u32[]{:S(2)}, u32[]{:S(2)}) collective-permute-start(bf16[2,256,128]{2,1,0:T(8,128)(2,1)} %get-tuple-element.55.refs_0_.refs_5_), channel_id=1, source_target_pairs={{0,16},{4,20},{8,24},{12,28},{16,0},{20,4},{24,8},{28,12},{1,17},{... | collective-permute-start | bytes 393224 | tf_op jit(solution)/shard_map/banks_dp4/ppermute | solution.py:359
  7.3 15.1 %copy-start.3 = (bf16[128,128]{1,0:T(8,128)(2,1)S(1)}, bf16[128,128]{1,0:T(8,128)(2,1)}, u32[]{:S(2)}) copy-start(bf16[128,128]{1,0:T(8,128)(2,1)} %k_ref.3) | copy-start | bytes 98308
  7.3 16.3 %collective-permute-start = (bf16[128,2176]{1,0:T(8,128)(2,1)}, bf16[128,2176]{1,0:T(8,128)(2,1)S(1)}, u32[]{:S(2)}, u32[]{:S(2)}) collective-permute-start(bf16[128,2176]{1,0:T(8,128)(2,1)} %get-tuple-element.54), channel_id=1, source_target_pairs={{0,8},{4,12},{8,0},{12,4},{16,24},{20,28},{24,16},{28,20},{1,9},{5... | collective-permute-start | bytes 1671176 | tf_op jit(solution)/shard_map/rows_dp2/ppermute | solution.py:359
  8.9 7.6 %collective-permute-start.7 = (bf16[2,256,128]{2,1,0:T(8,128)(2,1)}, bf16[2,256,128]{2,1,0:T(8,128)(2,1)S(1)}, u32[]{:S(2)}, u32[]{:S(2)}) collective-permute-start(bf16[2,256,128]{2,1,0:T(8,128)(2,1)} %get-tuple-element.55.refs_0_.refs_5_), channel_id=1, source_target_pairs={{0,3},{1,2},{2,1},{3,0},{4,7},{5,6},{6,5},{7,4},{8,11},{9,10},{10,... | collective-permute-start | bytes 393224 | tf_op jit(solution)/shard_map/banks_expert3/ppermute | solution.py:363
  11.3 9.6 %collective-permute-start.6 = (bf16[2,256,128]{2,1,0:T(8,128)(2,1)}, bf16[2,256,128]{2,1,0:T(8,128)(2,1)S(1)}, u32[]{:S(2)}, u32[]{:S(2)}) collective-permute-start(bf16[2,256,128]{2,1,0:T(8,128)(2,1)} %get-tuple-element.55.refs_0_.refs_5_), channel_id=1, source_target_pairs={{0,2},{1,3},{2,0},{3,1},{4,6},{5,7},{6,4},{7,5},{8,10},{9,11},{10,... | collective-permute-start | bytes 393224 | tf_op jit(solution)/shard_map/banks_expert2/ppermute | solution.py:363
  11.8 10.9 %collective-permute-start.5 = (bf16[2,256,128]{2,1,0:T(8,128)(2,1)}, bf16[2,256,128]{2,1,0:T(8,128)(2,1)S(1)}, u32[]{:S(2)}, u32[]{:S(2)}) collective-permute-start(bf16[2,256,128]{2,1,0:T(8,128)(2,1)} %get-tuple-element.55.refs_0_.refs_5_), channel_id=1, source_target_pairs={{0,1},{1,0},{2,3},{3,2},{4,5},{5,4},{6,7},{7,6},{8,9},{9,8},{10,11... | collective-permute-start | bytes 393224 | tf_op jit(solution)/shard_map/banks_expert1/ppermute | solution.py:363
  13.9 9.9 %collective-permute-start.10 = (bf16[2,256,128]{2,1,0:T(8,128)(2,1)S(1)}, bf16[2,256,128]{2,1,0:T(8,128)(2,1)S(1)}, u32[]{:S(2)}, u32[]{:S(2)}) collective-permute-start(bf16[2,256,128]{2,1,0:T(8,128)(2,1)S(1)} %shard_map.137.refs_0_.refs_6_), channel_id=1, source_target_pairs={{0,3},{1,2},{2,1},{3,0},{4,7},{5,6},{6,5},{7,4},{8,11},{9,10},{10,... | collective-permute-start | bytes 393224 | tf_op jit(solution)/shard_map/other_banks_expert3/ppermute | solution.py:363
  16.5 7.9 %collective-permute-start.9 = (bf16[2,256,128]{2,1,0:T(8,128)(2,1)S(1)}, bf16[2,256,128]{2,1,0:T(8,128)(2,1)S(1)}, u32[]{:S(2)}, u32[]{:S(2)}) collective-permute-start(bf16[2,256,128]{2,1,0:T(8,128)(2,1)S(1)} %shard_map.137.refs_0_.refs_6_), channel_id=1, source_target_pairs={{0,2},{1,3},{2,0},{3,1},{4,6},{5,7},{6,4},{7,5},{8,10},{9,11},{10,... | collective-permute-start | bytes 393224 | tf_op jit(solution)/shard_map/other_banks_expert2/ppermute | solution.py:363
  20.9 5.0 %collective-permute-start.8 = (bf16[2,256,128]{2,1,0:T(8,128)(2,1)S(1)}, bf16[2,256,128]{2,1,0:T(8,128)(2,1)S(1)}, u32[]{:S(2)}, u32[]{:S(2)}) collective-permute-start(bf16[2,256,128]{2,1,0:T(8,128)(2,1)S(1)} %shard_map.137.refs_0_.refs_6_), channel_id=1, source_target_pairs={{0,1},{1,0},{2,3},{3,2},{4,5},{5,4},{6,7},{7,6},{8,9},{9,8},{10,11... | collective-permute-start | bytes 393224 | tf_op jit(solution)/shard_map/other_banks_expert1/ppermute | solution.py:363
  22.8 4.0 %collective-permute-start.4 = (bf16[128,128]{1,0:T(8,128)(2,1)S(1)}, bf16[128,128]{1,0:T(8,128)(2,1)S(1)}, u32[]{:S(2)}, u32[]{:S(2)}) collective-permute-start(bf16[128,128]{1,0:T(8,128)(2,1)S(1)} %get-tuple-element.58.weights_ref), channel_id=1, source_target_pairs={{0,8},{4,12},{8,0},{12,4},{16,24},{20,28},{24,16},{28,20},{1,9},{5... | collective-permute-start | bytes 98312 | tf_op jit(solution)/shard_map/weights_dp2/ppermute | solution.py:359
  23.8 3.0 %collective-permute-start.2 = (bf16[128,1152]{1,0:T(8,128)(2,1)S(1)}, bf16[128,1152]{1,0:T(8,128)(2,1)S(1)}, u32[]{:S(2)}, u32[]{:S(2)}) collective-permute-start(bf16[128,1152]{1,0:T(8,128)(2,1)S(1)} %copy-done.6), channel_id=1, source_target_pairs={{0,4},{4,0},{8,12},{12,8},{16,20},{20,16},{24,28},{28,24},{1,5},{5... | collective-permute-start | bytes 884744 | tf_op jit(solution)/shard_map/rows_dp1/ppermute | solution.py:359
  23.8 3.0 %collective-permute-start.3 = (bf16[128,1152]{1,0:T(8,128)(2,1)S(1)}, bf16[128,1152]{1,0:T(8,128)(2,1)S(1)}, u32[]{:S(2)}, u32[]{:S(2)}) collective-permute-start(bf16[128,1152]{1,0:T(8,128)(2,1)S(1)} %shard_map.138), channel_id=1, source_target_pairs={{0,4},{4,0},{8,12},{12,8},{16,20},{20,16},{24,28},{28,24},{1,5},{5... | collective-permute-start | bytes 884744 | tf_op jit(solution)/shard_map/far_rows_dp1/ppermute | solution.py:359
  27.6 1.4 %collective-permute-start.11 = (bf16[256,256]{1,0:T(8,128)(2,1)S(1)}, bf16[256,256]{1,0:T(8,128)(2,1)S(1)}, u32[]{:S(2)}, u32[]{:S(2)}) collective-permute-start(bf16[256,256]{1,0:T(8,128)(2,1)S(1)} %get-tuple-element.62), channel_id=1, source_target_pairs={{0,4},{4,0},{8,12},{12,8},{16,20},{20,16},{24,28},{28,24},{1,5},{5... | collective-permute-start | bytes 393224 | tf_op jit(solution)/shard_map/partials_dp1/ppermute | solution.py:359
  29.1 5.6 %collective-permute-start.12 = (bf16[256,256]{1,0:T(8,128)(2,1)S(1)}, bf16[256,256]{1,0:T(8,128)(2,1)S(1)}, u32[]{:S(2)}, u32[]{:S(2)}) collective-permute-start(bf16[256,256]{1,0:T(8,128)(2,1)S(1)} %get-tuple-element.63), channel_id=1, source_target_pairs={{0,8},{4,12},{8,0},{12,4},{16,24},{20,28},{24,16},{28,20},{1,9},{5... | collective-permute-start | bytes 393224 | tf_op jit(solution)/shard_map/partials_dp2/ppermute | solution.py:359
  34.9 1.4 %collective-permute-start.13 = (bf16[256,256]{1,0:T(8,128)(2,1)S(1)}, bf16[256,256]{1,0:T(8,128)(2,1)S(1)}, u32[]{:S(2)}, u32[]{:S(2)}) collective-permute-start(bf16[256,256]{1,0:T(8,128)(2,1)S(1)} %get-tuple-element.72.refs_5_), channel_id=1, source_target_pairs={{0,4},{4,0},{8,12},{12,8},{16,20},{20,16},{24,28},{28,24},{1,5},{5... | collective-permute-start | bytes 393224 | tf_op jit(solution)/shard_map/head_rows_dp1/ppermute | solution.py:359
  37.6 3.7 %collective-permute-start.14 = (bf16[256,640]{1,0:T(8,128)(2,1)S(1)}, bf16[256,640]{1,0:T(8,128)(2,1)S(1)}, u32[]{:S(2)}, u32[]{:S(2)}) collective-permute-start(bf16[256,640]{1,0:T(8,128)(2,1)S(1)} %get-tuple-element.74), channel_id=1, source_target_pairs={{0,4},{4,0},{8,12},{12,8},{16,20},{20,16},{24,28},{28,24},{1,5},{5... | collective-permute-start | bytes 983048 | tf_op jit(solution)/shard_map/token_back_dp1/ppermute | solution.py:359
  37.8 6.3 %collective-permute-start.19 = (bf16[2,256,128]{2,1,0:T(8,128)(2,1)S(1)}, bf16[2,256,128]{2,1,0:T(8,128)(2,1)S(1)}, u32[]{:S(2)}, u32[]{:S(2)}) collective-permute-start(bf16[2,256,128]{2,1,0:T(8,128)(2,1)S(1)} %get-tuple-element.83), channel_id=1, source_target_pairs={{0,1},{1,0},{2,3},{3,2},{4,5},{5,4},{6,7},{7,6},{8,9},{9,8},{10,11... | collective-permute-start | bytes 393224 | tf_op jit(solution)/shard_map/grads_expert1/ppermute | solution.py:363
  38.6 8.2 %collective-permute-start.20 = (bf16[2,256,128]{2,1,0:T(8,128)(2,1)S(1)}, bf16[2,256,128]{2,1,0:T(8,128)(2,1)S(1)}, u32[]{:S(2)}, u32[]{:S(2)}) collective-permute-start(bf16[2,256,128]{2,1,0:T(8,128)(2,1)S(1)} %get-tuple-element.84), channel_id=1, source_target_pairs={{0,2},{1,3},{2,0},{3,1},{4,6},{5,7},{6,4},{7,5},{8,10},{9,11},{10,... | collective-permute-start | bytes 393224 | tf_op jit(solution)/shard_map/grads_expert2/ppermute | solution.py:363
  39.9 8.4 %collective-permute-start.21 = (bf16[2,256,128]{2,1,0:T(8,128)(2,1)S(1)}, bf16[2,256,128]{2,1,0:T(8,128)(2,1)S(1)}, u32[]{:S(2)}, u32[]{:S(2)}) collective-permute-start(bf16[2,256,128]{2,1,0:T(8,128)(2,1)S(1)} %get-tuple-element.85), channel_id=1, source_target_pairs={{0,3},{1,2},{2,1},{3,0},{4,7},{5,6},{6,5},{7,4},{8,11},{9,10},{10,... | collective-permute-start | bytes 393224 | tf_op jit(solution)/shard_map/grads_expert3/ppermute | solution.py:363
  41.8 8.9 %collective-permute-start.15 = (bf16[128,1152]{1,0:T(8,128)(2,1)S(1)}, bf16[128,1152]{1,0:T(8,128)(2,1)S(1)}, u32[]{:S(2)}, u32[]{:S(2)}) collective-permute-start(bf16[128,1152]{1,0:T(8,128)(2,1)S(1)} %get-tuple-element.76), channel_id=1, source_target_pairs={{0,8},{4,12},{8,0},{12,4},{16,24},{20,28},{24,16},{28,20},{1,9},{5... | collective-permute-start | bytes 884744 | tf_op jit(solution)/shard_map/token_back_dp2/ppermute | solution.py:359
  42.2 10.7 %collective-permute-start.16 = (bf16[2,256,128]{2,1,0:T(8,128)(2,1)S(1)}, bf16[2,256,128]{2,1,0:T(8,128)(2,1)S(1)}, u32[]{:S(2)}, u32[]{:S(2)}) collective-permute-start(bf16[2,256,128]{2,1,0:T(8,128)(2,1)S(1)} %get-tuple-element.79), channel_id=1, source_target_pairs={{0,1},{1,0},{2,3},{3,2},{4,5},{5,4},{6,7},{7,6},{8,9},{9,8},{10,11... | collective-permute-start | bytes 393224 | tf_op jit(solution)/shard_map/grads_expert1/ppermute | solution.py:363
  44.2 8.7 %collective-permute-start.17 = (bf16[2,256,128]{2,1,0:T(8,128)(2,1)S(1)}, bf16[2,256,128]{2,1,0:T(8,128)(2,1)S(1)}, u32[]{:S(2)}, u32[]{:S(2)}) collective-permute-start(bf16[2,256,128]{2,1,0:T(8,128)(2,1)S(1)} %get-tuple-element.80), channel_id=1, source_target_pairs={{0,2},{1,3},{2,0},{3,1},{4,6},{5,7},{6,4},{7,5},{8,10},{9,11},{10,... | collective-permute-start | bytes 393224 | tf_op jit(solution)/shard_map/grads_expert2/ppermute | solution.py:363
  46.8 6.1 %collective-permute-start.18 = (bf16[2,256,128]{2,1,0:T(8,128)(2,1)S(1)}, bf16[2,256,128]{2,1,0:T(8,128)(2,1)S(1)}, u32[]{:S(2)}, u32[]{:S(2)}) collective-permute-start(bf16[2,256,128]{2,1,0:T(8,128)(2,1)S(1)} %get-tuple-element.81), channel_id=1, source_target_pairs={{0,3},{1,2},{2,1},{3,0},{4,7},{5,6},{6,5},{7,4},{8,11},{9,10},{10,... | collective-permute-start | bytes 393224 | tf_op jit(solution)/shard_map/grads_expert3/ppermute | solution.py:363
  48.3 7.3 %collective-permute-start.22 = (bf16[2,256,128]{2,1,0:T(8,128)(2,1)S(1)}, bf16[2,256,128]{2,1,0:T(8,128)(2,1)S(1)}, u32[]{:S(2)}, u32[]{:S(2)}) collective-permute-start(bf16[2,256,128]{2,1,0:T(8,128)(2,1)S(1)} %shard_map.152), channel_id=1, source_target_pairs={{0,16},{4,20},{8,24},{12,28},{16,0},{20,4},{24,8},{28,12},{1,17},{... | collective-permute-start | bytes 393224 | tf_op jit(solution)/shard_map/grads_dp4/ppermute | solution.py:359
  (6 other events, 29.6 us)

commit v6 on v5

--- a/solution.py
+++ b/solution.py
@@ -72,15 +72,17 @@
         )
 
 
-def pack_body(block, quads, groups, at_ref, me_ref, tokens_ref, cotangent_ref, value_ref, output_ref, *refs):
-    small_refs, bank_ref, out_refs, held_refs, sems = refs[:3], refs[3], refs[4:7], refs[7:10], refs[10]
+def pack_body(block, quads, groups, bank_count, at_ref, me_ref, tokens_ref, cotangent_ref, *refs):
+    bank_refs, refs = refs[:bank_count], refs[bank_count:]
+    small_refs, held_refs, sems = refs[:3], refs[-4:-1], refs[-1]
+    out_refs = refs[-4 - len(groups) : -4]
     small = [
         pltpu.make_async_copy(ref, held, sems.at[i])
         for i, (ref, held) in enumerate(zip(small_refs, held_refs))
     ]
     copies = [
-        pltpu.make_async_copy(ref.at[0], bank_ref.at[i], sems.at[3 + i])
-        for i, ref in enumerate((value_ref, output_ref))
+        pltpu.make_async_copy(ref.at[0], refs[3].at[i], sems.at[3 + i])
+        for i, ref in enumerate(bank_refs)
     ]
     for group, out_ref in zip(groups, out_refs):
         to = 0
@@ -368,23 +370,27 @@
     routing = (gate_logits.T, value_routes.T, output_routes.T)
     flips = ((2, 3), (1,), (0,))
     if aligned:
-        own_banks, sent_rows, core_rows, own_rows = kernel_call(
-            lambda *refs: pack_body(block, quads, flips, *refs),
-            [((2, block, size), BF16)]
-            + [((count, 2 * half * len(group) + 128), BF16) for group in flips],
-            at[None],
-            me[None],
-            tokens,
-            cotangent,
-            value_weight,
-            output_weight,
-            *routing,
-            scalars=2,
-            where=pl.ANY,
-            scratch=[pltpu.VMEM(x.shape, x.dtype) for x in routing]
-            + [pltpu.SemaphoreType.DMA((5 + 8 * quads,))],
-            vmem=60,
-        )
+
+        def pack(groups, *banks):
+            return kernel_call(
+                lambda *refs: pack_body(block, quads, groups, len(banks), *refs),
+                [((2, block, size), BF16)] * (len(banks) // 2)
+                + [((count, 2 * half * len(group) + 128), BF16) for group in groups],
+                at[None],
+                me[None],
+                tokens,
+                cotangent,
+                *banks,
+                *routing,
+                scalars=2,
+                where=pl.ANY,
+                scratch=[pltpu.VMEM(x.shape, x.dtype) for x in routing]
+                + [pltpu.SemaphoreType.DMA((5 + 8 * quads,))],
+                vmem=60,
+            )
+
+        own_banks, sent_rows = pack(flips[:1], value_weight, output_weight)
+        core_rows, own_rows = pack(flips[1:])
     else:
         own_banks = jnp.concatenate([value_weight, output_weight], axis=0)
         (own_table,) = kernel_call(

time: 56.6 us -> 56 us (0.989)
  waiting for transfers between devices: 19 us -> 13.7 us
  starting transfers between devices: 24.8 us -> 27.8 us
  Pallas kernels: 10.9 us -> 12.7 us
    ppermute x12, waiting for transfers between devices: 6.89 us -> 2.85 us  [over_experts(): return lax.ppermute(x, 'expert', [(i, i ^ flip) for i in range(experts)])]
    pallas_call x19 -> x20, Pallas kernels: 10.9 us -> 12.7 us  [kernel_call(): pl.pallas_call(body, out_shape=[jax.ShapeDtypeStruct(s, t) for s, t in ou...]
    ppermute x12, starting transfers between devices: 16.2 us -> 17.8 us  [over_experts(): return lax.ppermute(x, 'expert', [(i, i ^ flip) for i in range(experts)])]
    ppermute x11, starting transfers between devices: 8.66 us -> 10 us  [over_dp(): return lax.ppermute(x, 'dp', [(i, i ^ flip) for i in range(groups)])]
    ppermute x11, waiting for transfers between devices: 12.1 us -> 10.9 us  [over_dp(): return lax.ppermute(x, 'dp', [(i, i ^ flip) for i in range(groups)])]
  transfers between devices with their start and end apart: 23 -> 23, of which waited for: 12 -> 9; matrix products, arithmetic and copies ran while one was open for 0% -> 0% of each run, Pallas kernels for 9% -> 13%
where the time goes in v6:
time: 56 us; the launch traced here: 55.8 us
  starting transfers between devices  27.8 us (50%)
  waiting for transfers between devices  13.7 us (24%)
  Pallas kernels  12.7 us (23%)
  between operations  0.86 us (2%)
  local copies, waits for them, and re-layouts  0.71 us (1%)
    ppermute x12, starting transfers between devices, over_experts(): return lax.ppermute(x, 'expert', [(i, i ^ flip) for i in range(experts)])  17.8 us
    pallas_call x20, Pallas kernels, kernel_call(): pl.pallas_call(body, out_shape=[jax.ShapeDtypeStruct(s, t) for s, t in ou...  12.7 us
    ppermute x11, waiting for transfers between devices, over_dp(): return lax.ppermute(x, 'dp', [(i, i ^ flip) for i in range(groups)])  10.9 us
    ppermute x11, starting transfers between devices, over_dp(): return lax.ppermute(x, 'dp', [(i, i ^ flip) for i in range(groups)])  10 us
    ppermute x12, waiting for transfers between devices, over_experts(): return lax.ppermute(x, 'expert', [(i, i ^ flip) for i in range(experts)])  2.85 us
  transfers between devices with their start and end apart: 23, of which 9 were waited for; matrix products, arithmetic and copies ran while one was open for 0% of the time, Pallas kernels for 13%

profile of v6, /device:TPU:0, one launch (start us, length us, event | category | flops | bytes accessed | tf_op | source)
XLA Modules:
  0.0 55.8 jit_solution(9803400187843560894)
XLA Ops:
  0.6 2.2 %shard_map.137 = (bf16[2,256,128]{2,1,0:T(8,128)(2,1)}, bf16[128,2176]{1,0:T(8,128)(2,1)}) custom-call(s32[1]{0:T(128)} %bitcast.refs_0_, s32[1]{0:T(128)} %bitcast.1.refs_1_, bf16[128,2048]{1,0:T(8,128)(2,1)} %refs_2_.3, bf16[128,2048]{1,0:T(8,128)(2,1)} %refs_3_.3, bf16[1,256,128]{2,1,0:T(8,128)(2,1)} %refs_4_.1, bf16[1,256,128]{2,1,0:T(8,128)(2,1)} %refs_5_.1, ...), custom_call_target="tpu_custom_call" | custom-call | bytes 1873928 | tf_op jit(solution)/shard_map/pallas_call | solution.py:16
  2.8 4.1 %collective-permute-start.1 = (bf16[2,256,128]{2,1,0:T(8,128)(2,1)}, bf16[2,256,128]{2,1,0:T(8,128)(2,1)S(1)}, u32[]{:S(2)}, u32[]{:S(2)}) collective-permute-start(bf16[2,256,128]{2,1,0:T(8,128)(2,1)} %get-tuple-element.55.refs_0_.refs_5_), channel_id=1, source_target_pairs={{0,16},{4,20},{8,24},{12,28},{16,0},{20,4},{24,8},{28,12},{1,17},{... | collective-permute-start | bytes 393224 | tf_op jit(solution)/shard_map/banks_dp4/ppermute | solution.py:361
  6.9 1.6 %collective-permute-start = (bf16[128,2176]{1,0:T(8,128)(2,1)}, bf16[128,2176]{1,0:T(8,128)(2,1)S(1)}, u32[]{:S(2)}, u32[]{:S(2)}) collective-permute-start(bf16[128,2176]{1,0:T(8,128)(2,1)} %get-tuple-element.54), channel_id=1, source_target_pairs={{0,8},{4,12},{8,0},{12,4},{16,24},{20,28},{24,16},{28,20},{1,9},{5... | collective-permute-start | bytes 1671176 | tf_op jit(solution)/shard_map/rows_dp2/ppermute | solution.py:361
  8.5 2.4 %collective-permute-start.7 = (bf16[2,256,128]{2,1,0:T(8,128)(2,1)}, bf16[2,256,128]{2,1,0:T(8,128)(2,1)S(1)}, u32[]{:S(2)}, u32[]{:S(2)}) collective-permute-start(bf16[2,256,128]{2,1,0:T(8,128)(2,1)} %get-tuple-element.55.refs_0_.refs_5_), channel_id=1, source_target_pairs={{0,3},{1,2},{2,1},{3,0},{4,7},{5,6},{6,5},{7,4},{8,11},{9,10},{10,... | collective-permute-start | bytes 393224 | tf_op jit(solution)/shard_map/banks_expert3/ppermute | solution.py:365
  12.0 2.1 %shard_map.136 = (bf16[128,1152]{1,0:T(8,128)(2,1)}, bf16[128,1152]{1,0:T(8,128)(2,1)}) custom-call(s32[1]{0:T(128)} %bitcast.refs_0_, s32[1]{0:T(128)} %bitcast.1.refs_1_, bf16[128,2048]{1,0:T(8,128)(2,1)} %refs_2_.3, bf16[128,2048]{1,0:T(8,128)(2,1)} %refs_3_.3, f32[8,128]{1,0:T(8,128)} %bitcast.13, s32[2,128]{1,0:T(2,128)} %bitcast.7, s32[2,128]{1,0:T(2,128)} %bitcast.10), custom_call_target="tpu_custom_call" | custom-call | bytes 1644552 | tf_op jit(solution)/shard_map/pallas_call | solution.py:16
  14.2 2.5 %collective-permute-start.10 = (bf16[2,256,128]{2,1,0:T(8,128)(2,1)S(1)}, bf16[2,256,128]{2,1,0:T(8,128)(2,1)S(1)}, u32[]{:S(2)}, u32[]{:S(2)}) collective-permute-start(bf16[2,256,128]{2,1,0:T(8,128)(2,1)S(1)} %shard_map.138.refs_0_.refs_6_), channel_id=1, source_target_pairs={{0,3},{1,2},{2,1},{3,0},{4,7},{5,6},{6,5},{7,4},{8,11},{9,10},{10,... | collective-permute-start | bytes 393224 | tf_op jit(solution)/shard_map/other_banks_expert3/ppermute | solution.py:365
  17.3 1.2 %collective-permute-done.6.refs_2_.refs_9_ = bf16[2,256,128]{2,1,0:T(8,128)(2,1)S(1)} collective-permute-done((bf16[2,256,128]{2,1,0:T(8,128)(2,1)}, bf16[2,256,128]{2,1,0:T(8,128)(2,1)S(1)}, u32[]{:S(2)}, u32[]{:S(2)}) %collective-permute-start.6) | collective-permute-done | bytes 131104 | tf_op jit(solution)/shard_map/banks_expert2/ppermute | solution.py:365
  18.5 2.9 %collective-permute-start.8 = (bf16[2,256,128]{2,1,0:T(8,128)(2,1)S(1)}, bf16[2,256,128]{2,1,0:T(8,128)(2,1)S(1)}, u32[]{:S(2)}, u32[]{:S(2)}) collective-permute-start(bf16[2,256,128]{2,1,0:T(8,128)(2,1)S(1)} %shard_map.138.refs_0_.refs_6_), channel_id=1, source_target_pairs={{0,1},{1,0},{2,3},{3,2},{4,5},{5,4},{6,7},{7,6},{8,9},{9,8},{10,11... | collective-permute-start | bytes 393224 | tf_op jit(solution)/shard_map/other_banks_expert1/ppermute | solution.py:365
  22.0 1.2 %collective-permute-done.in_ref.refs_1_ = bf16[128,2176]{1,0:T(8,128)(2,1)S(1)} collective-permute-done((bf16[128,2176]{1,0:T(8,128)(2,1)}, bf16[128,2176]{1,0:T(8,128)(2,1)S(1)}, u32[]{:S(2)}, u32[]{:S(2)}) %collective-permute-start) | collective-permute-done | bytes 557088 | tf_op jit(solution)/shard_map/rows_dp2/ppermute | solution.py:361
  24.5 1.3 %collective-permute-done.4.refs_4_.far_weights_ref = bf16[128,128]{1,0:T(8,128)(2,1)S(1)} collective-permute-done((bf16[128,128]{1,0:T(8,128)(2,1)S(1)}, bf16[128,128]{1,0:T(8,128)(2,1)S(1)}, u32[]{:S(2)}, u32[]{:S(2)}) %collective-permute-start.4) | collective-permute-done | bytes 32800 | tf_op jit(solution)/shard_map/weights_dp2/ppermute | solution.py:361
  26.7 1.3 %collective-permute-done.11.got_ref = bf16[256,256]{1,0:T(8,128)(2,1)S(1)} collective-permute-done((bf16[256,256]{1,0:T(8,128)(2,1)S(1)}, bf16[256,256]{1,0:T(8,128)(2,1)S(1)}, u32[]{:S(2)}, u32[]{:S(2)}) %collective-permute-start.11) | collective-permute-done | bytes 131104 | tf_op jit(solution)/shard_map/partials_dp1/ppermute | solution.py:361
  29.4 1.2 %shard_map.147.refs_4_ = bf16[512,512]{1,0:T(8,128)(2,1)S(1)} custom-call(bf16[128,1152]{1,0:T(8,128)(2,1)S(1)} %copy-done, bf16[128,2176]{1,0:T(8,128)(2,1)S(1)} %collective-permute-done.in_ref.refs_1_, bf16[128,1152]{1,0:T(8,128)(2,1)S(1)} %collective-permute-done.2.refs_2_, bf16[128,1152]{1,0:T(8,128)(2,1)S(1)} %collective-permute-done.3.refs_3_, ...), custom_call_target="tpu_custom_call" | custom-call | flops 536870912 | bytes 3276800 | tf_op jit(solution)/shard_map/pallas_call | solution.py:16
  30.6 3.1 %collective-permute-done.12.got_ref = bf16[256,256]{1,0:T(8,128)(2,1)S(1)} collective-permute-done((bf16[256,256]{1,0:T(8,128)(2,1)S(1)}, bf16[256,256]{1,0:T(8,128)(2,1)S(1)}, u32[]{:S(2)}, u32[]{:S(2)}) %collective-permute-start.12) | collective-permute-done | bytes 131104 | tf_op jit(solution)/shard_map/partials_dp2/ppermute | solution.py:361
  34.0 1.3 %collective-permute-done.13.refs_6_ = bf16[256,256]{1,0:T(8,128)(2,1)S(1)} collective-permute-done((bf16[256,256]{1,0:T(8,128)(2,1)S(1)}, bf16[256,256]{1,0:T(8,128)(2,1)S(1)}, u32[]{:S(2)}, u32[]{:S(2)}) %collective-permute-start.13) | collective-permute-done | bytes 131104 | tf_op jit(solution)/shard_map/head_rows_dp1/ppermute | solution.py:361
  35.3 1.3 %shard_map.149 = (f32[2,256,128]{2,1,0:T(8,128)S(1)}, f32[2,256,128]{2,1,0:T(8,128)S(1)}, bf16[2,256,128]{2,1,0:T(8,128)(2,1)S(1)}, bf16[2,256,128]{2,1,0:T(8,12...) custom-call(bf16[1024,512]{1,0:T(8,128)(2,1)S(1)} %shard_map.146.ref, ...), custom_call_target="tpu_custom_call" | custom-call | flops 805306368 | bytes 4587520 | tf_op jit(solution)/shard_map/pallas_call | solution.py:16
  36.9 1.0 %collective-permute-start.19 = (bf16[2,256,128]{2,1,0:T(8,128)(2,1)S(1)}, bf16[2,256,128]{2,1,0:T(8,128)(2,1)S(1)}, u32[]{:S(2)}, u32[]{:S(2)}) collective-permute-start(bf16[2,256,128]{2,1,0:T(8,128)(2,1)S(1)} %get-tuple-element.83), channel_id=1, source_target_pairs={{0,1},{1,0},{2,3},{3,2},{4,5},{5,4},{6,7},{7,6},{8,9},{9,8},{10,11... | collective-permute-start | bytes 393224 | tf_op jit(solution)/shard_map/grads_expert1/ppermute | solution.py:365
  37.9 1.5 %collective-permute-start.20 = (bf16[2,256,128]{2,1,0:T(8,128)(2,1)S(1)}, bf16[2,256,128]{2,1,0:T(8,128)(2,1)S(1)}, u32[]{:S(2)}, u32[]{:S(2)}) collective-permute-start(bf16[2,256,128]{2,1,0:T(8,128)(2,1)S(1)} %get-tuple-element.84), channel_id=1, source_target_pairs={{0,2},{1,3},{2,0},{3,1},{4,6},{5,7},{6,4},{7,5},{8,10},{9,11},{10,... | collective-permute-start | bytes 393224 | tf_op jit(solution)/shard_map/grads_expert2/ppermute | solution.py:365
  41.8 1.5 %collective-permute-start.16 = (bf16[2,256,128]{2,1,0:T(8,128)(2,1)S(1)}, bf16[2,256,128]{2,1,0:T(8,128)(2,1)S(1)}, u32[]{:S(2)}, u32[]{:S(2)}) collective-permute-start(bf16[2,256,128]{2,1,0:T(8,128)(2,1)S(1)} %get-tuple-element.79), channel_id=1, source_target_pairs={{0,1},{1,0},{2,3},{3,2},{4,5},{5,4},{6,7},{7,6},{8,9},{9,8},{10,11... | collective-permute-start | bytes 393224 | tf_op jit(solution)/shard_map/grads_expert1/ppermute | solution.py:365
  43.3 1.5 %collective-permute-start.17 = (bf16[2,256,128]{2,1,0:T(8,128)(2,1)S(1)}, bf16[2,256,128]{2,1,0:T(8,128)(2,1)S(1)}, u32[]{:S(2)}, u32[]{:S(2)}) collective-permute-start(bf16[2,256,128]{2,1,0:T(8,128)(2,1)S(1)} %get-tuple-element.80), channel_id=1, source_target_pairs={{0,2},{1,3},{2,0},{3,1},{4,6},{5,7},{6,4},{7,5},{8,10},{9,11},{10,... | collective-permute-start | bytes 393224 | tf_op jit(solution)/shard_map/grads_expert2/ppermute | solution.py:365
  44.8 1.1 %collective-permute-done.20.refs_2_ = bf16[2,256,128]{2,1,0:T(8,128)(2,1)S(1)} collective-permute-done((bf16[2,256,128]{2,1,0:T(8,128)(2,1)S(1)}, bf16[2,256,128]{2,1,0:T(8,128)(2,1)S(1)}, u32[]{:S(2)}, u32[]{:S(2)}) %collective-permute-start.20) | collective-permute-done | bytes 131104 | tf_op jit(solution)/shard_map/grads_expert2/ppermute | solution.py:365
  45.9 1.8 %collective-permute-start.18 = (bf16[2,256,128]{2,1,0:T(8,128)(2,1)S(1)}, bf16[2,256,128]{2,1,0:T(8,128)(2,1)S(1)}, u32[]{:S(2)}, u32[]{:S(2)}) collective-permute-start(bf16[2,256,128]{2,1,0:T(8,128)(2,1)S(1)} %get-tuple-element.81), channel_id=1, source_target_pairs={{0,3},{1,2},{2,1},{3,0},{4,7},{5,6},{6,5},{7,4},{8,11},{9,10},{10,... | collective-permute-start | bytes 393224 | tf_op jit(solution)/shard_map/grads_expert3/ppermute | solution.py:365
  47.7 1.4 %collective-permute-start.22 = (bf16[2,256,128]{2,1,0:T(8,128)(2,1)S(1)}, bf16[2,256,128]{2,1,0:T(8,128)(2,1)S(1)}, u32[]{:S(2)}, u32[]{:S(2)}) collective-permute-start(bf16[2,256,128]{2,1,0:T(8,128)(2,1)S(1)} %shard_map.153), channel_id=1, source_target_pairs={{0,16},{4,20},{8,24},{12,28},{16,0},{20,4},{24,8},{28,12},{1,17},{... | collective-permute-start | bytes 393224 | tf_op jit(solution)/shard_map/grads_dp4/ppermute | solution.py:361
  49.1 1.1 %shard_map.154 = (bf16[128,128]{1,0:T(8,128)(2,1)}, bf16[128,128]{1,0:T(8,128)(2,1)}) custom-call(f32[128,128]{1,0:T(8,128)S(1)} %get-tuple-element.87.probs_ref, bf16[128,128]{1,0:T(8,128)(2,1)S(1)} %copy-done.2, bf16[128,128]{1,0:T(8,128)(2,1)S(1)} %copy-done.3, bf16[128,128]{1,0:T(8,128)(2,1)S(1)} %get-tuple-element.88.mixed_ref, ...), custom_call_target="tpu_custom_call" | custom-call | bytes 262144 | tf_op jit(solution)/shard_map/pallas_call | solution.py:16
  52.5 2.6 %collective-permute-done.22.refs_4_ = bf16[2,256,128]{2,1,0:T(8,128)(2,1)S(1)} collective-permute-done((bf16[2,256,128]{2,1,0:T(8,128)(2,1)S(1)}, bf16[2,256,128]{2,1,0:T(8,128)(2,1)S(1)}, u32[]{:S(2)}, u32[]{:S(2)}) %collective-permute-start.22) | collective-permute-done | bytes 131104 | tf_op jit(solution)/shard_map/grads_dp4/ppermute | solution.py:361
  (56 shorter events, 11.6 us)
Async XLA Ops:
  2.8 11.3 %collective-permute-start.1 = (bf16[2,256,128]{2,1,0:T(8,128)(2,1)}, bf16[2,256,128]{2,1,0:T(8,128)(2,1)S(1)}, u32[]{:S(2)}, u32[]{:S(2)}) collective-permute-start(bf16[2,256,128]{2,1,0:T(8,128)(2,1)} %get-tuple-element.55.refs_0_.refs_5_), channel_id=1, source_target_pairs={{0,16},{4,20},{8,24},{12,28},{16,0},{20,4},{24,8},{28,12},{1,17},{... | collective-permute-start | bytes 393224 | tf_op jit(solution)/shard_map/banks_dp4/ppermute | solution.py:361
  6.9 16.3 %collective-permute-start = (bf16[128,2176]{1,0:T(8,128)(2,1)}, bf16[128,2176]{1,0:T(8,128)(2,1)S(1)}, u32[]{:S(2)}, u32[]{:S(2)}) collective-permute-start(bf16[128,2176]{1,0:T(8,128)(2,1)} %get-tuple-element.54), channel_id=1, source_target_pairs={{0,8},{4,12},{8,0},{12,4},{16,24},{20,28},{24,16},{28,20},{1,9},{5... | collective-permute-start | bytes 1671176 | tf_op jit(solution)/shard_map/rows_dp2/ppermute | solution.py:361
  8.5 8.2 %collective-permute-start.7 = (bf16[2,256,128]{2,1,0:T(8,128)(2,1)}, bf16[2,256,128]{2,1,0:T(8,128)(2,1)S(1)}, u32[]{:S(2)}, u32[]{:S(2)}) collective-permute-start(bf16[2,256,128]{2,1,0:T(8,128)(2,1)} %get-tuple-element.55.refs_0_.refs_5_), channel_id=1, source_target_pairs={{0,3},{1,2},{2,1},{3,0},{4,7},{5,6},{6,5},{7,4},{8,11},{9,10},{10,... | collective-permute-start | bytes 393224 | tf_op jit(solution)/shard_map/banks_expert3/ppermute | solution.py:365
  11.0 7.6 %collective-permute-start.6 = (bf16[2,256,128]{2,1,0:T(8,128)(2,1)}, bf16[2,256,128]{2,1,0:T(8,128)(2,1)S(1)}, u32[]{:S(2)}, u32[]{:S(2)}) collective-permute-start(bf16[2,256,128]{2,1,0:T(8,128)(2,1)} %get-tuple-element.55.refs_0_.refs_5_), channel_id=1, source_target_pairs={{0,2},{1,3},{2,0},{3,1},{4,6},{5,7},{6,4},{7,5},{8,10},{9,11},{10,... | collective-permute-start | bytes 393224 | tf_op jit(solution)/shard_map/banks_expert2/ppermute | solution.py:365
  11.5 10.3 %collective-permute-start.5 = (bf16[2,256,128]{2,1,0:T(8,128)(2,1)}, bf16[2,256,128]{2,1,0:T(8,128)(2,1)S(1)}, u32[]{:S(2)}, u32[]{:S(2)}) collective-permute-start(bf16[2,256,128]{2,1,0:T(8,128)(2,1)} %get-tuple-element.55.refs_0_.refs_5_), channel_id=1, source_target_pairs={{0,1},{1,0},{2,3},{3,2},{4,5},{5,4},{6,7},{7,6},{8,9},{9,8},{10,11... | collective-permute-start | bytes 393224 | tf_op jit(solution)/shard_map/banks_expert1/ppermute | solution.py:365
  14.2 7.7 %copy-start.1 = (bf16[2,256,128]{2,1,0:T(8,128)(2,1)S(1)}, bf16[2,256,128]{2,1,0:T(8,128)(2,1)}, u32[]{:S(2)}) copy-start(bf16[2,256,128]{2,1,0:T(8,128)(2,1)} %get-tuple-element.55.refs_0_.refs_5_) | copy-start | bytes 393220
  14.2 9.1 %collective-permute-start.10 = (bf16[2,256,128]{2,1,0:T(8,128)(2,1)S(1)}, bf16[2,256,128]{2,1,0:T(8,128)(2,1)S(1)}, u32[]{:S(2)}, u32[]{:S(2)}) collective-permute-start(bf16[2,256,128]{2,1,0:T(8,128)(2,1)S(1)} %shard_map.138.refs_0_.refs_6_), channel_id=1, source_target_pairs={{0,3},{1,2},{2,1},{3,0},{4,7},{5,6},{6,5},{7,4},{8,11},{9,10},{10,... | collective-permute-start | bytes 393224 | tf_op jit(solution)/shard_map/other_banks_expert3/ppermute | solution.py:365
  16.7 7.1 %collective-permute-start.9 = (bf16[2,256,128]{2,1,0:T(8,128)(2,1)S(1)}, bf16[2,256,128]{2,1,0:T(8,128)(2,1)S(1)}, u32[]{:S(2)}, u32[]{:S(2)}) collective-permute-start(bf16[2,256,128]{2,1,0:T(8,128)(2,1)S(1)} %shard_map.138.refs_0_.refs_6_), channel_id=1, source_target_pairs={{0,2},{1,3},{2,0},{3,1},{4,6},{5,7},{6,4},{7,5},{8,10},{9,11},{10,... | collective-permute-start | bytes 393224 | tf_op jit(solution)/shard_map/other_banks_expert2/ppermute | solution.py:365
  18.5 5.9 %collective-permute-start.8 = (bf16[2,256,128]{2,1,0:T(8,128)(2,1)S(1)}, bf16[2,256,128]{2,1,0:T(8,128)(2,1)S(1)}, u32[]{:S(2)}, u32[]{:S(2)}) collective-permute-start(bf16[2,256,128]{2,1,0:T(8,128)(2,1)S(1)} %shard_map.138.refs_0_.refs_6_), channel_id=1, source_target_pairs={{0,1},{1,0},{2,3},{3,2},{4,5},{5,4},{6,7},{7,6},{8,9},{9,8},{10,11... | collective-permute-start | bytes 393224 | tf_op jit(solution)/shard_map/other_banks_expert1/ppermute | solution.py:365
  21.8 4.0 %collective-permute-start.4 = (bf16[128,128]{1,0:T(8,128)(2,1)S(1)}, bf16[128,128]{1,0:T(8,128)(2,1)S(1)}, u32[]{:S(2)}, u32[]{:S(2)}) collective-permute-start(bf16[128,128]{1,0:T(8,128)(2,1)S(1)} %get-tuple-element.58.weights_ref), channel_id=1, source_target_pairs={{0,8},{4,12},{8,0},{12,4},{16,24},{20,28},{24,16},{28,20},{1,9},{5... | collective-permute-start | bytes 98312 | tf_op jit(solution)/shard_map/weights_dp2/ppermute | solution.py:361
  23.2 2.6 %collective-permute-start.2 = (bf16[128,1152]{1,0:T(8,128)(2,1)S(1)}, bf16[128,1152]{1,0:T(8,128)(2,1)S(1)}, u32[]{:S(2)}, u32[]{:S(2)}) collective-permute-start(bf16[128,1152]{1,0:T(8,128)(2,1)S(1)} %copy-done.6), channel_id=1, source_target_pairs={{0,4},{4,0},{8,12},{12,8},{16,20},{20,16},{24,28},{28,24},{1,5},{5... | collective-permute-start | bytes 884744 | tf_op jit(solution)/shard_map/rows_dp1/ppermute | solution.py:361
  23.3 2.5 %collective-permute-start.3 = (bf16[128,1152]{1,0:T(8,128)(2,1)S(1)}, bf16[128,1152]{1,0:T(8,128)(2,1)S(1)}, u32[]{:S(2)}, u32[]{:S(2)}) collective-permute-start(bf16[128,1152]{1,0:T(8,128)(2,1)S(1)} %shard_map.139), channel_id=1, source_target_pairs={{0,4},{4,0},{8,12},{12,8},{16,20},{20,16},{24,28},{28,24},{1,5},{5... | collective-permute-start | bytes 884744 | tf_op jit(solution)/shard_map/far_rows_dp1/ppermute | solution.py:361
  26.7 1.4 %collective-permute-start.11 = (bf16[256,256]{1,0:T(8,128)(2,1)S(1)}, bf16[256,256]{1,0:T(8,128)(2,1)S(1)}, u32[]{:S(2)}, u32[]{:S(2)}) collective-permute-start(bf16[256,256]{1,0:T(8,128)(2,1)S(1)} %get-tuple-element.62), channel_id=1, source_target_pairs={{0,4},{4,0},{8,12},{12,8},{16,20},{20,16},{24,28},{28,24},{1,5},{5... | collective-permute-start | bytes 393224 | tf_op jit(solution)/shard_map/partials_dp1/ppermute | solution.py:361
  28.1 5.6 %collective-permute-start.12 = (bf16[256,256]{1,0:T(8,128)(2,1)S(1)}, bf16[256,256]{1,0:T(8,128)(2,1)S(1)}, u32[]{:S(2)}, u32[]{:S(2)}) collective-permute-start(bf16[256,256]{1,0:T(8,128)(2,1)S(1)} %get-tuple-element.63), channel_id=1, source_target_pairs={{0,8},{4,12},{8,0},{12,4},{16,24},{20,28},{24,16},{28,20},{1,9},{5... | collective-permute-start | bytes 393224 | tf_op jit(solution)/shard_map/partials_dp2/ppermute | solution.py:361
  33.9 1.4 %collective-permute-start.13 = (bf16[256,256]{1,0:T(8,128)(2,1)S(1)}, bf16[256,256]{1,0:T(8,128)(2,1)S(1)}, u32[]{:S(2)}, u32[]{:S(2)}) collective-permute-start(bf16[256,256]{1,0:T(8,128)(2,1)S(1)} %get-tuple-element.72.refs_5_), channel_id=1, source_target_pairs={{0,4},{4,0},{8,12},{12,8},{16,20},{20,16},{24,28},{28,24},{1,5},{5... | collective-permute-start | bytes 393224 | tf_op jit(solution)/shard_map/head_rows_dp1/ppermute | solution.py:361
  36.6 3.7 %collective-permute-start.14 = (bf16[256,640]{1,0:T(8,128)(2,1)S(1)}, bf16[256,640]{1,0:T(8,128)(2,1)S(1)}, u32[]{:S(2)}, u32[]{:S(2)}) collective-permute-start(bf16[256,640]{1,0:T(8,128)(2,1)S(1)} %get-tuple-element.74), channel_id=1, source_target_pairs={{0,4},{4,0},{8,12},{12,8},{16,20},{20,16},{24,28},{28,24},{1,5},{5... | collective-permute-start | bytes 983048 | tf_op jit(solution)/shard_map/token_back_dp1/ppermute | solution.py:361
  36.9 6.4 %collective-permute-start.19 = (bf16[2,256,128]{2,1,0:T(8,128)(2,1)S(1)}, bf16[2,256,128]{2,1,0:T(8,128)(2,1)S(1)}, u32[]{:S(2)}, u32[]{:S(2)}) collective-permute-start(bf16[2,256,128]{2,1,0:T(8,128)(2,1)S(1)} %get-tuple-element.83), channel_id=1, source_target_pairs={{0,1},{1,0},{2,3},{3,2},{4,5},{5,4},{6,7},{7,6},{8,9},{9,8},{10,11... | collective-permute-start | bytes 393224 | tf_op jit(solution)/shard_map/grads_expert1/ppermute | solution.py:365
  37.9 8.0 %collective-permute-start.20 = (bf16[2,256,128]{2,1,0:T(8,128)(2,1)S(1)}, bf16[2,256,128]{2,1,0:T(8,128)(2,1)S(1)}, u32[]{:S(2)}, u32[]{:S(2)}) collective-permute-start(bf16[2,256,128]{2,1,0:T(8,128)(2,1)S(1)} %get-tuple-element.84), channel_id=1, source_target_pairs={{0,2},{1,3},{2,0},{3,1},{4,6},{5,7},{6,4},{7,5},{8,10},{9,11},{10,... | collective-permute-start | bytes 393224 | tf_op jit(solution)/shard_map/grads_expert2/ppermute | solution.py:365
  39.4 8.2 %collective-permute-start.21 = (bf16[2,256,128]{2,1,0:T(8,128)(2,1)S(1)}, bf16[2,256,128]{2,1,0:T(8,128)(2,1)S(1)}, u32[]{:S(2)}, u32[]{:S(2)}) collective-permute-start(bf16[2,256,128]{2,1,0:T(8,128)(2,1)S(1)} %get-tuple-element.85), channel_id=1, source_target_pairs={{0,3},{1,2},{2,1},{3,0},{4,7},{5,6},{6,5},{7,4},{8,11},{9,10},{10,... | collective-permute-start | bytes 393224 | tf_op jit(solution)/shard_map/grads_expert3/ppermute | solution.py:365
  40.8 9.4 %collective-permute-start.15 = (bf16[128,1152]{1,0:T(8,128)(2,1)S(1)}, bf16[128,1152]{1,0:T(8,128)(2,1)S(1)}, u32[]{:S(2)}, u32[]{:S(2)}) collective-permute-start(bf16[128,1152]{1,0:T(8,128)(2,1)S(1)} %get-tuple-element.76), channel_id=1, source_target_pairs={{0,8},{4,12},{8,0},{12,4},{16,24},{20,28},{24,16},{28,20},{1,9},{5... | collective-permute-start | bytes 884744 | tf_op jit(solution)/shard_map/token_back_dp2/ppermute | solution.py:361
  41.8 10.7 %collective-permute-start.16 = (bf16[2,256,128]{2,1,0:T(8,128)(2,1)S(1)}, bf16[2,256,128]{2,1,0:T(8,128)(2,1)S(1)}, u32[]{:S(2)}, u32[]{:S(2)}) collective-permute-start(bf16[2,256,128]{2,1,0:T(8,128)(2,1)S(1)} %get-tuple-element.79), channel_id=1, source_target_pairs={{0,1},{1,0},{2,3},{3,2},{4,5},{5,4},{6,7},{7,6},{8,9},{9,8},{10,11... | collective-permute-start | bytes 393224 | tf_op jit(solution)/shard_map/grads_expert1/ppermute | solution.py:365
  43.3 9.2 %collective-permute-start.17 = (bf16[2,256,128]{2,1,0:T(8,128)(2,1)S(1)}, bf16[2,256,128]{2,1,0:T(8,128)(2,1)S(1)}, u32[]{:S(2)}, u32[]{:S(2)}) collective-permute-start(bf16[2,256,128]{2,1,0:T(8,128)(2,1)S(1)} %get-tuple-element.80), channel_id=1, source_target_pairs={{0,2},{1,3},{2,0},{3,1},{4,6},{5,7},{6,4},{7,5},{8,10},{9,11},{10,... | collective-permute-start | bytes 393224 | tf_op jit(solution)/shard_map/grads_expert2/ppermute | solution.py:365
  45.9 6.6 %collective-permute-start.18 = (bf16[2,256,128]{2,1,0:T(8,128)(2,1)S(1)}, bf16[2,256,128]{2,1,0:T(8,128)(2,1)S(1)}, u32[]{:S(2)}, u32[]{:S(2)}) collective-permute-start(bf16[2,256,128]{2,1,0:T(8,128)(2,1)S(1)} %get-tuple-element.81), channel_id=1, source_target_pairs={{0,3},{1,2},{2,1},{3,0},{4,7},{5,6},{6,5},{7,4},{8,11},{9,10},{10,... | collective-permute-start | bytes 393224 | tf_op jit(solution)/shard_map/grads_expert3/ppermute | solution.py:365
  47.7 7.3 %collective-permute-start.22 = (bf16[2,256,128]{2,1,0:T(8,128)(2,1)S(1)}, bf16[2,256,128]{2,1,0:T(8,128)(2,1)S(1)}, u32[]{:S(2)}, u32[]{:S(2)}) collective-permute-start(bf16[2,256,128]{2,1,0:T(8,128)(2,1)S(1)} %shard_map.153), channel_id=1, source_target_pairs={{0,16},{4,20},{8,24},{12,28},{16,0},{20,4},{24,8},{28,12},{1,17},{... | collective-permute-start | bytes 393224 | tf_op jit(solution)/shard_map/grads_dp4/ppermute | solution.py:361
  (6 other events, 20.1 us)

commit v7 on v6

--- a/solution.py
+++ b/solution.py
@@ -320,7 +320,7 @@
     total = refs[0][...]
     for ref in refs[1:-2]:
         total += ref[...].astype(F32)
-    total = total / groups
+    total = total * (1.0 / groups)
     for side in range(2):
         refs[side - 2][0] = total[side]
 

time: 56 us -> 56 us (level)
  no operation moved by 1% of the time
where the time goes in v7:
time: 56 us; the launch traced here: 55.8 us
  starting transfers between devices  27.8 us (50%)
  waiting for transfers between devices  13.7 us (24%)
  Pallas kernels  12.7 us (23%)
  between operations  0.86 us (2%)
  local copies, waits for them, and re-layouts  0.71 us (1%)
    ppermute x12, starting transfers between devices, over_experts(): return lax.ppermute(x, 'expert', [(i, i ^ flip) for i in range(experts)])  17.8 us
    pallas_call x20, Pallas kernels, kernel_call(): pl.pallas_call(body, out_shape=[jax.ShapeDtypeStruct(s, t) for s, t in ou...  12.7 us
    ppermute x11, waiting for transfers between devices, over_dp(): return lax.ppermute(x, 'dp', [(i, i ^ flip) for i in range(groups)])  10.9 us
    ppermute x11, starting transfers between devices, over_dp(): return lax.ppermute(x, 'dp', [(i, i ^ flip) for i in range(groups)])  10 us
    ppermute x12, waiting for transfers between devices, over_experts(): return lax.ppermute(x, 'expert', [(i, i ^ flip) for i in range(experts)])  2.85 us
  transfers between devices with their start and end apart: 23, of which 9 were waited for; matrix products, arithmetic and copies ran while one was open for 0% of the time, Pallas kernels for 13%

profile of v7, /device:TPU:0, one launch (start us, length us, event | category | flops | bytes accessed | tf_op | source)
XLA Modules:
  0.0 55.8 jit_solution(9803400187843560894)
XLA Ops:
  0.6 2.2 %shard_map.137 = (bf16[2,256,128]{2,1,0:T(8,128)(2,1)}, bf16[128,2176]{1,0:T(8,128)(2,1)}) custom-call(s32[1]{0:T(128)} %bitcast.refs_0_, s32[1]{0:T(128)} %bitcast.1.refs_1_, bf16[128,2048]{1,0:T(8,128)(2,1)} %refs_2_.3, bf16[128,2048]{1,0:T(8,128)(2,1)} %refs_3_.3, bf16[1,256,128]{2,1,0:T(8,128)(2,1)} %refs_4_.1, bf16[1,256,128]{2,1,0:T(8,128)(2,1)} %refs_5_.1, ...), custom_call_target="tpu_custom_call" | custom-call | bytes 1873928 | tf_op jit(solution)/shard_map/pallas_call | solution.py:16
  2.8 4.1 %collective-permute-start.1 = (bf16[2,256,128]{2,1,0:T(8,128)(2,1)}, bf16[2,256,128]{2,1,0:T(8,128)(2,1)S(1)}, u32[]{:S(2)}, u32[]{:S(2)}) collective-permute-start(bf16[2,256,128]{2,1,0:T(8,128)(2,1)} %get-tuple-element.55.refs_0_.refs_5_), channel_id=1, source_target_pairs={{0,16},{4,20},{8,24},{12,28},{16,0},{20,4},{24,8},{28,12},{1,17},{... | collective-permute-start | bytes 393224 | tf_op jit(solution)/shard_map/banks_dp4/ppermute | solution.py:361
  6.9 1.6 %collective-permute-start = (bf16[128,2176]{1,0:T(8,128)(2,1)}, bf16[128,2176]{1,0:T(8,128)(2,1)S(1)}, u32[]{:S(2)}, u32[]{:S(2)}) collective-permute-start(bf16[128,2176]{1,0:T(8,128)(2,1)} %get-tuple-element.54), channel_id=1, source_target_pairs={{0,8},{4,12},{8,0},{12,4},{16,24},{20,28},{24,16},{28,20},{1,9},{5... | collective-permute-start | bytes 1671176 | tf_op jit(solution)/shard_map/rows_dp2/ppermute | solution.py:361
  8.5 2.4 %collective-permute-start.7 = (bf16[2,256,128]{2,1,0:T(8,128)(2,1)}, bf16[2,256,128]{2,1,0:T(8,128)(2,1)S(1)}, u32[]{:S(2)}, u32[]{:S(2)}) collective-permute-start(bf16[2,256,128]{2,1,0:T(8,128)(2,1)} %get-tuple-element.55.refs_0_.refs_5_), channel_id=1, source_target_pairs={{0,3},{1,2},{2,1},{3,0},{4,7},{5,6},{6,5},{7,4},{8,11},{9,10},{10,... | collective-permute-start | bytes 393224 | tf_op jit(solution)/shard_map/banks_expert3/ppermute | solution.py:365
  12.0 2.1 %shard_map.136 = (bf16[128,1152]{1,0:T(8,128)(2,1)}, bf16[128,1152]{1,0:T(8,128)(2,1)}) custom-call(s32[1]{0:T(128)} %bitcast.refs_0_, s32[1]{0:T(128)} %bitcast.1.refs_1_, bf16[128,2048]{1,0:T(8,128)(2,1)} %refs_2_.3, bf16[128,2048]{1,0:T(8,128)(2,1)} %refs_3_.3, f32[8,128]{1,0:T(8,128)} %bitcast.13, s32[2,128]{1,0:T(2,128)} %bitcast.7, s32[2,128]{1,0:T(2,128)} %bitcast.10), custom_call_target="tpu_custom_call" | custom-call | bytes 1644552 | tf_op jit(solution)/shard_map/pallas_call | solution.py:16
  14.2 2.5 %collective-permute-start.10 = (bf16[2,256,128]{2,1,0:T(8,128)(2,1)S(1)}, bf16[2,256,128]{2,1,0:T(8,128)(2,1)S(1)}, u32[]{:S(2)}, u32[]{:S(2)}) collective-permute-start(bf16[2,256,128]{2,1,0:T(8,128)(2,1)S(1)} %shard_map.138.refs_0_.refs_6_), channel_id=1, source_target_pairs={{0,3},{1,2},{2,1},{3,0},{4,7},{5,6},{6,5},{7,4},{8,11},{9,10},{10,... | collective-permute-start | bytes 393224 | tf_op jit(solution)/shard_map/other_banks_expert3/ppermute | solution.py:365
  17.3 1.2 %collective-permute-done.6.refs_2_.refs_9_ = bf16[2,256,128]{2,1,0:T(8,128)(2,1)S(1)} collective-permute-done((bf16[2,256,128]{2,1,0:T(8,128)(2,1)}, bf16[2,256,128]{2,1,0:T(8,128)(2,1)S(1)}, u32[]{:S(2)}, u32[]{:S(2)}) %collective-permute-start.6) | collective-permute-done | bytes 131104 | tf_op jit(solution)/shard_map/banks_expert2/ppermute | solution.py:365
  18.5 2.9 %collective-permute-start.8 = (bf16[2,256,128]{2,1,0:T(8,128)(2,1)S(1)}, bf16[2,256,128]{2,1,0:T(8,128)(2,1)S(1)}, u32[]{:S(2)}, u32[]{:S(2)}) collective-permute-start(bf16[2,256,128]{2,1,0:T(8,128)(2,1)S(1)} %shard_map.138.refs_0_.refs_6_), channel_id=1, source_target_pairs={{0,1},{1,0},{2,3},{3,2},{4,5},{5,4},{6,7},{7,6},{8,9},{9,8},{10,11... | collective-permute-start | bytes 393224 | tf_op jit(solution)/shard_map/other_banks_expert1/ppermute | solution.py:365
  22.0 1.2 %collective-permute-done.in_ref.refs_1_ = bf16[128,2176]{1,0:T(8,128)(2,1)S(1)} collective-permute-done((bf16[128,2176]{1,0:T(8,128)(2,1)}, bf16[128,2176]{1,0:T(8,128)(2,1)S(1)}, u32[]{:S(2)}, u32[]{:S(2)}) %collective-permute-start) | collective-permute-done | bytes 557088 | tf_op jit(solution)/shard_map/rows_dp2/ppermute | solution.py:361
  24.5 1.3 %collective-permute-done.4.refs_4_.far_weights_ref = bf16[128,128]{1,0:T(8,128)(2,1)S(1)} collective-permute-done((bf16[128,128]{1,0:T(8,128)(2,1)S(1)}, bf16[128,128]{1,0:T(8,128)(2,1)S(1)}, u32[]{:S(2)}, u32[]{:S(2)}) %collective-permute-start.4) | collective-permute-done | bytes 32800 | tf_op jit(solution)/shard_map/weights_dp2/ppermute | solution.py:361
  26.7 1.3 %collective-permute-done.11.got_ref = bf16[256,256]{1,0:T(8,128)(2,1)S(1)} collective-permute-done((bf16[256,256]{1,0:T(8,128)(2,1)S(1)}, bf16[256,256]{1,0:T(8,128)(2,1)S(1)}, u32[]{:S(2)}, u32[]{:S(2)}) %collective-permute-start.11) | collective-permute-done | bytes 131104 | tf_op jit(solution)/shard_map/partials_dp1/ppermute | solution.py:361
  29.4 1.2 %shard_map.147.refs_4_ = bf16[512,512]{1,0:T(8,128)(2,1)S(1)} custom-call(bf16[128,1152]{1,0:T(8,128)(2,1)S(1)} %copy-done, bf16[128,2176]{1,0:T(8,128)(2,1)S(1)} %collective-permute-done.in_ref.refs_1_, bf16[128,1152]{1,0:T(8,128)(2,1)S(1)} %collective-permute-done.2.refs_2_, bf16[128,1152]{1,0:T(8,128)(2,1)S(1)} %collective-permute-done.3.refs_3_, ...), custom_call_target="tpu_custom_call" | custom-call | flops 536870912 | bytes 3276800 | tf_op jit(solution)/shard_map/pallas_call | solution.py:16
  30.6 3.1 %collective-permute-done.12.got_ref = bf16[256,256]{1,0:T(8,128)(2,1)S(1)} collective-permute-done((bf16[256,256]{1,0:T(8,128)(2,1)S(1)}, bf16[256,256]{1,0:T(8,128)(2,1)S(1)}, u32[]{:S(2)}, u32[]{:S(2)}) %collective-permute-start.12) | collective-permute-done | bytes 131104 | tf_op jit(solution)/shard_map/partials_dp2/ppermute | solution.py:361
  34.0 1.3 %collective-permute-done.13.refs_6_ = bf16[256,256]{1,0:T(8,128)(2,1)S(1)} collective-permute-done((bf16[256,256]{1,0:T(8,128)(2,1)S(1)}, bf16[256,256]{1,0:T(8,128)(2,1)S(1)}, u32[]{:S(2)}, u32[]{:S(2)}) %collective-permute-start.13) | collective-permute-done | bytes 131104 | tf_op jit(solution)/shard_map/head_rows_dp1/ppermute | solution.py:361
  35.3 1.3 %shard_map.149 = (f32[2,256,128]{2,1,0:T(8,128)S(1)}, f32[2,256,128]{2,1,0:T(8,128)S(1)}, bf16[2,256,128]{2,1,0:T(8,128)(2,1)S(1)}, bf16[2,256,128]{2,1,0:T(8,12...) custom-call(bf16[1024,512]{1,0:T(8,128)(2,1)S(1)} %shard_map.146.ref, ...), custom_call_target="tpu_custom_call" | custom-call | flops 805306368 | bytes 4587520 | tf_op jit(solution)/shard_map/pallas_call | solution.py:16
  36.9 1.0 %collective-permute-start.19 = (bf16[2,256,128]{2,1,0:T(8,128)(2,1)S(1)}, bf16[2,256,128]{2,1,0:T(8,128)(2,1)S(1)}, u32[]{:S(2)}, u32[]{:S(2)}) collective-permute-start(bf16[2,256,128]{2,1,0:T(8,128)(2,1)S(1)} %get-tuple-element.83), channel_id=1, source_target_pairs={{0,1},{1,0},{2,3},{3,2},{4,5},{5,4},{6,7},{7,6},{8,9},{9,8},{10,11... | collective-permute-start | bytes 393224 | tf_op jit(solution)/shard_map/grads_expert1/ppermute | solution.py:365
  37.9 1.5 %collective-permute-start.20 = (bf16[2,256,128]{2,1,0:T(8,128)(2,1)S(1)}, bf16[2,256,128]{2,1,0:T(8,128)(2,1)S(1)}, u32[]{:S(2)}, u32[]{:S(2)}) collective-permute-start(bf16[2,256,128]{2,1,0:T(8,128)(2,1)S(1)} %get-tuple-element.84), channel_id=1, source_target_pairs={{0,2},{1,3},{2,0},{3,1},{4,6},{5,7},{6,4},{7,5},{8,10},{9,11},{10,... | collective-permute-start | bytes 393224 | tf_op jit(solution)/shard_map/grads_expert2/ppermute | solution.py:365
  41.8 1.5 %collective-permute-start.16 = (bf16[2,256,128]{2,1,0:T(8,128)(2,1)S(1)}, bf16[2,256,128]{2,1,0:T(8,128)(2,1)S(1)}, u32[]{:S(2)}, u32[]{:S(2)}) collective-permute-start(bf16[2,256,128]{2,1,0:T(8,128)(2,1)S(1)} %get-tuple-element.79), channel_id=1, source_target_pairs={{0,1},{1,0},{2,3},{3,2},{4,5},{5,4},{6,7},{7,6},{8,9},{9,8},{10,11... | collective-permute-start | bytes 393224 | tf_op jit(solution)/shard_map/grads_expert1/ppermute | solution.py:365
  43.3 1.5 %collective-permute-start.17 = (bf16[2,256,128]{2,1,0:T(8,128)(2,1)S(1)}, bf16[2,256,128]{2,1,0:T(8,128)(2,1)S(1)}, u32[]{:S(2)}, u32[]{:S(2)}) collective-permute-start(bf16[2,256,128]{2,1,0:T(8,128)(2,1)S(1)} %get-tuple-element.80), channel_id=1, source_target_pairs={{0,2},{1,3},{2,0},{3,1},{4,6},{5,7},{6,4},{7,5},{8,10},{9,11},{10,... | collective-permute-start | bytes 393224 | tf_op jit(solution)/shard_map/grads_expert2/ppermute | solution.py:365
  44.8 1.1 %collective-permute-done.20.refs_2_ = bf16[2,256,128]{2,1,0:T(8,128)(2,1)S(1)} collective-permute-done((bf16[2,256,128]{2,1,0:T(8,128)(2,1)S(1)}, bf16[2,256,128]{2,1,0:T(8,128)(2,1)S(1)}, u32[]{:S(2)}, u32[]{:S(2)}) %collective-permute-start.20) | collective-permute-done | bytes 131104 | tf_op jit(solution)/shard_map/grads_expert2/ppermute | solution.py:365
  45.9 1.8 %collective-permute-start.18 = (bf16[2,256,128]{2,1,0:T(8,128)(2,1)S(1)}, bf16[2,256,128]{2,1,0:T(8,128)(2,1)S(1)}, u32[]{:S(2)}, u32[]{:S(2)}) collective-permute-start(bf16[2,256,128]{2,1,0:T(8,128)(2,1)S(1)} %get-tuple-element.81), channel_id=1, source_target_pairs={{0,3},{1,2},{2,1},{3,0},{4,7},{5,6},{6,5},{7,4},{8,11},{9,10},{10,... | collective-permute-start | bytes 393224 | tf_op jit(solution)/shard_map/grads_expert3/ppermute | solution.py:365
  47.7 1.4 %collective-permute-start.22 = (bf16[2,256,128]{2,1,0:T(8,128)(2,1)S(1)}, bf16[2,256,128]{2,1,0:T(8,128)(2,1)S(1)}, u32[]{:S(2)}, u32[]{:S(2)}) collective-permute-start(bf16[2,256,128]{2,1,0:T(8,128)(2,1)S(1)} %shard_map.153), channel_id=1, source_target_pairs={{0,16},{4,20},{8,24},{12,28},{16,0},{20,4},{24,8},{28,12},{1,17},{... | collective-permute-start | bytes 393224 | tf_op jit(solution)/shard_map/grads_dp4/ppermute | solution.py:361
  49.1 1.1 %shard_map.154 = (bf16[128,128]{1,0:T(8,128)(2,1)}, bf16[128,128]{1,0:T(8,128)(2,1)}) custom-call(f32[128,128]{1,0:T(8,128)S(1)} %get-tuple-element.87.probs_ref, bf16[128,128]{1,0:T(8,128)(2,1)S(1)} %copy-done.2, bf16[128,128]{1,0:T(8,128)(2,1)S(1)} %copy-done.3, bf16[128,128]{1,0:T(8,128)(2,1)S(1)} %get-tuple-element.88.mixed_ref, ...), custom_call_target="tpu_custom_call" | custom-call | bytes 262144 | tf_op jit(solution)/shard_map/pallas_call | solution.py:16
  52.5 2.6 %collective-permute-done.22.refs_4_ = bf16[2,256,128]{2,1,0:T(8,128)(2,1)S(1)} collective-permute-done((bf16[2,256,128]{2,1,0:T(8,128)(2,1)S(1)}, bf16[2,256,128]{2,1,0:T(8,128)(2,1)S(1)}, u32[]{:S(2)}, u32[]{:S(2)}) %collective-permute-start.22) | collective-permute-done | bytes 131104 | tf_op jit(solution)/shard_map/grads_dp4/ppermute | solution.py:361
  (56 shorter events, 11.6 us)
Async XLA Ops:
  2.8 11.3 %collective-permute-start.1 = (bf16[2,256,128]{2,1,0:T(8,128)(2,1)}, bf16[2,256,128]{2,1,0:T(8,128)(2,1)S(1)}, u32[]{:S(2)}, u32[]{:S(2)}) collective-permute-start(bf16[2,256,128]{2,1,0:T(8,128)(2,1)} %get-tuple-element.55.refs_0_.refs_5_), channel_id=1, source_target_pairs={{0,16},{4,20},{8,24},{12,28},{16,0},{20,4},{24,8},{28,12},{1,17},{... | collective-permute-start | bytes 393224 | tf_op jit(solution)/shard_map/banks_dp4/ppermute | solution.py:361
  6.9 16.3 %collective-permute-start = (bf16[128,2176]{1,0:T(8,128)(2,1)}, bf16[128,2176]{1,0:T(8,128)(2,1)S(1)}, u32[]{:S(2)}, u32[]{:S(2)}) collective-permute-start(bf16[128,2176]{1,0:T(8,128)(2,1)} %get-tuple-element.54), channel_id=1, source_target_pairs={{0,8},{4,12},{8,0},{12,4},{16,24},{20,28},{24,16},{28,20},{1,9},{5... | collective-permute-start | bytes 1671176 | tf_op jit(solution)/shard_map/rows_dp2/ppermute | solution.py:361
  8.5 8.2 %collective-permute-start.7 = (bf16[2,256,128]{2,1,0:T(8,128)(2,1)}, bf16[2,256,128]{2,1,0:T(8,128)(2,1)S(1)}, u32[]{:S(2)}, u32[]{:S(2)}) collective-permute-start(bf16[2,256,128]{2,1,0:T(8,128)(2,1)} %get-tuple-element.55.refs_0_.refs_5_), channel_id=1, source_target_pairs={{0,3},{1,2},{2,1},{3,0},{4,7},{5,6},{6,5},{7,4},{8,11},{9,10},{10,... | collective-permute-start | bytes 393224 | tf_op jit(solution)/shard_map/banks_expert3/ppermute | solution.py:365
  11.0 7.6 %collective-permute-start.6 = (bf16[2,256,128]{2,1,0:T(8,128)(2,1)}, bf16[2,256,128]{2,1,0:T(8,128)(2,1)S(1)}, u32[]{:S(2)}, u32[]{:S(2)}) collective-permute-start(bf16[2,256,128]{2,1,0:T(8,128)(2,1)} %get-tuple-element.55.refs_0_.refs_5_), channel_id=1, source_target_pairs={{0,2},{1,3},{2,0},{3,1},{4,6},{5,7},{6,4},{7,5},{8,10},{9,11},{10,... | collective-permute-start | bytes 393224 | tf_op jit(solution)/shard_map/banks_expert2/ppermute | solution.py:365
  11.5 10.3 %collective-permute-start.5 = (bf16[2,256,128]{2,1,0:T(8,128)(2,1)}, bf16[2,256,128]{2,1,0:T(8,128)(2,1)S(1)}, u32[]{:S(2)}, u32[]{:S(2)}) collective-permute-start(bf16[2,256,128]{2,1,0:T(8,128)(2,1)} %get-tuple-element.55.refs_0_.refs_5_), channel_id=1, source_target_pairs={{0,1},{1,0},{2,3},{3,2},{4,5},{5,4},{6,7},{7,6},{8,9},{9,8},{10,11... | collective-permute-start | bytes 393224 | tf_op jit(solution)/shard_map/banks_expert1/ppermute | solution.py:365
  14.2 7.7 %copy-start.1 = (bf16[2,256,128]{2,1,0:T(8,128)(2,1)S(1)}, bf16[2,256,128]{2,1,0:T(8,128)(2,1)}, u32[]{:S(2)}) copy-start(bf16[2,256,128]{2,1,0:T(8,128)(2,1)} %get-tuple-element.55.refs_0_.refs_5_) | copy-start | bytes 393220
  14.2 9.1 %collective-permute-start.10 = (bf16[2,256,128]{2,1,0:T(8,128)(2,1)S(1)}, bf16[2,256,128]{2,1,0:T(8,128)(2,1)S(1)}, u32[]{:S(2)}, u32[]{:S(2)}) collective-permute-start(bf16[2,256,128]{2,1,0:T(8,128)(2,1)S(1)} %shard_map.138.refs_0_.refs_6_), channel_id=1, source_target_pairs={{0,3},{1,2},{2,1},{3,0},{4,7},{5,6},{6,5},{7,4},{8,11},{9,10},{10,... | collective-permute-start | bytes 393224 | tf_op jit(solution)/shard_map/other_banks_expert3/ppermute | solution.py:365
  16.7 7.1 %collective-permute-start.9 = (bf16[2,256,128]{2,1,0:T(8,128)(2,1)S(1)}, bf16[2,256,128]{2,1,0:T(8,128)(2,1)S(1)}, u32[]{:S(2)}, u32[]{:S(2)}) collective-permute-start(bf16[2,256,128]{2,1,0:T(8,128)(2,1)S(1)} %shard_map.138.refs_0_.refs_6_), channel_id=1, source_target_pairs={{0,2},{1,3},{2,0},{3,1},{4,6},{5,7},{6,4},{7,5},{8,10},{9,11},{10,... | collective-permute-start | bytes 393224 | tf_op jit(solution)/shard_map/other_banks_expert2/ppermute | solution.py:365
  18.5 5.9 %collective-permute-start.8 = (bf16[2,256,128]{2,1,0:T(8,128)(2,1)S(1)}, bf16[2,256,128]{2,1,0:T(8,128)(2,1)S(1)}, u32[]{:S(2)}, u32[]{:S(2)}) collective-permute-start(bf16[2,256,128]{2,1,0:T(8,128)(2,1)S(1)} %shard_map.138.refs_0_.refs_6_), channel_id=1, source_target_pairs={{0,1},{1,0},{2,3},{3,2},{4,5},{5,4},{6,7},{7,6},{8,9},{9,8},{10,11... | collective-permute-start | bytes 393224 | tf_op jit(solution)/shard_map/other_banks_expert1/ppermute | solution.py:365
  21.8 4.0 %collective-permute-start.4 = (bf16[128,128]{1,0:T(8,128)(2,1)S(1)}, bf16[128,128]{1,0:T(8,128)(2,1)S(1)}, u32[]{:S(2)}, u32[]{:S(2)}) collective-permute-start(bf16[128,128]{1,0:T(8,128)(2,1)S(1)} %get-tuple-element.58.weights_ref), channel_id=1, source_target_pairs={{0,8},{4,12},{8,0},{12,4},{16,24},{20,28},{24,16},{28,20},{1,9},{5... | collective-permute-start | bytes 98312 | tf_op jit(solution)/shard_map/weights_dp2/ppermute | solution.py:361
  23.2 2.6 %collective-permute-start.2 = (bf16[128,1152]{1,0:T(8,128)(2,1)S(1)}, bf16[128,1152]{1,0:T(8,128)(2,1)S(1)}, u32[]{:S(2)}, u32[]{:S(2)}) collective-permute-start(bf16[128,1152]{1,0:T(8,128)(2,1)S(1)} %copy-done.6), channel_id=1, source_target_pairs={{0,4},{4,0},{8,12},{12,8},{16,20},{20,16},{24,28},{28,24},{1,5},{5... | collective-permute-start | bytes 884744 | tf_op jit(solution)/shard_map/rows_dp1/ppermute | solution.py:361
  23.3 2.5 %collective-permute-start.3 = (bf16[128,1152]{1,0:T(8,128)(2,1)S(1)}, bf16[128,1152]{1,0:T(8,128)(2,1)S(1)}, u32[]{:S(2)}, u32[]{:S(2)}) collective-permute-start(bf16[128,1152]{1,0:T(8,128)(2,1)S(1)} %shard_map.139), channel_id=1, source_target_pairs={{0,4},{4,0},{8,12},{12,8},{16,20},{20,16},{24,28},{28,24},{1,5},{5... | collective-permute-start | bytes 884744 | tf_op jit(solution)/shard_map/far_rows_dp1/ppermute | solution.py:361
  26.7 1.4 %collective-permute-start.11 = (bf16[256,256]{1,0:T(8,128)(2,1)S(1)}, bf16[256,256]{1,0:T(8,128)(2,1)S(1)}, u32[]{:S(2)}, u32[]{:S(2)}) collective-permute-start(bf16[256,256]{1,0:T(8,128)(2,1)S(1)} %get-tuple-element.62), channel_id=1, source_target_pairs={{0,4},{4,0},{8,12},{12,8},{16,20},{20,16},{24,28},{28,24},{1,5},{5... | collective-permute-start | bytes 393224 | tf_op jit(solution)/shard_map/partials_dp1/ppermute | solution.py:361
  28.1 5.6 %collective-permute-start.12 = (bf16[256,256]{1,0:T(8,128)(2,1)S(1)}, bf16[256,256]{1,0:T(8,128)(2,1)S(1)}, u32[]{:S(2)}, u32[]{:S(2)}) collective-permute-start(bf16[256,256]{1,0:T(8,128)(2,1)S(1)} %get-tuple-element.63), channel_id=1, source_target_pairs={{0,8},{4,12},{8,0},{12,4},{16,24},{20,28},{24,16},{28,20},{1,9},{5... | collective-permute-start | bytes 393224 | tf_op jit(solution)/shard_map/partials_dp2/ppermute | solution.py:361
  33.9 1.4 %collective-permute-start.13 = (bf16[256,256]{1,0:T(8,128)(2,1)S(1)}, bf16[256,256]{1,0:T(8,128)(2,1)S(1)}, u32[]{:S(2)}, u32[]{:S(2)}) collective-permute-start(bf16[256,256]{1,0:T(8,128)(2,1)S(1)} %get-tuple-element.72.refs_5_), channel_id=1, source_target_pairs={{0,4},{4,0},{8,12},{12,8},{16,20},{20,16},{24,28},{28,24},{1,5},{5... | collective-permute-start | bytes 393224 | tf_op jit(solution)/shard_map/head_rows_dp1/ppermute | solution.py:361
  36.6 3.7 %collective-permute-start.14 = (bf16[256,640]{1,0:T(8,128)(2,1)S(1)}, bf16[256,640]{1,0:T(8,128)(2,1)S(1)}, u32[]{:S(2)}, u32[]{:S(2)}) collective-permute-start(bf16[256,640]{1,0:T(8,128)(2,1)S(1)} %get-tuple-element.74), channel_id=1, source_target_pairs={{0,4},{4,0},{8,12},{12,8},{16,20},{20,16},{24,28},{28,24},{1,5},{5... | collective-permute-start | bytes 983048 | tf_op jit(solution)/shard_map/token_back_dp1/ppermute | solution.py:361
  36.9 6.4 %collective-permute-start.19 = (bf16[2,256,128]{2,1,0:T(8,128)(2,1)S(1)}, bf16[2,256,128]{2,1,0:T(8,128)(2,1)S(1)}, u32[]{:S(2)}, u32[]{:S(2)}) collective-permute-start(bf16[2,256,128]{2,1,0:T(8,128)(2,1)S(1)} %get-tuple-element.83), channel_id=1, source_target_pairs={{0,1},{1,0},{2,3},{3,2},{4,5},{5,4},{6,7},{7,6},{8,9},{9,8},{10,11... | collective-permute-start | bytes 393224 | tf_op jit(solution)/shard_map/grads_expert1/ppermute | solution.py:365
  37.9 8.0 %collective-permute-start.20 = (bf16[2,256,128]{2,1,0:T(8,128)(2,1)S(1)}, bf16[2,256,128]{2,1,0:T(8,128)(2,1)S(1)}, u32[]{:S(2)}, u32[]{:S(2)}) collective-permute-start(bf16[2,256,128]{2,1,0:T(8,128)(2,1)S(1)} %get-tuple-element.84), channel_id=1, source_target_pairs={{0,2},{1,3},{2,0},{3,1},{4,6},{5,7},{6,4},{7,5},{8,10},{9,11},{10,... | collective-permute-start | bytes 393224 | tf_op jit(solution)/shard_map/grads_expert2/ppermute | solution.py:365
  39.4 8.2 %collective-permute-start.21 = (bf16[2,256,128]{2,1,0:T(8,128)(2,1)S(1)}, bf16[2,256,128]{2,1,0:T(8,128)(2,1)S(1)}, u32[]{:S(2)}, u32[]{:S(2)}) collective-permute-start(bf16[2,256,128]{2,1,0:T(8,128)(2,1)S(1)} %get-tuple-element.85), channel_id=1, source_target_pairs={{0,3},{1,2},{2,1},{3,0},{4,7},{5,6},{6,5},{7,4},{8,11},{9,10},{10,... | collective-permute-start | bytes 393224 | tf_op jit(solution)/shard_map/grads_expert3/ppermute | solution.py:365
  40.8 9.4 %collective-permute-start.15 = (bf16[128,1152]{1,0:T(8,128)(2,1)S(1)}, bf16[128,1152]{1,0:T(8,128)(2,1)S(1)}, u32[]{:S(2)}, u32[]{:S(2)}) collective-permute-start(bf16[128,1152]{1,0:T(8,128)(2,1)S(1)} %get-tuple-element.76), channel_id=1, source_target_pairs={{0,8},{4,12},{8,0},{12,4},{16,24},{20,28},{24,16},{28,20},{1,9},{5... | collective-permute-start | bytes 884744 | tf_op jit(solution)/shard_map/token_back_dp2/ppermute | solution.py:361
  41.8 10.7 %collective-permute-start.16 = (bf16[2,256,128]{2,1,0:T(8,128)(2,1)S(1)}, bf16[2,256,128]{2,1,0:T(8,128)(2,1)S(1)}, u32[]{:S(2)}, u32[]{:S(2)}) collective-permute-start(bf16[2,256,128]{2,1,0:T(8,128)(2,1)S(1)} %get-tuple-element.79), channel_id=1, source_target_pairs={{0,1},{1,0},{2,3},{3,2},{4,5},{5,4},{6,7},{7,6},{8,9},{9,8},{10,11... | collective-permute-start | bytes 393224 | tf_op jit(solution)/shard_map/grads_expert1/ppermute | solution.py:365
  43.3 9.2 %collective-permute-start.17 = (bf16[2,256,128]{2,1,0:T(8,128)(2,1)S(1)}, bf16[2,256,128]{2,1,0:T(8,128)(2,1)S(1)}, u32[]{:S(2)}, u32[]{:S(2)}) collective-permute-start(bf16[2,256,128]{2,1,0:T(8,128)(2,1)S(1)} %get-tuple-element.80), channel_id=1, source_target_pairs={{0,2},{1,3},{2,0},{3,1},{4,6},{5,7},{6,4},{7,5},{8,10},{9,11},{10,... | collective-permute-start | bytes 393224 | tf_op jit(solution)/shard_map/grads_expert2/ppermute | solution.py:365
  45.9 6.6 %collective-permute-start.18 = (bf16[2,256,128]{2,1,0:T(8,128)(2,1)S(1)}, bf16[2,256,128]{2,1,0:T(8,128)(2,1)S(1)}, u32[]{:S(2)}, u32[]{:S(2)}) collective-permute-start(bf16[2,256,128]{2,1,0:T(8,128)(2,1)S(1)} %get-tuple-element.81), channel_id=1, source_target_pairs={{0,3},{1,2},{2,1},{3,0},{4,7},{5,6},{6,5},{7,4},{8,11},{9,10},{10,... | collective-permute-start | bytes 393224 | tf_op jit(solution)/shard_map/grads_expert3/ppermute | solution.py:365
  47.7 7.3 %collective-permute-start.22 = (bf16[2,256,128]{2,1,0:T(8,128)(2,1)S(1)}, bf16[2,256,128]{2,1,0:T(8,128)(2,1)S(1)}, u32[]{:S(2)}, u32[]{:S(2)}) collective-permute-start(bf16[2,256,128]{2,1,0:T(8,128)(2,1)S(1)} %shard_map.153), channel_id=1, source_target_pairs={{0,16},{4,20},{8,24},{12,28},{16,0},{20,4},{24,8},{28,12},{1,17},{... | collective-permute-start | bytes 393224 | tf_op jit(solution)/shard_map/grads_dp4/ppermute | solution.py:361
  (6 other events, 20.1 us)
